TPU v7x, 32 devices: a whole 2x2x4 slice. The times are simulated.
32 devices in a mesh: segment: 4 (over y, x), lon: 8 (over z, core).
Axes of the slice: x: 2, y: 2, z: 4, core: 2. Of those that a mesh axis runs over, the one named last changes fastest.
Arguments:
- patches: bfloat16 [4, 1, 64, 640], P(None, None, 'lon'), may hold values from -4 to 4
- encoder_weight: bfloat16 [640, 1024], replicated, may hold values from -4 to 4
- layer_weights: bfloat16 [4, 4, 1024, 1024], P('segment'), may hold values from -0.1875 to 0.1875
- layer_gains: float32 [4, 1024], P('segment'), may hold values from 0.25 to 1.75
- final_gain: float32 [1024], replicated, may hold values from 0.25 to 1.75
- decoder_weight: bfloat16 [1024, 640], replicated, may hold values from -0.1875 to 0.1875
Outputs:
- forecast: float32 [4, 1, 64, 640], P('segment', None, 'lon')
All inputs are finite; a program needn't handle non-finite values.
Results may differ from a plain program's by a relative error of at most 0.015.
Values may be sent and summed in bfloat16 or wider, within the bound.
No kernel may reach another device: no remote copies, remote signals or barrier semaphores. Data moves between devices by JAX's collectives and lax.ppermute only.
A program may use at most 64 MiB of HBM per device.

v0:
```python
import jax
import jax.numpy as jnp
from jax import lax
from jax.sharding import PartitionSpec as P

HEADS = 16


SOFTCAP = 5.0
EPSILON = 1e-06


def shifted(value, axis, steps):
    count = lax.axis_size(axis)
    initial, last = (max(0, -steps), min(count, count - steps))
    return lax.ppermute(value, axis, [(source, source + steps) for source in range(initial, last)])


def norm_rows(latent, gain):
    square = jnp.mean(latent * latent, axis=-1, keepdims=True)
    return latent * lax.rsqrt(square + EPSILON) * gain


def body(patches, encoder_weight, layer_weights, layer_gains, final_gain, decoder_weight):
    segment_count = lax.axis_size("segment")
    segment_id = lax.axis_index("segment")
    batches = patches.shape[0]
    owned_count = batches // segment_count
    band_rows = patches.shape[1]
    lon_local = patches.shape[2]
    model_width = encoder_weight.shape[1]
    out_values = decoder_weight.shape[1]
    head_size = model_width // HEADS
    weights_here = layer_weights[0]
    gain_here = layer_gains[0]
    last_segment = segment_count - 1
    rounds = batches + segment_count - 1

    def project_rows(piece):
        flat = piece.reshape(-1, model_width)
        keys_part = jnp.dot(flat, weights_here[1], preferred_element_type=jnp.float32).astype(
            jnp.bfloat16
        )
        values_part = jnp.dot(flat, weights_here[2], preferred_element_type=jnp.float32).astype(
            jnp.bfloat16
        )
        joined = jnp.concatenate([keys_part, values_part], axis=-1)
        return joined.reshape(piece.shape[0], piece.shape[1], 2 * model_width)

    def attend(queries, both, latent):
        keys_all = both[..., :model_width].reshape(band_rows, -1, HEADS, head_size)
        values_all = both[..., model_width:].reshape(band_rows, -1, HEADS, head_size)
        query_heads = queries.reshape(band_rows, lon_local, HEADS, head_size)
        scores = jnp.einsum(
            "blhe,bmhe->bhlm", query_heads, keys_all, preferred_element_type=jnp.float32
        ) * head_size ** (-0.5)
        capped = SOFTCAP * jnp.tanh(scores / SOFTCAP)
        raised = jnp.exp(capped)
        probability = (raised / jnp.sum(raised, axis=-1, keepdims=True)).astype(jnp.bfloat16)
        attended = jnp.einsum(
            "bhlm,bmhe->blhe", probability, values_all, preferred_element_type=jnp.float32
        )
        attended = attended.astype(jnp.bfloat16).reshape(-1, model_width)
        mixed = latent.astype(jnp.float32).reshape(-1, model_width) + jnp.dot(
            attended, weights_here[3], preferred_element_type=jnp.float32
        )
        return mixed.astype(jnp.bfloat16).reshape(band_rows, lon_local, model_width)

    def tick_step(tick_index, carry):
        incoming, returning, stored = carry
        index_here = tick_index - segment_id
        active = jnp.logical_and(index_here >= 0, index_here < batches)
        slot_index = jnp.clip(index_here, 0, batches - 1)

        def encode():
            fresh = lax.dynamic_index_in_dim(patches, slot_index, 0, keepdims=False)
            encoded = jnp.dot(
                fresh.reshape(-1, fresh.shape[-1]),
                encoder_weight,
                preferred_element_type=jnp.float32,
            )
            return encoded.astype(jnp.bfloat16).reshape(band_rows, lon_local, model_width)

        latent = lax.cond(segment_id == 0, encode, lambda: incoming)
        normed = norm_rows(latent.astype(jnp.float32), gain_here).astype(jnp.bfloat16)
        piece = lax.all_gather(normed, "lon", axis=1, tiled=True)
        empty_rows = jnp.zeros((piece.shape[0], piece.shape[1], 2 * model_width), jnp.bfloat16)
        both = lax.cond(active, lambda: project_rows(piece), lambda: empty_rows)

        def local_work():
            queries = jnp.dot(
                normed.reshape(-1, model_width), weights_here[0], preferred_element_type=jnp.float32
            ).astype(jnp.bfloat16)
            return attend(queries, both, latent)

        mixed = lax.cond(active, local_work, lambda: jnp.zeros_like(latent))

        def decode():
            final = (
                norm_rows(mixed.astype(jnp.float32), final_gain)
                .astype(jnp.bfloat16)
                .reshape(-1, model_width)
            )
            decoded_rows = jnp.dot(final, decoder_weight, preferred_element_type=jnp.float32)
            return decoded_rows.reshape(band_rows, lon_local, out_values)

        decoded = lax.cond(
            jnp.logical_and(active, segment_id == last_segment),
            decode,
            lambda: jnp.zeros_like(returning),
        )
        seen = jnp.where(segment_id == last_segment, decoded, returning)
        travelled = tick_index - 2 * segment_count + 2 + segment_id
        item_index = jnp.where(segment_id == last_segment, index_here, travelled)
        is_owner = (
            (item_index >= 0) & (item_index < batches) & (item_index // owned_count == segment_id)
        )
        position = jnp.clip(item_index - segment_id * owned_count, 0, owned_count - 1)
        updated = lax.dynamic_update_index_in_dim(stored, seen, position, 0)
        stored = jnp.where(is_owner, updated, stored)
        handed = shifted(mixed, "segment", 1)
        passed = shifted(seen, "segment", -1)
        return (handed, passed, stored)

    start_latent = jnp.zeros((band_rows, lon_local, model_width), jnp.bfloat16)
    start_return = jnp.zeros((band_rows, lon_local, out_values), jnp.float32)
    start_stored = jnp.zeros((owned_count, band_rows, lon_local, out_values), jnp.float32)
    finished = lax.fori_loop(0, rounds, tick_step, (start_latent, start_return, start_stored))
    return finished[2]


def solution(mesh):
    in_specs = (
        P(None, None, "lon", None),
        P(),
        P("segment", None, None, None),
        P("segment", None),
        P(),
        P(),
    )
    out_specs = P("segment", None, "lon", None)
    return jax.shard_map(body, mesh=mesh, in_specs=in_specs, out_specs=out_specs, check_vma=False)
```

profile of v0, /device:TPU:5, one launch (start us, length us, event | category | flops | bytes accessed | tf_op | source)
XLA Modules:
  0.0 240.7 jit_solution(15639427997163985223)
XLA Ops:
  0.6 239.5 %while.25 = (s32[]{:T(128)}, bf16[1,8,1024]{2,1,0:T(8,128)(2,1)}, f32[1,8,640]{2,1,0:T(8,128)S(1)}, f32[1,1,8,640]{3,2,1,0:T(8,128)S(1)}, s32[]{:T(128)}, /*inde...) while((s32[]{:T(128)}, bf16[1,8,1024]{2,1,0:T(8,128)(2,1)}, ...), condition=%wide.region_13.14_spmd.clone, body=%wide.region_0.13_spmd.clone.sunk | while | flops 325926112 | bytes 19491668 | solution.py:128
  2.2 14.7 %all_gather.15 = bf16[1,64,1024]{2,1,0:T(8,128)(2,1)S(1)} all-gather(bf16[1,8,1024]{2,1,0:T(8,128)(2,1)S(1)} %multiply_convert_fusion.2), channel_id=1, replica_groups=mesh['segment'=4,'lon'=8] {'lon'}, dimensions={1}, use_global_device_ids=true | all-gather | bytes 147456 | tf_op jit(solution)/shard_map/while/body/eval_jaxpr/all_gather | solution.py:86
  18.3 3.1 %collective-permute-start.1 = (f32[1,8,640]{2,1,0:T(8,128)S(1)}, f32[1,8,640]{2,1,0:T(8,128)S(1)}, u32[]{:S(2)}, u32[]{:S(2)}) collective-permute-start(f32[1,8,640]{2,1,0:T(8,128)S(1)} %get-tuple-element.659), channel_id=1, source_target_pairs={{8,0},{16,8},{24,16},{9,1},{17,9},{25,17},{10,2},{18,10},{26,18},{... | collective-permute-start | bytes 61448 | tf_op jit(solution)/shard_map/while/body/eval_jaxpr/ppermute | solution.py:16
  21.4 2.2 collective-permute-start
  23.6 11.5 %collective-permute-done = bf16[1,8,1024]{2,1,0:T(8,128)(2,1)} collective-permute-done((bf16[1,8,1024]{2,1,0:T(8,128)(2,1)S(1)}, bf16[1,8,1024]{2,1,0:T(8,128)(2,1)}, u32[]{:S(2)}, u32[]{:S(2)}) %collective-permute-start) | collective-permute-done | bytes 16416 | tf_op jit(solution)/shard_map/while/body/eval_jaxpr/ppermute | solution.py:16
  36.8 15.2 %all_gather.15 = bf16[1,64,1024]{2,1,0:T(8,128)(2,1)S(1)} all-gather(bf16[1,8,1024]{2,1,0:T(8,128)(2,1)S(1)} %multiply_convert_fusion.2), channel_id=1, replica_groups=mesh['segment'=4,'lon'=8] {'lon'}, dimensions={1}, use_global_device_ids=true | all-gather | bytes 147456 | tf_op jit(solution)/shard_map/while/body/eval_jaxpr/all_gather | solution.py:86
  53.3 11.8 %collective-permute-start.1 = (f32[1,8,640]{2,1,0:T(8,128)S(1)}, f32[1,8,640]{2,1,0:T(8,128)S(1)}, u32[]{:S(2)}, u32[]{:S(2)}) collective-permute-start(f32[1,8,640]{2,1,0:T(8,128)S(1)} %get-tuple-element.659), channel_id=1, source_target_pairs={{8,0},{16,8},{24,16},{9,1},{17,9},{25,17},{10,2},{18,10},{26,18},{... | collective-permute-start | bytes 61448 | tf_op jit(solution)/shard_map/while/body/eval_jaxpr/ppermute | solution.py:16
  67.1 3.6 %collective-permute-done = bf16[1,8,1024]{2,1,0:T(8,128)(2,1)} collective-permute-done((bf16[1,8,1024]{2,1,0:T(8,128)(2,1)S(1)}, bf16[1,8,1024]{2,1,0:T(8,128)(2,1)}, u32[]{:S(2)}, u32[]{:S(2)}) %collective-permute-start) | collective-permute-done | bytes 16416 | tf_op jit(solution)/shard_map/while/body/eval_jaxpr/ppermute | solution.py:16
  72.3 15.4 %all_gather.15 = bf16[1,64,1024]{2,1,0:T(8,128)(2,1)S(1)} all-gather(bf16[1,8,1024]{2,1,0:T(8,128)(2,1)S(1)} %multiply_convert_fusion.2), channel_id=1, replica_groups=mesh['segment'=4,'lon'=8] {'lon'}, dimensions={1}, use_global_device_ids=true | all-gather | bytes 147456 | tf_op jit(solution)/shard_map/while/body/eval_jaxpr/all_gather | solution.py:86
  87.6 4.2 %conditional.13 = (bf16[1,64,2048]{2,1,0:T(8,128)(2,1)S(1)}) conditional(s32[]{:T(128)} %convert_element_type.159, () %tuple.117, (bf16[1,64,1024]{2,1,0:T(8,128)(2,1)S(1)}, bf16[4,1024,1024]{2,1,0:T(8,128)(2,1)}) %tuple.118), branch_computations={%region_5.5_spmd, %region_6.6_spmd} | conditional | flops 269090816 | bytes 5242888 | solution.py:88
  91.9 5.3 %conditional.14 = (bf16[1,8,1024]{2,1,0:T(8,128)(2,1)S(1)}) conditional(s32[]{:T(128)} %convert_element_type.159, () %tuple.115, (bf16[1,8,1024]{2,1,0:T(8,128)(2,1)}, bf16[1,8,1024]{2,1,0:T(8,128)(2,1)S(1)}, bf16[4,1024,1024]{2,1,0:T(8,128)(2,1)}, bf16[1,64,2048]{2,1,0:T(8,128)(2,1)S(1)}) %tuple.119), branch_computations={%region_7.7_spmd, %region_8.0_spmd} | conditional | flops 35725504 | bytes 5783560 | solution.py:96
  97.2 2.6 %collective-permute-start.1 = (f32[1,8,640]{2,1,0:T(8,128)S(1)}, f32[1,8,640]{2,1,0:T(8,128)S(1)}, u32[]{:S(2)}, u32[]{:S(2)}) collective-permute-start(f32[1,8,640]{2,1,0:T(8,128)S(1)} %get-tuple-element.659), channel_id=1, source_target_pairs={{8,0},{16,8},{24,16},{9,1},{17,9},{25,17},{10,2},{18,10},{26,18},{... | collective-permute-start | bytes 61448 | tf_op jit(solution)/shard_map/while/body/eval_jaxpr/ppermute | solution.py:16
  99.8 2.7 %collective-permute-start = (bf16[1,8,1024]{2,1,0:T(8,128)(2,1)S(1)}, bf16[1,8,1024]{2,1,0:T(8,128)(2,1)}, u32[]{:S(2)}, u32[]{:S(2)}) collective-permute-start(bf16[1,8,1024]{2,1,0:T(8,128)(2,1)S(1)} %get-tuple-element.719), channel_id=1, source_target_pairs={{0,8},{8,16},{16,24},{1,9},{9,17},{17,25},{2,10},{10,18},{18,26},{... | collective-permute-start | bytes 49160 | tf_op jit(solution)/shard_map/while/body/eval_jaxpr/ppermute | solution.py:16
  102.5 2.8 %collective-permute-done = bf16[1,8,1024]{2,1,0:T(8,128)(2,1)} collective-permute-done((bf16[1,8,1024]{2,1,0:T(8,128)(2,1)S(1)}, bf16[1,8,1024]{2,1,0:T(8,128)(2,1)}, u32[]{:S(2)}, u32[]{:S(2)}) %collective-permute-start) | collective-permute-done | bytes 16416 | tf_op jit(solution)/shard_map/while/body/eval_jaxpr/ppermute | solution.py:16
  106.9 15.4 %all_gather.15 = bf16[1,64,1024]{2,1,0:T(8,128)(2,1)S(1)} all-gather(bf16[1,8,1024]{2,1,0:T(8,128)(2,1)S(1)} %multiply_convert_fusion.2), channel_id=1, replica_groups=mesh['segment'=4,'lon'=8] {'lon'}, dimensions={1}, use_global_device_ids=true | all-gather | bytes 147456 | tf_op jit(solution)/shard_map/while/body/eval_jaxpr/all_gather | solution.py:86
  122.3 4.2 %conditional.13 = (bf16[1,64,2048]{2,1,0:T(8,128)(2,1)S(1)}) conditional(s32[]{:T(128)} %convert_element_type.159, () %tuple.117, (bf16[1,64,1024]{2,1,0:T(8,128)(2,1)S(1)}, bf16[4,1024,1024]{2,1,0:T(8,128)(2,1)}) %tuple.118), branch_computations={%region_5.5_spmd, %region_6.6_spmd} | conditional | flops 269090816 | bytes 5242888 | solution.py:88
  126.6 5.3 %conditional.14 = (bf16[1,8,1024]{2,1,0:T(8,128)(2,1)S(1)}) conditional(s32[]{:T(128)} %convert_element_type.159, () %tuple.115, (bf16[1,8,1024]{2,1,0:T(8,128)(2,1)}, bf16[1,8,1024]{2,1,0:T(8,128)(2,1)S(1)}, bf16[4,1024,1024]{2,1,0:T(8,128)(2,1)}, bf16[1,64,2048]{2,1,0:T(8,128)(2,1)S(1)}) %tuple.119), branch_computations={%region_7.7_spmd, %region_8.0_spmd} | conditional | flops 35725504 | bytes 5783560 | solution.py:96
  131.9 2.6 %collective-permute-start.1 = (f32[1,8,640]{2,1,0:T(8,128)S(1)}, f32[1,8,640]{2,1,0:T(8,128)S(1)}, u32[]{:S(2)}, u32[]{:S(2)}) collective-permute-start(f32[1,8,640]{2,1,0:T(8,128)S(1)} %get-tuple-element.659), channel_id=1, source_target_pairs={{8,0},{16,8},{24,16},{9,1},{17,9},{25,17},{10,2},{18,10},{26,18},{... | collective-permute-start | bytes 61448 | tf_op jit(solution)/shard_map/while/body/eval_jaxpr/ppermute | solution.py:16
  134.5 2.7 %collective-permute-start = (bf16[1,8,1024]{2,1,0:T(8,128)(2,1)S(1)}, bf16[1,8,1024]{2,1,0:T(8,128)(2,1)}, u32[]{:S(2)}, u32[]{:S(2)}) collective-permute-start(bf16[1,8,1024]{2,1,0:T(8,128)(2,1)S(1)} %get-tuple-element.719), channel_id=1, source_target_pairs={{0,8},{8,16},{16,24},{1,9},{9,17},{17,25},{2,10},{10,18},{18,26},{... | collective-permute-start | bytes 49160 | tf_op jit(solution)/shard_map/while/body/eval_jaxpr/ppermute | solution.py:16
  137.2 2.8 %collective-permute-done = bf16[1,8,1024]{2,1,0:T(8,128)(2,1)} collective-permute-done((bf16[1,8,1024]{2,1,0:T(8,128)(2,1)S(1)}, bf16[1,8,1024]{2,1,0:T(8,128)(2,1)}, u32[]{:S(2)}, u32[]{:S(2)}) %collective-permute-start) | collective-permute-done | bytes 16416 | tf_op jit(solution)/shard_map/while/body/eval_jaxpr/ppermute | solution.py:16
  141.6 15.4 %all_gather.15 = bf16[1,64,1024]{2,1,0:T(8,128)(2,1)S(1)} all-gather(bf16[1,8,1024]{2,1,0:T(8,128)(2,1)S(1)} %multiply_convert_fusion.2), channel_id=1, replica_groups=mesh['segment'=4,'lon'=8] {'lon'}, dimensions={1}, use_global_device_ids=true | all-gather | bytes 147456 | tf_op jit(solution)/shard_map/while/body/eval_jaxpr/all_gather | solution.py:86
  157.0 4.2 %conditional.13 = (bf16[1,64,2048]{2,1,0:T(8,128)(2,1)S(1)}) conditional(s32[]{:T(128)} %convert_element_type.159, () %tuple.117, (bf16[1,64,1024]{2,1,0:T(8,128)(2,1)S(1)}, bf16[4,1024,1024]{2,1,0:T(8,128)(2,1)}) %tuple.118), branch_computations={%region_5.5_spmd, %region_6.6_spmd} | conditional | flops 269090816 | bytes 5242888 | solution.py:88
  161.2 5.3 %conditional.14 = (bf16[1,8,1024]{2,1,0:T(8,128)(2,1)S(1)}) conditional(s32[]{:T(128)} %convert_element_type.159, () %tuple.115, (bf16[1,8,1024]{2,1,0:T(8,128)(2,1)}, bf16[1,8,1024]{2,1,0:T(8,128)(2,1)S(1)}, bf16[4,1024,1024]{2,1,0:T(8,128)(2,1)}, bf16[1,64,2048]{2,1,0:T(8,128)(2,1)S(1)}) %tuple.119), branch_computations={%region_7.7_spmd, %region_8.0_spmd} | conditional | flops 35725504 | bytes 5783560 | solution.py:96
  166.5 2.6 %collective-permute-start.1 = (f32[1,8,640]{2,1,0:T(8,128)S(1)}, f32[1,8,640]{2,1,0:T(8,128)S(1)}, u32[]{:S(2)}, u32[]{:S(2)}) collective-permute-start(f32[1,8,640]{2,1,0:T(8,128)S(1)} %get-tuple-element.659), channel_id=1, source_target_pairs={{8,0},{16,8},{24,16},{9,1},{17,9},{25,17},{10,2},{18,10},{26,18},{... | collective-permute-start | bytes 61448 | tf_op jit(solution)/shard_map/while/body/eval_jaxpr/ppermute | solution.py:16
  169.1 2.7 %collective-permute-start = (bf16[1,8,1024]{2,1,0:T(8,128)(2,1)S(1)}, bf16[1,8,1024]{2,1,0:T(8,128)(2,1)}, u32[]{:S(2)}, u32[]{:S(2)}) collective-permute-start(bf16[1,8,1024]{2,1,0:T(8,128)(2,1)S(1)} %get-tuple-element.719), channel_id=1, source_target_pairs={{0,8},{8,16},{16,24},{1,9},{9,17},{17,25},{2,10},{10,18},{18,26},{... | collective-permute-start | bytes 49160 | tf_op jit(solution)/shard_map/while/body/eval_jaxpr/ppermute | solution.py:16
  171.8 2.8 %collective-permute-done = bf16[1,8,1024]{2,1,0:T(8,128)(2,1)} collective-permute-done((bf16[1,8,1024]{2,1,0:T(8,128)(2,1)S(1)}, bf16[1,8,1024]{2,1,0:T(8,128)(2,1)}, u32[]{:S(2)}, u32[]{:S(2)}) %collective-permute-start) | collective-permute-done | bytes 16416 | tf_op jit(solution)/shard_map/while/body/eval_jaxpr/ppermute | solution.py:16
  176.2 15.4 %all_gather.15 = bf16[1,64,1024]{2,1,0:T(8,128)(2,1)S(1)} all-gather(bf16[1,8,1024]{2,1,0:T(8,128)(2,1)S(1)} %multiply_convert_fusion.2), channel_id=1, replica_groups=mesh['segment'=4,'lon'=8] {'lon'}, dimensions={1}, use_global_device_ids=true | all-gather | bytes 147456 | tf_op jit(solution)/shard_map/while/body/eval_jaxpr/all_gather | solution.py:86
  191.6 4.2 %conditional.13 = (bf16[1,64,2048]{2,1,0:T(8,128)(2,1)S(1)}) conditional(s32[]{:T(128)} %convert_element_type.159, () %tuple.117, (bf16[1,64,1024]{2,1,0:T(8,128)(2,1)S(1)}, bf16[4,1024,1024]{2,1,0:T(8,128)(2,1)}) %tuple.118), branch_computations={%region_5.5_spmd, %region_6.6_spmd} | conditional | flops 269090816 | bytes 5242888 | solution.py:88
  195.8 5.3 %conditional.14 = (bf16[1,8,1024]{2,1,0:T(8,128)(2,1)S(1)}) conditional(s32[]{:T(128)} %convert_element_type.159, () %tuple.115, (bf16[1,8,1024]{2,1,0:T(8,128)(2,1)}, bf16[1,8,1024]{2,1,0:T(8,128)(2,1)S(1)}, bf16[4,1024,1024]{2,1,0:T(8,128)(2,1)}, bf16[1,64,2048]{2,1,0:T(8,128)(2,1)S(1)}) %tuple.119), branch_computations={%region_7.7_spmd, %region_8.0_spmd} | conditional | flops 35725504 | bytes 5783560 | solution.py:96
  203.0 3.4 %collective-permute-start = (bf16[1,8,1024]{2,1,0:T(8,128)(2,1)S(1)}, bf16[1,8,1024]{2,1,0:T(8,128)(2,1)}, u32[]{:S(2)}, u32[]{:S(2)}) collective-permute-start(bf16[1,8,1024]{2,1,0:T(8,128)(2,1)S(1)} %get-tuple-element.719), channel_id=1, source_target_pairs={{0,8},{8,16},{16,24},{1,9},{9,17},{17,25},{2,10},{10,18},{18,26},{... | collective-permute-start | bytes 49160 | tf_op jit(solution)/shard_map/while/body/eval_jaxpr/ppermute | solution.py:16
  210.1 15.1 %all_gather.15 = bf16[1,64,1024]{2,1,0:T(8,128)(2,1)S(1)} all-gather(bf16[1,8,1024]{2,1,0:T(8,128)(2,1)S(1)} %multiply_convert_fusion.2), channel_id=1, replica_groups=mesh['segment'=4,'lon'=8] {'lon'}, dimensions={1}, use_global_device_ids=true | all-gather | bytes 147456 | tf_op jit(solution)/shard_map/while/body/eval_jaxpr/all_gather | solution.py:86
  228.5 10.7 %collective-permute-start = (bf16[1,8,1024]{2,1,0:T(8,128)(2,1)S(1)}, bf16[1,8,1024]{2,1,0:T(8,128)(2,1)}, u32[]{:S(2)}, u32[]{:S(2)}) collective-permute-start(bf16[1,8,1024]{2,1,0:T(8,128)(2,1)S(1)} %get-tuple-element.719), channel_id=1, source_target_pairs={{0,8},{8,16},{16,24},{1,9},{9,17},{17,25},{2,10},{10,18},{18,26},{... | collective-permute-start | bytes 49160 | tf_op jit(solution)/shard_map/while/body/eval_jaxpr/ppermute | solution.py:16
  (158 shorter events, 68.8 us)
Async XLA Ops:
  17.0 1.3 copy-start
  17.0 1.3 copy-start.2
  18.3 16.8 %collective-permute-start.1 = (f32[1,8,640]{2,1,0:T(8,128)S(1)}, f32[1,8,640]{2,1,0:T(8,128)S(1)}, u32[]{:S(2)}, u32[]{:S(2)}) collective-permute-start(f32[1,8,640]{2,1,0:T(8,128)S(1)} %get-tuple-element.659), channel_id=1, source_target_pairs={{8,0},{16,8},{24,16},{9,1},{17,9},{25,17},{10,2},{18,10},{26,18},{... | collective-permute-start | bytes 61448 | tf_op jit(solution)/shard_map/while/body/eval_jaxpr/ppermute | solution.py:16
  21.4 13.8 %collective-permute-start = (bf16[1,8,1024]{2,1,0:T(8,128)(2,1)S(1)}, bf16[1,8,1024]{2,1,0:T(8,128)(2,1)}, u32[]{:S(2)}, u32[]{:S(2)}) collective-permute-start(bf16[1,8,1024]{2,1,0:T(8,128)(2,1)S(1)} %get-tuple-element.719), channel_id=1, source_target_pairs={{0,8},{8,16},{16,24},{1,9},{9,17},{17,25},{2,10},{10,18},{18,26},{... | collective-permute-start | bytes 49160 | tf_op jit(solution)/shard_map/while/body/eval_jaxpr/ppermute | solution.py:16
  52.0 1.3 copy-start
  52.0 1.3 copy-start.2
  53.3 17.3 %collective-permute-start.1 = (f32[1,8,640]{2,1,0:T(8,128)S(1)}, f32[1,8,640]{2,1,0:T(8,128)S(1)}, u32[]{:S(2)}, u32[]{:S(2)}) collective-permute-start(f32[1,8,640]{2,1,0:T(8,128)S(1)} %get-tuple-element.659), channel_id=1, source_target_pairs={{8,0},{16,8},{24,16},{9,1},{17,9},{25,17},{10,2},{18,10},{26,18},{... | collective-permute-start | bytes 61448 | tf_op jit(solution)/shard_map/while/body/eval_jaxpr/ppermute | solution.py:16
  65.1 5.5 %collective-permute-start = (bf16[1,8,1024]{2,1,0:T(8,128)(2,1)S(1)}, bf16[1,8,1024]{2,1,0:T(8,128)(2,1)}, u32[]{:S(2)}, u32[]{:S(2)}) collective-permute-start(bf16[1,8,1024]{2,1,0:T(8,128)(2,1)S(1)} %get-tuple-element.719), channel_id=1, source_target_pairs={{0,8},{8,16},{16,24},{1,9},{9,17},{17,25},{2,10},{10,18},{18,26},{... | collective-permute-start | bytes 49160 | tf_op jit(solution)/shard_map/while/body/eval_jaxpr/ppermute | solution.py:16
  91.8 5.3 %copy-start = (bf16[1024,640]{1,0:T(8,128)(2,1)S(1)}, bf16[1024,640]{1,0:T(8,128)(2,1)}, u32[]{:S(2)}) copy-start(bf16[1024,640]{1,0:T(8,128)(2,1)} %get-tuple-element.713) | copy-start | bytes 3932164 | tf_op jit(solution)/shard_map/while
  91.8 5.3 %copy-start.2 = (f32[1024]{0:T(1024)S(1)}, f32[1024]{0:T(1024)}, u32[]{:S(2)}) copy-start(f32[1024]{0:T(1024)} %get-tuple-element.712) | copy-start | bytes 12292 | tf_op jit(solution)/shard_map/while
  97.2 8.1 %collective-permute-start.1 = (f32[1,8,640]{2,1,0:T(8,128)S(1)}, f32[1,8,640]{2,1,0:T(8,128)S(1)}, u32[]{:S(2)}, u32[]{:S(2)}) collective-permute-start(f32[1,8,640]{2,1,0:T(8,128)S(1)} %get-tuple-element.659), channel_id=1, source_target_pairs={{8,0},{16,8},{24,16},{9,1},{17,9},{25,17},{10,2},{18,10},{26,18},{... | collective-permute-start | bytes 61448 | tf_op jit(solution)/shard_map/while/body/eval_jaxpr/ppermute | solution.py:16
  99.8 5.5 %collective-permute-start = (bf16[1,8,1024]{2,1,0:T(8,128)(2,1)S(1)}, bf16[1,8,1024]{2,1,0:T(8,128)(2,1)}, u32[]{:S(2)}, u32[]{:S(2)}) collective-permute-start(bf16[1,8,1024]{2,1,0:T(8,128)(2,1)S(1)} %get-tuple-element.719), channel_id=1, source_target_pairs={{0,8},{8,16},{16,24},{1,9},{9,17},{17,25},{2,10},{10,18},{18,26},{... | collective-permute-start | bytes 49160 | tf_op jit(solution)/shard_map/while/body/eval_jaxpr/ppermute | solution.py:16
  126.5 5.3 %copy-start = (bf16[1024,640]{1,0:T(8,128)(2,1)S(1)}, bf16[1024,640]{1,0:T(8,128)(2,1)}, u32[]{:S(2)}) copy-start(bf16[1024,640]{1,0:T(8,128)(2,1)} %get-tuple-element.713) | copy-start | bytes 3932164 | tf_op jit(solution)/shard_map/while
  126.5 5.3 %copy-start.2 = (f32[1024]{0:T(1024)S(1)}, f32[1024]{0:T(1024)}, u32[]{:S(2)}) copy-start(f32[1024]{0:T(1024)} %get-tuple-element.712) | copy-start | bytes 12292 | tf_op jit(solution)/shard_map/while
  131.9 8.1 %collective-permute-start.1 = (f32[1,8,640]{2,1,0:T(8,128)S(1)}, f32[1,8,640]{2,1,0:T(8,128)S(1)}, u32[]{:S(2)}, u32[]{:S(2)}) collective-permute-start(f32[1,8,640]{2,1,0:T(8,128)S(1)} %get-tuple-element.659), channel_id=1, source_target_pairs={{8,0},{16,8},{24,16},{9,1},{17,9},{25,17},{10,2},{18,10},{26,18},{... | collective-permute-start | bytes 61448 | tf_op jit(solution)/shard_map/while/body/eval_jaxpr/ppermute | solution.py:16
  134.5 5.5 %collective-permute-start = (bf16[1,8,1024]{2,1,0:T(8,128)(2,1)S(1)}, bf16[1,8,1024]{2,1,0:T(8,128)(2,1)}, u32[]{:S(2)}, u32[]{:S(2)}) collective-permute-start(bf16[1,8,1024]{2,1,0:T(8,128)(2,1)S(1)} %get-tuple-element.719), channel_id=1, source_target_pairs={{0,8},{8,16},{16,24},{1,9},{9,17},{17,25},{2,10},{10,18},{18,26},{... | collective-permute-start | bytes 49160 | tf_op jit(solution)/shard_map/while/body/eval_jaxpr/ppermute | solution.py:16
  161.1 5.3 %copy-start = (bf16[1024,640]{1,0:T(8,128)(2,1)S(1)}, bf16[1024,640]{1,0:T(8,128)(2,1)}, u32[]{:S(2)}) copy-start(bf16[1024,640]{1,0:T(8,128)(2,1)} %get-tuple-element.713) | copy-start | bytes 3932164 | tf_op jit(solution)/shard_map/while
  161.2 5.3 %copy-start.2 = (f32[1024]{0:T(1024)S(1)}, f32[1024]{0:T(1024)}, u32[]{:S(2)}) copy-start(f32[1024]{0:T(1024)} %get-tuple-element.712) | copy-start | bytes 12292 | tf_op jit(solution)/shard_map/while
  166.5 8.1 %collective-permute-start.1 = (f32[1,8,640]{2,1,0:T(8,128)S(1)}, f32[1,8,640]{2,1,0:T(8,128)S(1)}, u32[]{:S(2)}, u32[]{:S(2)}) collective-permute-start(f32[1,8,640]{2,1,0:T(8,128)S(1)} %get-tuple-element.659), channel_id=1, source_target_pairs={{8,0},{16,8},{24,16},{9,1},{17,9},{25,17},{10,2},{18,10},{26,18},{... | collective-permute-start | bytes 61448 | tf_op jit(solution)/shard_map/while/body/eval_jaxpr/ppermute | solution.py:16
  169.1 5.5 %collective-permute-start = (bf16[1,8,1024]{2,1,0:T(8,128)(2,1)S(1)}, bf16[1,8,1024]{2,1,0:T(8,128)(2,1)}, u32[]{:S(2)}, u32[]{:S(2)}) collective-permute-start(bf16[1,8,1024]{2,1,0:T(8,128)(2,1)S(1)} %get-tuple-element.719), channel_id=1, source_target_pairs={{0,8},{8,16},{16,24},{1,9},{9,17},{17,25},{2,10},{10,18},{18,26},{... | collective-permute-start | bytes 49160 | tf_op jit(solution)/shard_map/while/body/eval_jaxpr/ppermute | solution.py:16
  195.8 5.3 %copy-start = (bf16[1024,640]{1,0:T(8,128)(2,1)S(1)}, bf16[1024,640]{1,0:T(8,128)(2,1)}, u32[]{:S(2)}) copy-start(bf16[1024,640]{1,0:T(8,128)(2,1)} %get-tuple-element.713) | copy-start | bytes 3932164 | tf_op jit(solution)/shard_map/while
  195.8 5.3 %copy-start.2 = (f32[1024]{0:T(1024)S(1)}, f32[1024]{0:T(1024)}, u32[]{:S(2)}) copy-start(f32[1024]{0:T(1024)} %get-tuple-element.712) | copy-start | bytes 12292 | tf_op jit(solution)/shard_map/while
  201.1 7.4 %collective-permute-start.1 = (f32[1,8,640]{2,1,0:T(8,128)S(1)}, f32[1,8,640]{2,1,0:T(8,128)S(1)}, u32[]{:S(2)}, u32[]{:S(2)}) collective-permute-start(f32[1,8,640]{2,1,0:T(8,128)S(1)} %get-tuple-element.659), channel_id=1, source_target_pairs={{8,0},{16,8},{24,16},{9,1},{17,9},{25,17},{10,2},{18,10},{26,18},{... | collective-permute-start | bytes 61448 | tf_op jit(solution)/shard_map/while/body/eval_jaxpr/ppermute | solution.py:16
  203.0 5.5 %collective-permute-start = (bf16[1,8,1024]{2,1,0:T(8,128)(2,1)S(1)}, bf16[1,8,1024]{2,1,0:T(8,128)(2,1)}, u32[]{:S(2)}, u32[]{:S(2)}) collective-permute-start(bf16[1,8,1024]{2,1,0:T(8,128)(2,1)S(1)} %get-tuple-element.719), channel_id=1, source_target_pairs={{0,8},{8,16},{16,24},{1,9},{9,17},{17,25},{2,10},{10,18},{18,26},{... | collective-permute-start | bytes 49160 | tf_op jit(solution)/shard_map/while/body/eval_jaxpr/ppermute | solution.py:16
  225.3 1.3 copy-start
  225.3 1.3 copy-start.2
  226.6 13.5 %collective-permute-start.1 = (f32[1,8,640]{2,1,0:T(8,128)S(1)}, f32[1,8,640]{2,1,0:T(8,128)S(1)}, u32[]{:S(2)}, u32[]{:S(2)}) collective-permute-start(f32[1,8,640]{2,1,0:T(8,128)S(1)} %get-tuple-element.659), channel_id=1, source_target_pairs={{8,0},{16,8},{24,16},{9,1},{17,9},{25,17},{10,2},{18,10},{26,18},{... | collective-permute-start | bytes 61448 | tf_op jit(solution)/shard_map/while/body/eval_jaxpr/ppermute | solution.py:16
  228.5 11.6 %collective-permute-start = (bf16[1,8,1024]{2,1,0:T(8,128)(2,1)S(1)}, bf16[1,8,1024]{2,1,0:T(8,128)(2,1)}, u32[]{:S(2)}, u32[]{:S(2)}) collective-permute-start(bf16[1,8,1024]{2,1,0:T(8,128)(2,1)S(1)} %get-tuple-element.719), channel_id=1, source_target_pairs={{0,8},{8,16},{16,24},{1,9},{9,17},{17,25},{2,10},{10,18},{18,26},{... | collective-permute-start | bytes 49160 | tf_op jit(solution)/shard_map/while/body/eval_jaxpr/ppermute | solution.py:16
  240.1 0.6 copy-start.1
where the time goes:
time: 244 us; the launch traced here: 241 us
  blocking collectives  107 us (44%)
  starting transfers between devices  52.8 us (22%)
  matrix products  34.9 us (14%)
  waiting for transfers between devices  26.4 us (11%)
  other arithmetic  11.4 us (5%)
  local copies, waits for them, and re-layouts  7.53 us (3%)
    all_gather x7, blocking collectives, tick_step(): piece = lax.all_gather(normed, 'lon', axis=1, tiled=True)  107 us
    ppermute x14, starting transfers between devices, shifted(): lax.ppermute(value, axis, [(source, source + steps) for source in range(i...  52.8 us
    ppermute x14, waiting for transfers between devices, shifted(): lax.ppermute(value, axis, [(source, source + steps) for source in range(i...  26.4 us
    dot_general x4, matrix products, local_work(): jnp.dot(normed.reshape(-1, model_width), weights_here[0], preferred_eleme...  8.42 us
    dot_general x4, matrix products, project_rows(): jnp.dot(flat, weights_here[2], preferred_element_type=jnp.float32)  8.29 us
    dot_general x4, matrix products, project_rows(): jnp.dot(flat, weights_here[1], preferred_element_type=jnp.float32)  8.28 us
    dot_general x4, matrix products, attend(): jnp.dot(attended, weights_here[3], preferred_element_type=jnp.float32)  7.92 us
    reduce_sum x7, other arithmetic, norm_rows(): square = jnp.mean(latent * latent, axis=-1, keepdims=True)  5.87 us
  transfers between devices with their start and end apart: 14, of which 7 were waited for; matrix products, arithmetic and copies ran while one was open for 0% of the time, Pallas kernels for 0%

commit v1 on v0

v1 whole, which is shorter than its diff:
```python
import functools

import jax
import jax.numpy as jnp
from jax import lax
from jax.experimental import pallas as pl
from jax.experimental.pallas import tpu as pltpu
from jax.sharding import PartitionSpec as P

HEADS = 16
SOFTCAP = 5.0
EPSILON = 1e-06
BOTH = ("segment", "lon")
VMEM_SPEC = pl.BlockSpec(memory_space=pltpu.VMEM)
SMEM_SPEC = pl.BlockSpec(memory_space=pltpu.SMEM)


def matmul(left, right):
    return jnp.dot(left, right, preferred_element_type=jnp.float32)


def norm_rows(latent, gain):
    square = jnp.mean(latent * latent, axis=-1, keepdims=True)
    return (latent * lax.rsqrt(square + EPSILON) * gain).astype(jnp.bfloat16)


def attend(queries, keys, values):
    rows, width = queries.shape
    head_size = width // HEADS
    heads = min(4, HEADS)
    lanes = heads * head_size
    lane_head = lax.broadcasted_iota(jnp.int32, (rows, lanes), 1) // head_size
    own = [lane_head == head for head in range(heads)]
    row_head = lax.broadcasted_iota(jnp.int32, (heads * rows, heads * rows), 0) // rows
    column_head = lax.broadcasted_iota(jnp.int32, (heads * rows, heads * rows), 1) // rows
    same_head = jnp.where(row_head == column_head, 1.0, 0.0).astype(jnp.bfloat16)
    outs = []
    for start in range(0, width, lanes):
        cut = slice(start, start + lanes)
        zero = jnp.zeros((rows, lanes), jnp.bfloat16)
        key_block = jnp.concatenate([jnp.where(mask, keys[:, cut], zero) for mask in own], axis=0)
        value_block = jnp.concatenate([jnp.where(mask, values[:, cut], zero) for mask in own], axis=0)
        scores = lax.dot_general(
            queries[:, cut], key_block, (((1,), (1,)), ((), ())), preferred_element_type=jnp.float32
        )
        raised = jnp.exp(SOFTCAP * jnp.tanh(scores * (head_size ** (-0.5) / SOFTCAP)))
        high = raised.astype(jnp.bfloat16)
        low = (raised - high.astype(jnp.float32)).astype(jnp.bfloat16)
        total = matmul(high, same_head) + matmul(low, same_head)
        probability = (raised / total).astype(jnp.bfloat16)
        outs.append(matmul(probability, value_block).astype(jnp.bfloat16))
    return jnp.concatenate(outs, axis=-1)


def layer(latent, weights, gain):
    wide = latent.astype(jnp.float32)
    normed = norm_rows(wide, gain)
    queries, keys, values = [matmul(normed, weights[i]).astype(jnp.bfloat16) for i in range(3)]
    attended = attend(queries, keys, values)
    return (wide + matmul(attended, weights[3])).astype(jnp.bfloat16)


def first_kernel(place, patches, encoder, weights, gain, out):
    @pl.when(place[0] == 1)
    def _():
        latent = matmul(patches[...], encoder[...]).astype(jnp.bfloat16)
        out[...] = layer(latent, weights, gain[...])


def middle_kernel(place, latent, weights, gain, out):
    @pl.when(place[0] == 1)
    def _():
        out[...] = layer(latent[...], weights, gain[...])


def last_kernel(group, place, latent, weights, gain, final_gain, decoder, *rest):
    outs, decoded = rest[:-1], rest[-1]

    @pl.when(place[0] == 1)
    def _():
        mixed = layer(latent[...], weights, gain[...])
        final = norm_rows(mixed.astype(jnp.float32), final_gain[...])
        decoded[...] = matmul(final, decoder[...])
        rows = outs[0].shape[0]
        for index, out in enumerate(outs):
            start = pl.multiple_of((index * group + place[1]) * rows, 8)
            out[...] = decoded[pl.ds(start, rows), :]


def in_vmem(value):
    return pltpu.with_memory_space_constraint(value, pltpu.VMEM)


def call(kernel, out_shape, place, operands, scratch=()):
    return pl.pallas_call(
        kernel,
        out_shape=out_shape,
        in_specs=[SMEM_SPEC] + [VMEM_SPEC] * len(operands),
        out_specs=jax.tree.map(lambda _: VMEM_SPEC, out_shape),
        scratch_shapes=list(scratch),
        compiler_params=pltpu.CompilerParams(vmem_limit_bytes=24 * 1024 * 1024),
    )(place, *operands)


def body(patches, encoder_weight, layer_weights, layer_gains, final_gain, decoder_weight):
    segments = lax.axis_size("segment")
    lons = lax.axis_size("lon")
    segment_id = lax.axis_index("segment")
    lon_id = lax.axis_index("lon")
    bands, band_rows, lon_local, patch_values = patches.shape
    assert band_rows == 1 and bands == segments and lons % bands == 0
    group = lons // bands
    columns = lons * lon_local
    width = encoder_weight.shape[1]
    out_values = decoder_weight.shape[1]

    weights = in_vmem(layer_weights[0])
    gain = layer_gains
    member = lon_id % group

    sent = jnp.repeat(patches[:, 0], group, axis=0)
    circle = lax.all_to_all(sent, "lon", 0, 0, tiled=True).reshape(columns, patch_values)

    latent_shape = jax.ShapeDtypeStruct((columns, width), jnp.bfloat16)
    latent = None
    for tick in range(segments):
        place = jnp.stack([(segment_id == tick).astype(jnp.int32), member.astype(jnp.int32)])
        if tick == 0:
            latent = call(
                first_kernel, latent_shape, place, [circle, in_vmem(encoder_weight), weights, gain]
            )
        elif tick < segments - 1:
            latent = call(middle_kernel, latent_shape, place, [latent, weights, gain])
        if tick < segments - 1:
            pairs = [(tick * lons + i, (tick + 1) * lons + i) for i in range(lons)]
            latent = lax.ppermute(latent, BOTH, pairs)
            continue
        part_shape = jax.ShapeDtypeStruct((lon_local, out_values), jnp.float32)
        parts = call(
            functools.partial(last_kernel, group),
            [part_shape] * bands,
            place,
            [latent, weights, gain, final_gain[None], in_vmem(decoder_weight)],
            [pltpu.VMEM((columns, out_values), jnp.float32)],
        )
    received = []
    for index, part in enumerate(parts):
        pairs = [
            ((segments - 1) * lons + band * group + i, band * lons + index * group + i)
            for band in range(bands)
            for i in range(group)
        ]
        received.append(lax.ppermute(part, BOTH, pairs))
    return sum(received[1:], received[0])[None, None]


def solution(mesh):
    in_specs = (
        P(None, None, "lon", None),
        P(),
        P("segment", None, None, None),
        P("segment", None),
        P(),
        P(),
    )
    out_specs = P("segment", None, "lon", None)
    return jax.shard_map(body, mesh=mesh, in_specs=in_specs, out_specs=out_specs, check_vma=False)
```

time: 244 us -> 68 us (0.28)
  the two profiles are of different devices: /device:TPU:5 before, /device:TPU:24 now
where the time goes in v1:
time: 68 us; the launch traced here: 67.5 us
  waiting for transfers between devices  33.2 us (49%)
  local copies, waits for them, and re-layouts  17 us (25%)
  starting transfers between devices  11 us (16%)
  Pallas kernels  5.21 us (8%)
  other arithmetic  0.92 us (1%)
    ppermute x4, waiting for transfers between devices, body(): received.append(lax.ppermute(part, BOTH, pairs))  27.1 us
    unnamed x18, local copies, waits for them, and re-layouts  15.5 us
    pallas_call x4, Pallas kernels, call(): pl.pallas_call(kernel, out_shape=out_shape, in_specs=[SMEM_SPEC] + [VMEM_...  5.21 us
    all_to_all x1, starting transfers between devices, body(): lax.all_to_all(sent, 'lon', 0, 0, tiled=True).reshape(columns, patch_values)  5.1 us
    ppermute x4, starting transfers between devices, body(): received.append(lax.ppermute(part, BOTH, pairs))  3.28 us
    all_to_all x1, waiting for transfers between devices, body(): lax.all_to_all(sent, 'lon', 0, 0, tiled=True).reshape(columns, patch_values)  3.24 us
    ppermute x3, waiting for transfers between devices, body(): latent = lax.ppermute(latent, BOTH, pairs)  2.81 us
    ppermute x3, starting transfers between devices, body(): latent = lax.ppermute(latent, BOTH, pairs)  2.64 us
  transfers between devices with their start and end apart: 8, of which 3 were waited for; matrix products, arithmetic and copies ran while one was open for 0% of the time, Pallas kernels for 0%

profile of v1, /device:TPU:24, one launch (start us, length us, event | category | flops | bytes accessed | tf_op | source)
XLA Modules:
  0.0 67.5 jit_solution(985131460579270789)
XLA Ops:
  0.0 1.4 %broadcast_in_dim.9 = bf16[4,2,8,640]{3,2,1,0:T(8,128)(2,1)} broadcast(bf16[4,8,640]{2,1,0:T(8,128)(2,1)} %bitcast.18), dimensions={0,2,3} | broadcast | bytes 122880 | tf_op jit(solution)/shard_map/broadcast_in_dim | solution.py:121
  1.4 5.1 %all-to-all-start = ((bf16[8,8,640]{2,1,0:T(8,128)(2,1)}), bf16[8,8,640]{2,1,0:T(8,128)(2,1)S(1)}, u32[]{:S(2)}, u32[]{:S(2)}) async-start(bf16[8,8,640]{2,1,0:T(8,128)(2,1)} %bitcast.6), calls=%async_computation | async-start | bytes 163840 | tf_op jit(solution)/shard_map/all_to_all | solution.py:122
  6.5 0.1 pad_add_fusion.3.place
  6.6 3.2 %all-to-all-done = bf16[8,8,640]{2,1,0:T(8,128)(2,1)S(1)} async-done(((bf16[8,8,640]{2,1,0:T(8,128)(2,1)}), bf16[8,8,640]{2,1,0:T(8,128)(2,1)S(1)}, u32[]{:S(2)}, u32[]{:S(2)}) %all-to-all-start) | async-done | bytes 81952 | tf_op jit(solution)/shard_map/all_to_all | solution.py:122
  9.8 3.4 %copy-done = bf16[1,4,1024,1024]{3,2,1,0:T(8,128)(2,1)S(1)} copy-done((bf16[1,4,1024,1024]{3,2,1,0:T(8,128)(2,1)S(1)}, bf16[1,4,1024,1024]{3,2,1,0:T(8,128)(2,1)}, u32[]{:S(2)}) %copy-start) | copy-done | bytes 8388632
  13.2 1.3 %copy-done.4 = bf16[640,1024]{1,0:T(8,128)(2,1)S(1)} copy-done((bf16[640,1024]{1,0:T(8,128)(2,1)S(1)}, bf16[640,1024]{1,0:T(8,128)(2,1)}, u32[]{:S(2)}) %copy-start.4) | copy-done | bytes 1310744
  14.5 0.7 %copy-done.6 = f32[1,1024]{1,0:T(1,128)S(1)} copy-done((f32[1,1024]{1,0:T(1,128)S(1)}, f32[1,1024]{1,0:T(1,128)}, u32[]{:S(2)}) %copy-start.6) | copy-done | bytes 4120
  15.2 3.6 %shard_map.64 = bf16[64,1024]{1,0:T(8,128)(2,1)S(1)} custom-call(s32[2]{0:T(128)S(1)} %pad_add_fusion.3.place, bf16[64,640]{1,0:T(8,128)(2,1)S(1)} %bitcast.16, bf16[640,1024]{1,0:T(8,128)(2,1)S(1)} %copy-done.4, bf16[4,1024,1024]{2,1,0:T(8,128)(2,1)S(1)} %bitcast.12, f32[1,1024]{1,0:T(1,128)S(1)} %copy-done.6), custom_call_target="tpu_custom_call" | custom-call | tf_op jit(solution)/shard_map/pallas_call | solution.py:95
  18.8 1.3 %collective-permute-start = (bf16[64,1024]{1,0:T(8,128)(2,1)S(1)}, bf16[64,1024]{1,0:T(8,128)(2,1)S(1)}, u32[]{:S(2)}, u32[]{:S(2)}) collective-permute-start(bf16[64,1024]{1,0:T(8,128)(2,1)S(1)} %shard_map.64), channel_id=1, source_target_pairs={{0,8},{1,9},{2,10},{3,11},{4,12},{5,13},{6,14},{7,15}} | collective-permute-start | bytes 393224 | tf_op jit(solution)/shard_map/ppermute | solution.py:136
  20.1 0.1 pad_add_fusion.2.place
  20.2 2.8 %collective-permute-done.latent = bf16[64,1024]{1,0:T(8,128)(2,1)S(1)} collective-permute-done((bf16[64,1024]{1,0:T(8,128)(2,1)S(1)}, bf16[64,1024]{1,0:T(8,128)(2,1)S(1)}, u32[]{:S(2)}, u32[]{:S(2)}) %collective-permute-start) | collective-permute-done | bytes 131104 | tf_op jit(solution)/shard_map/ppermute | solution.py:136
  23.0 3.4 %copy-done.1 = bf16[1,4,1024,1024]{3,2,1,0:T(8,128)(2,1)S(1)} copy-done((bf16[1,4,1024,1024]{3,2,1,0:T(8,128)(2,1)S(1)}, bf16[1,4,1024,1024]{3,2,1,0:T(8,128)(2,1)}, u32[]{:S(2)}) %copy-start.1) | copy-done | bytes 8388632
  26.4 0.5 shard_map.65
  26.9 0.7 collective-permute-start.1
  27.6 0.1 pad_add_fusion.1.place
  27.7 0.0 collective-permute-done.1.latent
  27.7 3.4 %copy-done.2 = bf16[1,4,1024,1024]{3,2,1,0:T(8,128)(2,1)S(1)} copy-done((bf16[1,4,1024,1024]{3,2,1,0:T(8,128)(2,1)S(1)}, bf16[1,4,1024,1024]{3,2,1,0:T(8,128)(2,1)}, u32[]{:S(2)}) %copy-start.2) | copy-done | bytes 8388632
  31.1 0.5 shard_map.66
  31.7 0.7 collective-permute-start.2
  32.3 0.1 pad_add_fusion.place
  32.4 0.0 collective-permute-done.2.latent
  32.4 0.0 copy-start.3
  32.4 3.4 %copy-done.3 = bf16[1,4,1024,1024]{3,2,1,0:T(8,128)(2,1)S(1)} copy-done((bf16[1,4,1024,1024]{3,2,1,0:T(8,128)(2,1)S(1)}, bf16[1,4,1024,1024]{3,2,1,0:T(8,128)(2,1)}, u32[]{:S(2)}) %copy-start.3) | copy-done | bytes 8388632
  35.8 0.5 shard_map.67
  36.4 0.7 collective-permute-start.3
  37.0 0.7 collective-permute-start.4
  37.7 0.7 collective-permute-start.5
  38.4 1.3 %collective-permute-start.6 = (f32[8,640]{1,0:T(8,128)S(1)}, f32[8,640]{1,0:T(8,128)S(1)}, u32[]{:S(2)}, u32[]{:S(2)}) collective-permute-start(f32[8,640]{1,0:T(8,128)S(1)} %get-tuple-element.12), channel_id=1, source_target_pairs={{24,6},{25,7},{26,14},{27,15},{28,22},{29,23},{30,30},{31,31}} | collective-permute-start | bytes 61448 | tf_op jit(solution)/shard_map/ppermute | solution.py:153
  39.7 0.0 collective-permute-done.3
  39.7 0.0 collective-permute-done.5
  39.7 27.1 %collective-permute-done.6 = f32[8,640]{1,0:T(8,128)S(1)} collective-permute-done((f32[8,640]{1,0:T(8,128)S(1)}, f32[8,640]{1,0:T(8,128)S(1)}, u32[]{:S(2)}, u32[]{:S(2)}) %collective-permute-start.6) | collective-permute-done | bytes 20512 | tf_op jit(solution)/shard_map/ppermute | solution.py:153
  66.8 0.6 add_bitcast_fusion
  (12 shorter events, 0.0 us)
Async XLA Ops:
  1.4 8.4 %all-to-all-start = ((bf16[8,8,640]{2,1,0:T(8,128)(2,1)}), bf16[8,8,640]{2,1,0:T(8,128)(2,1)S(1)}, u32[]{:S(2)}, u32[]{:S(2)}) async-start(bf16[8,8,640]{2,1,0:T(8,128)(2,1)} %bitcast.6), calls=%async_computation | async-start | bytes 163840 | tf_op jit(solution)/shard_map/all_to_all | solution.py:122
  9.8 3.4 %copy-start = (bf16[1,4,1024,1024]{3,2,1,0:T(8,128)(2,1)S(1)}, bf16[1,4,1024,1024]{3,2,1,0:T(8,128)(2,1)}, u32[]{:S(2)}) copy-start(bf16[1,4,1024,1024]{3,2,1,0:T(8,128)(2,1)} %param.8) | copy-start | bytes 25165828
  13.2 1.3 %copy-start.4 = (bf16[640,1024]{1,0:T(8,128)(2,1)S(1)}, bf16[640,1024]{1,0:T(8,128)(2,1)}, u32[]{:S(2)}) copy-start(bf16[640,1024]{1,0:T(8,128)(2,1)} %encoder.1) | copy-start | bytes 3932164
  14.5 0.7 %copy-start.6 = (f32[1,1024]{1,0:T(1,128)S(1)}, f32[1,1024]{1,0:T(1,128)}, u32[]{:S(2)}) copy-start(f32[1,1024]{1,0:T(1,128)} %gain.7) | copy-start | bytes 12292
  15.2 7.8 %copy-start.7 = (f32[1,1024]{1,0:T(1,128)S(1)}, f32[1,1024]{1,0:T(1,128)}, u32[]{:S(2)}) copy-start(f32[1,1024]{1,0:T(1,128)} %gain.7) | copy-start | bytes 12292
  18.8 4.2 %collective-permute-start = (bf16[64,1024]{1,0:T(8,128)(2,1)S(1)}, bf16[64,1024]{1,0:T(8,128)(2,1)S(1)}, u32[]{:S(2)}, u32[]{:S(2)}) collective-permute-start(bf16[64,1024]{1,0:T(8,128)(2,1)S(1)} %shard_map.64), channel_id=1, source_target_pairs={{0,8},{1,9},{2,10},{3,11},{4,12},{5,13},{6,14},{7,15}} | collective-permute-start | bytes 393224 | tf_op jit(solution)/shard_map/ppermute | solution.py:136
  23.0 3.4 %copy-start.1 = (bf16[1,4,1024,1024]{3,2,1,0:T(8,128)(2,1)S(1)}, bf16[1,4,1024,1024]{3,2,1,0:T(8,128)(2,1)}, u32[]{:S(2)}) copy-start(bf16[1,4,1024,1024]{3,2,1,0:T(8,128)(2,1)} %param.8) | copy-start | bytes 25165828
  26.9 0.8 %collective-permute-start.1 = (bf16[64,1024]{1,0:T(8,128)(2,1)S(1)}, bf16[64,1024]{1,0:T(8,128)(2,1)S(1)}, u32[]{:S(2)}, u32[]{:S(2)}) collective-permute-start(bf16[64,1024]{1,0:T(8,128)(2,1)S(1)} %shard_map.65), channel_id=1, source_target_pairs={{8,16},{9,17},{10,18},{11,19},{12,20},{13,21},{14,22},{15,23}} | collective-permute-start | bytes 393224 | tf_op jit(solution)/shard_map/ppermute | solution.py:136
  27.7 3.4 %copy-start.2 = (bf16[1,4,1024,1024]{3,2,1,0:T(8,128)(2,1)S(1)}, bf16[1,4,1024,1024]{3,2,1,0:T(8,128)(2,1)}, u32[]{:S(2)}) copy-start(bf16[1,4,1024,1024]{3,2,1,0:T(8,128)(2,1)} %param.8) | copy-start | bytes 25165828
  31.1 1.3 %copy-start.5 = (bf16[1024,640]{1,0:T(8,128)(2,1)S(1)}, bf16[1024,640]{1,0:T(8,128)(2,1)}, u32[]{:S(2)}) copy-start(bf16[1024,640]{1,0:T(8,128)(2,1)} %decoder.1) | copy-start | bytes 3932164
  31.1 1.3 %copy-start.8 = (f32[1024]{0:T(1024)S(1)}, f32[1024]{0:T(1024)}, u32[]{:S(2)}) copy-start(f32[1024]{0:T(1024)} %param.10) | copy-start | bytes 12292
  31.7 0.8 %collective-permute-start.2 = (bf16[64,1024]{1,0:T(8,128)(2,1)S(1)}, bf16[64,1024]{1,0:T(8,128)(2,1)S(1)}, u32[]{:S(2)}, u32[]{:S(2)}) collective-permute-start(bf16[64,1024]{1,0:T(8,128)(2,1)S(1)} %shard_map.66), channel_id=1, source_target_pairs={{16,24},{17,25},{18,26},{19,27},{20,28},{21,29},{22,30},{23,31}} | collective-permute-start | bytes 393224 | tf_op jit(solution)/shard_map/ppermute | solution.py:136
  32.4 3.4 %copy-start.3 = (bf16[1,4,1024,1024]{3,2,1,0:T(8,128)(2,1)S(1)}, bf16[1,4,1024,1024]{3,2,1,0:T(8,128)(2,1)}, u32[]{:S(2)}) copy-start(bf16[1,4,1024,1024]{3,2,1,0:T(8,128)(2,1)} %param.8) | copy-start | bytes 25165828
  36.4 3.3 %collective-permute-start.3 = (f32[8,640]{1,0:T(8,128)S(1)}, f32[8,640]{1,0:T(8,128)S(1)}, u32[]{:S(2)}, u32[]{:S(2)}) collective-permute-start(f32[8,640]{1,0:T(8,128)S(1)} %get-tuple-element.9), channel_id=1, source_target_pairs={{24,0},{25,1},{26,8},{27,9},{28,16},{29,17},{30,24},{31,25}} | collective-permute-start | bytes 61448 | tf_op jit(solution)/shard_map/ppermute | solution.py:153
  37.0 2.7 %collective-permute-start.4 = (f32[8,640]{1,0:T(8,128)S(1)}, f32[8,640]{1,0:T(8,128)S(1)}, u32[]{:S(2)}, u32[]{:S(2)}) collective-permute-start(f32[8,640]{1,0:T(8,128)S(1)} %get-tuple-element.10), channel_id=1, source_target_pairs={{24,2},{25,3},{26,10},{27,11},{28,18},{29,19},{30,26},{31,27}} | collective-permute-start | bytes 61448 | tf_op jit(solution)/shard_map/ppermute | solution.py:153
  37.7 2.0 %collective-permute-start.5 = (f32[8,640]{1,0:T(8,128)S(1)}, f32[8,640]{1,0:T(8,128)S(1)}, u32[]{:S(2)}, u32[]{:S(2)}) collective-permute-start(f32[8,640]{1,0:T(8,128)S(1)} %get-tuple-element.11), channel_id=1, source_target_pairs={{24,4},{25,5},{26,12},{27,13},{28,20},{29,21},{30,28},{31,29}} | collective-permute-start | bytes 61448 | tf_op jit(solution)/shard_map/ppermute | solution.py:153
  38.4 28.5 %collective-permute-start.6 = (f32[8,640]{1,0:T(8,128)S(1)}, f32[8,640]{1,0:T(8,128)S(1)}, u32[]{:S(2)}, u32[]{:S(2)}) collective-permute-start(f32[8,640]{1,0:T(8,128)S(1)} %get-tuple-element.12), channel_id=1, source_target_pairs={{24,6},{25,7},{26,14},{27,15},{28,22},{29,23},{30,30},{31,31}} | collective-permute-start | bytes 61448 | tf_op jit(solution)/shard_map/ppermute | solution.py:153

commit v2 on v1

--- a/solution.py
+++ b/solution.py
@@ -12,7 +12,6 @@
 EPSILON = 1e-06
 BOTH = ("segment", "lon")
 VMEM_SPEC = pl.BlockSpec(memory_space=pltpu.VMEM)
-SMEM_SPEC = pl.BlockSpec(memory_space=pltpu.SMEM)
 
 
 def matmul(left, right):
@@ -60,94 +59,126 @@
     return (wide + matmul(attended, weights[3])).astype(jnp.bfloat16)
 
 
-def first_kernel(place, patches, encoder, weights, gain, out):
-    @pl.when(place[0] == 1)
+def load_kernel(*refs):
+    count = (len(refs) - 1) // 2
+    sources, targets, sems = refs[:count], refs[count:-1], refs[-1]
+    copies = []
+    for source, target in zip(sources, targets):
+        for part in range(source.shape[0]):
+            sem = sems.at[len(copies)]
+            copies.append(pltpu.make_async_copy(source.at[part], target.at[part], sem))
+    for copy in copies:
+        copy.start()
+    for copy in copies:
+        copy.wait()
+
+
+def load(arrays):
+    size = sum(value.size * value.dtype.itemsize for value in arrays)
+    return pl.pallas_call(
+        load_kernel,
+        out_shape=[pltpu.VMEM(value.shape, value.dtype) for value in arrays],
+        in_specs=[pl.BlockSpec(memory_space=pltpu.HBM)] * len(arrays),
+        out_specs=[VMEM_SPEC] * len(arrays),
+        scratch_shapes=[pltpu.SemaphoreType.DMA((sum(value.shape[0] for value in arrays),))],
+        compiler_params=pltpu.CompilerParams(vmem_limit_bytes=1024 * 1024),
+        cost_estimate=pl.CostEstimate(flops=0, bytes_accessed=2 * size, transcendentals=0),
+    )(*[pltpu.with_memory_space_constraint(value, pltpu.HBM) for value in arrays])
+
+
+def first_kernel(*refs):
+    pieces, (encoder, weights, gain, out) = refs[:-4], refs[-4:]
+
+    @pl.when(lax.axis_index("segment") == 0)
     def _():
-        latent = matmul(patches[...], encoder[...]).astype(jnp.bfloat16)
+        patches = jnp.concatenate([piece[...] for piece in pieces], axis=0)
+        latent = matmul(patches, encoder[0]).astype(jnp.bfloat16)
         out[...] = layer(latent, weights, gain[...])
 
 
-def middle_kernel(place, latent, weights, gain, out):
-    @pl.when(place[0] == 1)
+def middle_kernel(tick, latent, weights, gain, out):
+    @pl.when(lax.axis_index("segment") == tick)
     def _():
         out[...] = layer(latent[...], weights, gain[...])
 
 
-def last_kernel(group, place, latent, weights, gain, final_gain, decoder, *rest):
+def last_kernel(tick, group, rows, latent, weights, gain, final_gain, decoder, *rest):
     outs, decoded = rest[:-1], rest[-1]
 
-    @pl.when(place[0] == 1)
+    @pl.when(lax.axis_index("segment") == tick)
     def _():
         mixed = layer(latent[...], weights, gain[...])
         final = norm_rows(mixed.astype(jnp.float32), final_gain[...])
-        decoded[...] = matmul(final, decoder[...])
-        rows = outs[0].shape[0]
+        decoded[...] = matmul(final, decoder[0])
         for index, out in enumerate(outs):
-            start = pl.multiple_of((index * group + place[1]) * rows, 8)
-            out[...] = decoded[pl.ds(start, rows), :]
+            start = index * group * rows
+            out[...] = decoded[start : start + rows, :]
 
 
 def in_vmem(value):
     return pltpu.with_memory_space_constraint(value, pltpu.VMEM)
 
 
-def call(kernel, out_shape, place, operands, scratch=()):
+def call(kernel, out_shape, operands, scratch=()):
     return pl.pallas_call(
         kernel,
         out_shape=out_shape,
-        in_specs=[SMEM_SPEC] + [VMEM_SPEC] * len(operands),
+        in_specs=[VMEM_SPEC] * len(operands),
         out_specs=jax.tree.map(lambda _: VMEM_SPEC, out_shape),
         scratch_shapes=list(scratch),
-        compiler_params=pltpu.CompilerParams(vmem_limit_bytes=24 * 1024 * 1024),
-    )(place, *operands)
+        compiler_params=pltpu.CompilerParams(vmem_limit_bytes=8 * 1024 * 1024),
+    )(*operands)
+
+
+def everywhere(segments, lons, mask):
+    return [(s * lons + i, s * lons + (i ^ mask)) for s in range(segments) for i in range(lons)]
 
 
 def body(patches, encoder_weight, layer_weights, layer_gains, final_gain, decoder_weight):
     segments = lax.axis_size("segment")
     lons = lax.axis_size("lon")
-    segment_id = lax.axis_index("segment")
-    lon_id = lax.axis_index("lon")
     bands, band_rows, lon_local, patch_values = patches.shape
     assert band_rows == 1 and bands == segments and lons % bands == 0
+    assert lons & (lons - 1) == 0 and bands & (bands - 1) == 0
     group = lons // bands
     columns = lons * lon_local
     width = encoder_weight.shape[1]
     out_values = decoder_weight.shape[1]
 
-    weights = in_vmem(layer_weights[0])
-    gain = layer_gains
-    member = lon_id % group
+    band = lax.axis_index("lon") // group
+    held = patches[:, 0]
+    step = 1
+    while step < group:
+        other = lax.ppermute(held, BOTH, everywhere(segments, lons, step))
+        held = jnp.concatenate([held, other], axis=1)
+        step *= 2
+    pieces = [lax.dynamic_index_in_dim(held, band, 0, keepdims=False)]
+    for k in range(1, bands):
+        sent = lax.dynamic_index_in_dim(held, band ^ k, 0, keepdims=False)
+        pieces.append(lax.ppermute(sent, BOTH, everywhere(segments, lons, k * group)))
 
-    sent = jnp.repeat(patches[:, 0], group, axis=0)
-    circle = lax.all_to_all(sent, "lon", 0, 0, tiled=True).reshape(columns, patch_values)
+    loaded = load([layer_weights[0], encoder_weight[None], decoder_weight[None], layer_gains, final_gain[None]])
+    weights, encoder, decoder, gain, final_gain = [in_vmem(value) for value in loaded]
 
     latent_shape = jax.ShapeDtypeStruct((columns, width), jnp.bfloat16)
-    latent = None
-    for tick in range(segments):
-        place = jnp.stack([(segment_id == tick).astype(jnp.int32), member.astype(jnp.int32)])
-        if tick == 0:
-            latent = call(
-                first_kernel, latent_shape, place, [circle, in_vmem(encoder_weight), weights, gain]
-            )
-        elif tick < segments - 1:
-            latent = call(middle_kernel, latent_shape, place, [latent, weights, gain])
+    part_shape = jax.ShapeDtypeStruct((lon_local, out_values), jnp.float32)
+    latent = call(first_kernel, latent_shape, pieces + [encoder, weights, gain])
+    for tick in range(1, segments):
+        pairs = [((tick - 1) * lons + i, tick * lons + i) for i in range(lons)]
+        latent = lax.ppermute(latent, BOTH, pairs)
         if tick < segments - 1:
-            pairs = [(tick * lons + i, (tick + 1) * lons + i) for i in range(lons)]
-            latent = lax.ppermute(latent, BOTH, pairs)
-            continue
-        part_shape = jax.ShapeDtypeStruct((lon_local, out_values), jnp.float32)
-        parts = call(
-            functools.partial(last_kernel, group),
-            [part_shape] * bands,
-            place,
-            [latent, weights, gain, final_gain[None], in_vmem(decoder_weight)],
-            [pltpu.VMEM((columns, out_values), jnp.float32)],
-        )
+            latent = call(functools.partial(middle_kernel, tick), latent_shape, [latent, weights, gain])
+    parts = call(
+        functools.partial(last_kernel, segments - 1, group, lon_local),
+        [part_shape] * bands,
+        [latent, weights, gain, final_gain, decoder],
+        [pltpu.VMEM((columns, out_values), jnp.float32)],
+    )
     received = []
     for index, part in enumerate(parts):
         pairs = [
-            ((segments - 1) * lons + band * group + i, band * lons + index * group + i)
-            for band in range(bands)
+            ((segments - 1) * lons + b * group + i, b * lons + (b ^ index) * group + i)
+            for b in range(bands)
             for i in range(group)
         ]
         received.append(lax.ppermute(part, BOTH, pairs))

time: 68 us -> 50.1 us (0.74)
  the two profiles are of different devices: /device:TPU:24 before, /device:TPU:6 now
where the time goes in v2:
time: 50.1 us; the launch traced here: 49.8 us
  waiting for transfers between devices  28 us (56%)
  starting transfers between devices  12.9 us (26%)
  Pallas kernels  7.36 us (15%)
  other arithmetic  1.38 us (3%)
    ppermute x3, waiting for transfers between devices, body(): latent = lax.ppermute(latent, BOTH, pairs)  21 us
    ppermute x4, starting transfers between devices, body(): received.append(lax.ppermute(part, BOTH, pairs))  5.79 us
    ppermute x4, waiting for transfers between devices, body(): received.append(lax.ppermute(part, BOTH, pairs))  5.53 us
    ppermute x3, starting transfers between devices, body(): lax.ppermute(sent, BOTH, everywhere(segments, lons, k * group))  4.45 us
    pallas_call x1, Pallas kernels, load(): pl.pallas_call(load_kernel, out_shape=[pltpu.VMEM(value.shape, value.dtyp...  4.22 us
    pallas_call x4, Pallas kernels, call(): pl.pallas_call(kernel, out_shape=out_shape, in_specs=[VMEM_SPEC] * len(op...  3.13 us
    ppermute x3, starting transfers between devices, body(): latent = lax.ppermute(latent, BOTH, pairs)  2.63 us
    ppermute x1, waiting for transfers between devices, body(): other = lax.ppermute(held, BOTH, everywhere(segments, lons, step))  1.43 us
  transfers between devices with their start and end apart: 11, of which 3 were waited for; matrix products, arithmetic and copies ran while one was open for 0% of the time, Pallas kernels for 8%

profile of v2, /device:TPU:6, one launch (start us, length us, event | category | flops | bytes accessed | tf_op | source)
XLA Modules:
  0.0 49.8 jit_solution(5333932533474941335)
XLA Ops:
  0.0 0.0 collective-permute-start
  0.0 1.4 %collective-permute-done = bf16[4,8,640]{2,1,0:T(8,128)(2,1)S(1)} collective-permute-done((bf16[4,8,640]{2,1,0:T(8,128)(2,1)}, bf16[4,8,640]{2,1,0:T(8,128)(2,1)S(1)}, u32[]{:S(2)}, u32[]{:S(2)}) %collective-permute-start) | collective-permute-done | bytes 40992 | tf_op jit(solution)/shard_map/ppermute | solution.py:152
  1.4 0.8 %fusion.1 = (bf16[16,640]{1,0:T(8,128)(2,1)S(1)}, bf16[16,640]{1,0:T(8,128)(2,1)S(1)}, bf16[16,640]{1,0:T(8,128)(2,1)S(1)}, bf16[16,640]{1,0:T(8,128)(2,1)S(1)}) fusion(s32[]{:T(128)S(6)} %select_n.22, bf16[4,8,640]{2,1,0:T(8,128)(2,1)} %bitcast.19, bf16[4,8,640]{2,1,0:T(8,128)(2,1)S(1)} %collective-permute-done, s32[]{:T(128)S(6)} %select_n.19, ...), kind=kLoop, calls=%fused_computation.9 | loop fusion | flops 163840 | bytes 163856 | tf_op jit(solution)/shard_map/jit(dynamic_index_in_dim)/squeeze | solution.py:157
  2.2 3.7 %collective-permute-start.3 = (bf16[16,640]{1,0:T(8,128)(2,1)S(1)}, bf16[16,640]{1,0:T(8,128)(2,1)S(1)}, u32[]{:S(2)}, u32[]{:S(2)}) collective-permute-start(bf16[16,640]{1,0:T(8,128)(2,1)S(1)} %get-tuple-element.23), channel_id=1, source_target_pairs={{0,6},{1,7},{2,4},{3,5},{4,2},{5,3},{6,0},{7,1},{8,14},{9,15},{10,... | collective-permute-start | bytes 61448 | tf_op jit(solution)/shard_map/ppermute | solution.py:158
  5.9 0.0 collective-permute-start.1
  5.9 0.8 %collective-permute-start.2 = (bf16[16,640]{1,0:T(8,128)(2,1)S(1)}, bf16[16,640]{1,0:T(8,128)(2,1)S(1)}, u32[]{:S(2)}, u32[]{:S(2)}) collective-permute-start(bf16[16,640]{1,0:T(8,128)(2,1)S(1)} %get-tuple-element.26), channel_id=1, source_target_pairs={{0,4},{1,5},{2,6},{3,7},{4,0},{5,1},{6,2},{7,3},{8,12},{9,13},{10,... | collective-permute-start | bytes 61448 | tf_op jit(solution)/shard_map/ppermute | solution.py:158
  6.6 4.2 %shard_map.64 = (bf16[4,1024,1024]{2,1,0:T(8,128)(2,1)S(1)}, bf16[1,640,1024]{2,1,0:T(8,128)(2,1)S(1)}, bf16[1,1024,640]{2,1,0:T(8,128)(2,1)S(1)}, f32[1,1024]{1,0:T(1,128)S(1)}, f32[1,1024]{1,0:T(1,128)S(1)}) custom-call(bf16[4,1024,1024]{2,1,0:T(8,128)(2,1)} %bitcast.15, bf16[1,640,1024]{2,1,0:T(8,128)(2,1)} %bitcast.16, bf16[1,1024,640]{2,1,0:T(8,128)(2,1)} %bitcast.17, ...), custom_call_target="tpu_custom_call" | custom-call | bytes 22036480 | tf_op jit(solution)/shard_map/pallas_call | solution.py:78
  10.9 0.0 collective-permute-done.3.refs_3_
  10.9 0.0 collective-permute-done.1.refs_1_
  10.9 0.0 collective-permute-done.2.refs_2_
  10.9 0.7 %collective-permute-start.4 = (bf16[64,1024]{1,0:T(8,128)(2,1)S(1)}, bf16[64,1024]{1,0:T(8,128)(2,1)S(1)}, u32[]{:S(2)}, u32[]{:S(2)}) collective-permute-start(bf16[64,1024]{1,0:T(8,128)(2,1)S(1)} %shard_map.65), channel_id=1, source_target_pairs={{0,8},{1,9},{2,10},{3,11},{4,12},{5,13},{6,14},{7,15}} | collective-permute-start | bytes 393224 | tf_op jit(solution)/shard_map/ppermute | solution.py:168
  11.6 0.0 collective-permute-done.4.latent
  11.7 0.7 %collective-permute-start.5 = (bf16[64,1024]{1,0:T(8,128)(2,1)S(1)}, bf16[64,1024]{1,0:T(8,128)(2,1)S(1)}, u32[]{:S(2)}, u32[]{:S(2)}) collective-permute-start(bf16[64,1024]{1,0:T(8,128)(2,1)S(1)} %shard_map.66), channel_id=1, source_target_pairs={{8,16},{9,17},{10,18},{11,19},{12,20},{13,21},{14,22},{15,23}} | collective-permute-start | bytes 393224 | tf_op jit(solution)/shard_map/ppermute | solution.py:168
  12.3 0.0 collective-permute-done.5.latent
  12.4 1.3 %collective-permute-start.6 = (bf16[64,1024]{1,0:T(8,128)(2,1)S(1)}, bf16[64,1024]{1,0:T(8,128)(2,1)S(1)}, u32[]{:S(2)}, u32[]{:S(2)}) collective-permute-start(bf16[64,1024]{1,0:T(8,128)(2,1)S(1)} %shard_map.67), channel_id=1, source_target_pairs={{16,24},{17,25},{18,26},{19,27},{20,28},{21,29},{22,30},{23,31}} | collective-permute-start | bytes 393224 | tf_op jit(solution)/shard_map/ppermute | solution.py:168
  13.7 21.0 %collective-permute-done.6.latent = bf16[64,1024]{1,0:T(8,128)(2,1)S(1)} collective-permute-done((bf16[64,1024]{1,0:T(8,128)(2,1)S(1)}, bf16[64,1024]{1,0:T(8,128)(2,1)S(1)}, u32[]{:S(2)}, u32[]{:S(2)}) %collective-permute-start.6) | collective-permute-done | bytes 131104 | tf_op jit(solution)/shard_map/ppermute | solution.py:168
  34.7 3.1 %shard_map.68 = (f32[8,640]{1,0:T(8,128)S(1)}, f32[8,640]{1,0:T(8,128)S(1)}, f32[8,640]{1,0:T(8,128)S(1)}, f32[8,640]{1,0:T(8,128)S(1)}) custom-call(bf16[64,1024]{1,0:T(8,128)(2,1)S(1)} %collective-permute-done.6.latent, bf16[4,1024,1024]{2,1,0:T(8,128)(2,1)S(1)} %get-tuple-element.15.refs_5_.weights, f32[1,1024]{1,0:T(1,128)S(1)} %get-tuple-element.16.refs_6_.gain, ...), custom_call_target="tpu_custom_call" | custom-call | tf_op jit(solution)/shard_map/pallas_call | solution.py:123
  37.8 1.3 %collective-permute-start.7 = (f32[8,640]{1,0:T(8,128)S(1)}, f32[8,640]{1,0:T(8,128)S(1)}, u32[]{:S(2)}, u32[]{:S(2)}) collective-permute-start(f32[8,640]{1,0:T(8,128)S(1)} %get-tuple-element.19), channel_id=1, source_target_pairs={{24,0},{25,1},{26,10},{27,11},{28,20},{29,21},{30,30},{31,31}} | collective-permute-start | bytes 61448 | tf_op jit(solution)/shard_map/ppermute | solution.py:184
  39.1 1.3 %collective-permute-start.8 = (f32[8,640]{1,0:T(8,128)S(1)}, f32[8,640]{1,0:T(8,128)S(1)}, u32[]{:S(2)}, u32[]{:S(2)}) collective-permute-start(f32[8,640]{1,0:T(8,128)S(1)} %get-tuple-element.20), channel_id=1, source_target_pairs={{24,2},{25,3},{26,8},{27,9},{28,22},{29,23},{30,28},{31,29}} | collective-permute-start | bytes 61448 | tf_op jit(solution)/shard_map/ppermute | solution.py:184
  40.4 1.3 %collective-permute-start.9 = (f32[8,640]{1,0:T(8,128)S(1)}, f32[8,640]{1,0:T(8,128)S(1)}, u32[]{:S(2)}, u32[]{:S(2)}) collective-permute-start(f32[8,640]{1,0:T(8,128)S(1)} %get-tuple-element.21), channel_id=1, source_target_pairs={{24,4},{25,5},{26,14},{27,15},{28,16},{29,17},{30,26},{31,27}} | collective-permute-start | bytes 61448 | tf_op jit(solution)/shard_map/ppermute | solution.py:184
  41.7 1.9 %collective-permute-start.10 = (f32[8,640]{1,0:T(8,128)S(1)}, f32[8,640]{1,0:T(8,128)S(1)}, u32[]{:S(2)}, u32[]{:S(2)}) collective-permute-start(f32[8,640]{1,0:T(8,128)S(1)} %get-tuple-element.22), channel_id=1, source_target_pairs={{24,6},{25,7},{26,12},{27,13},{28,18},{29,19},{30,24},{31,25}} | collective-permute-start | bytes 61448 | tf_op jit(solution)/shard_map/ppermute | solution.py:184
  43.6 0.0 collective-permute-done.7
  43.6 0.0 collective-permute-done.8
  43.6 0.0 collective-permute-done.9
  43.6 5.5 %collective-permute-done.10 = f32[8,640]{1,0:T(8,128)S(1)} collective-permute-done((f32[8,640]{1,0:T(8,128)S(1)}, f32[8,640]{1,0:T(8,128)S(1)}, u32[]{:S(2)}, u32[]{:S(2)}) %collective-permute-start.10) | collective-permute-done | bytes 20512 | tf_op jit(solution)/shard_map/ppermute | solution.py:184
  49.2 0.6 %add_bitcast_fusion = f32[1,1,8,640]{3,2,1,0:T(8,128)} fusion(f32[8,640]{1,0:T(8,128)S(1)} %collective-permute-done.10, f32[8,640]{1,0:T(8,128)S(1)} %collective-permute-done.9, f32[8,640]{1,0:T(8,128)S(1)} %collective-permute-done.7, f32[8,640]{1,0:T(8,128)S(1)} %collective-permute-done.8), kind=kLoop, calls=%fused_computation.16 | loop fusion | flops 15360 | bytes 102400 | tf_op jit(solution)/shard_map/broadcast_in_dim | solution.py:185
  (3 shorter events, 0.0 us)
Async XLA Ops:
  0.0 1.4 %collective-permute-start = (bf16[4,8,640]{2,1,0:T(8,128)(2,1)}, bf16[4,8,640]{2,1,0:T(8,128)(2,1)S(1)}, u32[]{:S(2)}, u32[]{:S(2)}) collective-permute-start(bf16[4,8,640]{2,1,0:T(8,128)(2,1)} %bitcast.18), channel_id=1, source_target_pairs={{0,1},{1,0},{2,3},{3,2},{4,5},{5,4},{6,7},{7,6},{8,9},{9,8},{10,11... | collective-permute-start | bytes 122888 | tf_op jit(solution)/shard_map/ppermute | solution.py:152
  2.2 8.7 %collective-permute-start.3 = (bf16[16,640]{1,0:T(8,128)(2,1)S(1)}, bf16[16,640]{1,0:T(8,128)(2,1)S(1)}, u32[]{:S(2)}, u32[]{:S(2)}) collective-permute-start(bf16[16,640]{1,0:T(8,128)(2,1)S(1)} %get-tuple-element.23), channel_id=1, source_target_pairs={{0,6},{1,7},{2,4},{3,5},{4,2},{5,3},{6,0},{7,1},{8,14},{9,15},{10,... | collective-permute-start | bytes 61448 | tf_op jit(solution)/shard_map/ppermute | solution.py:158
  5.9 5.0 %collective-permute-start.1 = (bf16[16,640]{1,0:T(8,128)(2,1)S(1)}, bf16[16,640]{1,0:T(8,128)(2,1)S(1)}, u32[]{:S(2)}, u32[]{:S(2)}) collective-permute-start(bf16[16,640]{1,0:T(8,128)(2,1)S(1)} %get-tuple-element.25), channel_id=1, source_target_pairs={{0,2},{1,3},{2,0},{3,1},{4,6},{5,7},{6,4},{7,5},{8,10},{9,11},{10,... | collective-permute-start | bytes 61448 | tf_op jit(solution)/shard_map/ppermute | solution.py:158
  5.9 5.0 %collective-permute-start.2 = (bf16[16,640]{1,0:T(8,128)(2,1)S(1)}, bf16[16,640]{1,0:T(8,128)(2,1)S(1)}, u32[]{:S(2)}, u32[]{:S(2)}) collective-permute-start(bf16[16,640]{1,0:T(8,128)(2,1)S(1)} %get-tuple-element.26), channel_id=1, source_target_pairs={{0,4},{1,5},{2,6},{3,7},{4,0},{5,1},{6,2},{7,3},{8,12},{9,13},{10,... | collective-permute-start | bytes 61448 | tf_op jit(solution)/shard_map/ppermute | solution.py:158
  10.9 0.7 %collective-permute-start.4 = (bf16[64,1024]{1,0:T(8,128)(2,1)S(1)}, bf16[64,1024]{1,0:T(8,128)(2,1)S(1)}, u32[]{:S(2)}, u32[]{:S(2)}) collective-permute-start(bf16[64,1024]{1,0:T(8,128)(2,1)S(1)} %shard_map.65), channel_id=1, source_target_pairs={{0,8},{1,9},{2,10},{3,11},{4,12},{5,13},{6,14},{7,15}} | collective-permute-start | bytes 393224 | tf_op jit(solution)/shard_map/ppermute | solution.py:168
  11.7 0.7 %collective-permute-start.5 = (bf16[64,1024]{1,0:T(8,128)(2,1)S(1)}, bf16[64,1024]{1,0:T(8,128)(2,1)S(1)}, u32[]{:S(2)}, u32[]{:S(2)}) collective-permute-start(bf16[64,1024]{1,0:T(8,128)(2,1)S(1)} %shard_map.66), channel_id=1, source_target_pairs={{8,16},{9,17},{10,18},{11,19},{12,20},{13,21},{14,22},{15,23}} | collective-permute-start | bytes 393224 | tf_op jit(solution)/shard_map/ppermute | solution.py:168
  12.4 22.3 %collective-permute-start.6 = (bf16[64,1024]{1,0:T(8,128)(2,1)S(1)}, bf16[64,1024]{1,0:T(8,128)(2,1)S(1)}, u32[]{:S(2)}, u32[]{:S(2)}) collective-permute-start(bf16[64,1024]{1,0:T(8,128)(2,1)S(1)} %shard_map.67), channel_id=1, source_target_pairs={{16,24},{17,25},{18,26},{19,27},{20,28},{21,29},{22,30},{23,31}} | collective-permute-start | bytes 393224 | tf_op jit(solution)/shard_map/ppermute | solution.py:168
  37.8 5.8 %collective-permute-start.7 = (f32[8,640]{1,0:T(8,128)S(1)}, f32[8,640]{1,0:T(8,128)S(1)}, u32[]{:S(2)}, u32[]{:S(2)}) collective-permute-start(f32[8,640]{1,0:T(8,128)S(1)} %get-tuple-element.19), channel_id=1, source_target_pairs={{24,0},{25,1},{26,10},{27,11},{28,20},{29,21},{30,30},{31,31}} | collective-permute-start | bytes 61448 | tf_op jit(solution)/shard_map/ppermute | solution.py:184
  39.1 4.5 %collective-permute-start.8 = (f32[8,640]{1,0:T(8,128)S(1)}, f32[8,640]{1,0:T(8,128)S(1)}, u32[]{:S(2)}, u32[]{:S(2)}) collective-permute-start(f32[8,640]{1,0:T(8,128)S(1)} %get-tuple-element.20), channel_id=1, source_target_pairs={{24,2},{25,3},{26,8},{27,9},{28,22},{29,23},{30,28},{31,29}} | collective-permute-start | bytes 61448 | tf_op jit(solution)/shard_map/ppermute | solution.py:184
  40.4 3.3 %collective-permute-start.9 = (f32[8,640]{1,0:T(8,128)S(1)}, f32[8,640]{1,0:T(8,128)S(1)}, u32[]{:S(2)}, u32[]{:S(2)}) collective-permute-start(f32[8,640]{1,0:T(8,128)S(1)} %get-tuple-element.21), channel_id=1, source_target_pairs={{24,4},{25,5},{26,14},{27,15},{28,16},{29,17},{30,26},{31,27}} | collective-permute-start | bytes 61448 | tf_op jit(solution)/shard_map/ppermute | solution.py:184
  41.7 7.5 %collective-permute-start.10 = (f32[8,640]{1,0:T(8,128)S(1)}, f32[8,640]{1,0:T(8,128)S(1)}, u32[]{:S(2)}, u32[]{:S(2)}) collective-permute-start(f32[8,640]{1,0:T(8,128)S(1)} %get-tuple-element.22), channel_id=1, source_target_pairs={{24,6},{25,7},{26,12},{27,13},{28,18},{29,19},{30,24},{31,25}} | collective-permute-start | bytes 61448 | tf_op jit(solution)/shard_map/ppermute | solution.py:184

commit v3 on v2

--- a/solution.py
+++ b/solution.py
@@ -11,6 +11,8 @@
 SOFTCAP = 5.0
 EPSILON = 1e-06
 BOTH = ("segment", "lon")
+HOP_POWER = 1
+OUT_POWER = 1
 VMEM_SPEC = pl.BlockSpec(memory_space=pltpu.VMEM)
 
 
@@ -111,7 +113,7 @@
         final = norm_rows(mixed.astype(jnp.float32), final_gain[...])
         decoded[...] = matmul(final, decoder[0])
         for index, out in enumerate(outs):
-            start = index * group * rows
+            start = (index * group + (index == 0)) * rows
             out[...] = decoded[start : start + rows, :]
 
 
@@ -130,6 +132,59 @@
     )(*operands)
 
 
+def assign(cost):
+    size = len(cost)
+    row_price, column_price, owner = [0.0] * (size + 1), [0.0] * (size + 1), [0] * (size + 1)
+    for row in range(1, size + 1):
+        owner[0], column = row, 0
+        slack, back, seen = [float("inf")] * (size + 1), [0] * (size + 1), [False] * (size + 1)
+        while owner[column]:
+            seen[column], at, low, best = True, owner[column], float("inf"), 0
+            for other in range(1, size + 1):
+                if not seen[other]:
+                    left = cost[at - 1][other - 1] - row_price[at] - column_price[other]
+                    if left < slack[other]:
+                        slack[other], back[other] = left, column
+                    if slack[other] < low:
+                        low, best = slack[other], other
+            for other in range(size + 1):
+                if seen[other]:
+                    row_price[owner[other]] += low
+                    column_price[other] -= low
+                else:
+                    slack[other] -= low
+            column = best
+        while column:
+            owner[column] = owner[back[column]]
+            column = back[column]
+    chosen = [0] * size
+    for column in range(1, size + 1):
+        chosen[owner[column] - 1] = column - 1
+    return chosen
+
+
+def apart(one, two):
+    return bin(one[0] ^ two[0]).count("1") + abs(one[1] - two[1])
+
+
+def full_pairs(edges, segments, groups, group, cross, power):
+    nodes = [(s, g) for s in range(segments) for g in range(groups)]
+    targets = set(edges.values())
+    senders = [node for node in nodes if node not in edges]
+    takers = [node for node in nodes if node not in targets]
+    table = [
+        [apart(one, two) ** power + 0.01 if one != two else 0.0 for two in takers] for one in senders
+    ]
+    filled = {one: takers[column] for one, column in zip(senders, assign(table))}
+    pairs = []
+    for one in nodes:
+        two = edges.get(one) or filled[one]
+        flip = 1 if one == two or (cross and one in edges) else 0
+        for c in range(group):
+            pairs.append(((one[0] * groups + one[1]) * group + c, (two[0] * groups + two[1]) * group + (c ^ flip)))
+    return pairs
+
+
 def everywhere(segments, lons, mask):
     return [(s * lons + i, s * lons + (i ^ mask)) for s in range(segments) for i in range(lons)]
 
@@ -139,23 +194,26 @@
     lons = lax.axis_size("lon")
     bands, band_rows, lon_local, patch_values = patches.shape
     assert band_rows == 1 and bands == segments and lons % bands == 0
-    assert lons & (lons - 1) == 0 and bands & (bands - 1) == 0
+    assert lons & (lons - 1) == 0 and bands & (bands - 1) == 0 and 1 < bands < lons
     group = lons // bands
     columns = lons * lon_local
     width = encoder_weight.shape[1]
     out_values = decoder_weight.shape[1]
 
-    band = lax.axis_index("lon") // group
-    held = patches[:, 0]
+    place = lax.axis_index("lon") // group
+    own = patches[:, 0]
     step = 1
     while step < group:
-        other = lax.ppermute(held, BOTH, everywhere(segments, lons, step))
-        held = jnp.concatenate([held, other], axis=1)
+        other = lax.ppermute(own, BOTH, everywhere(segments, lons, step))
+        picked = [lax.dynamic_index_in_dim(own, place ^ k ^ 1, 0, keepdims=False) for k in range(bands)]
+        picked = lax.optimization_barrier(picked) if step == 1 else picked
+        own = jnp.concatenate([own, other], axis=1)
         step *= 2
-    pieces = [lax.dynamic_index_in_dim(held, band, 0, keepdims=False)]
-    for k in range(1, bands):
-        sent = lax.dynamic_index_in_dim(held, band ^ k, 0, keepdims=False)
-        pieces.append(lax.ppermute(sent, BOTH, everywhere(segments, lons, k * group)))
+    pieces = []
+    for k in range(bands):
+        theirs = lax.dynamic_index_in_dim(other, place ^ k ^ 1, 0, keepdims=False)
+        piece = jnp.concatenate([picked[k], theirs], axis=0)
+        pieces.append(lax.ppermute(piece, BOTH, everywhere(segments, lons, k * group + 1)) if k else piece)
 
     loaded = load([layer_weights[0], encoder_weight[None], decoder_weight[None], layer_gains, final_gain[None]])
     weights, encoder, decoder, gain, final_gain = [in_vmem(value) for value in loaded]
@@ -164,8 +222,8 @@
     part_shape = jax.ShapeDtypeStruct((lon_local, out_values), jnp.float32)
     latent = call(first_kernel, latent_shape, pieces + [encoder, weights, gain])
     for tick in range(1, segments):
-        pairs = [((tick - 1) * lons + i, tick * lons + i) for i in range(lons)]
-        latent = lax.ppermute(latent, BOTH, pairs)
+        edges = {(tick - 1, g): (tick, g) for g in range(bands)}
+        latent = lax.ppermute(latent, BOTH, full_pairs(edges, segments, bands, group, False, HOP_POWER))
         if tick < segments - 1:
             latent = call(functools.partial(middle_kernel, tick), latent_shape, [latent, weights, gain])
     parts = call(
@@ -174,15 +232,13 @@
         [latent, weights, gain, final_gain, decoder],
         [pltpu.VMEM((columns, out_values), jnp.float32)],
     )
-    received = []
-    for index, part in enumerate(parts):
-        pairs = [
-            ((segments - 1) * lons + b * group + i, b * lons + (b ^ index) * group + i)
-            for b in range(bands)
-            for i in range(group)
-        ]
-        received.append(lax.ppermute(part, BOTH, pairs))
-    return sum(received[1:], received[0])[None, None]
+    segment_id = lax.axis_index("segment")
+    answer = None
+    for k, part in enumerate(parts):
+        edges = {(segments - 1, g): (g ^ 1, g ^ k) for g in range(bands)}
+        taken = lax.ppermute(part, BOTH, full_pairs(edges, segments, bands, group, True, OUT_POWER))
+        answer = taken if k == 0 else jnp.where(place ^ segment_id ^ 1 == k, taken, answer)
+    return answer[None, None]
 
 
 def solution(mesh):

time: 50.1 us -> 43.7 us (0.87)
  the two profiles are of different devices: /device:TPU:6 before, /device:TPU:5 now
where the time goes in v3:
time: 43.7 us; the launch traced here: 42.9 us
  starting transfers between devices  20.4 us (47%)
  waiting for transfers between devices  14 us (32%)
  Pallas kernels  6.91 us (16%)
  local copies, waits for them, and re-layouts  0.77 us (2%)
  other arithmetic  0.63 us (1%)
    ppermute x3, starting transfers between devices, body(): lax.ppermute(latent, BOTH, full_pairs(edges, segments, bands, group, Fals...  9.88 us
    ppermute x3, waiting for transfers between devices, body(): lax.ppermute(latent, BOTH, full_pairs(edges, segments, bands, group, Fals...  7.75 us
    ppermute x4, starting transfers between devices, body(): lax.ppermute(part, BOTH, full_pairs(edges, segments, bands, group, True,...  5.85 us
    pallas_call x1, Pallas kernels, load(): pl.pallas_call(load_kernel, out_shape=[pltpu.VMEM(value.shape, value.dtyp...  4.22 us
    ppermute x3, starting transfers between devices, body(): lax.ppermute(piece, BOTH, everywhere(segments, lons, k * group + 1))  4.04 us
    ppermute x3, waiting for transfers between devices, body(): lax.ppermute(piece, BOTH, everywhere(segments, lons, k * group + 1))  3.48 us
    ppermute x4, waiting for transfers between devices, body(): lax.ppermute(part, BOTH, full_pairs(edges, segments, bands, group, True,...  2.81 us
    pallas_call x4, Pallas kernels, call(): pl.pallas_call(kernel, out_shape=out_shape, in_specs=[VMEM_SPEC] * len(op...  2.69 us
  transfers between devices with their start and end apart: 11, of which 6 were waited for; matrix products, arithmetic and copies ran while one was open for 2% of the time, Pallas kernels for 10%

profile of v3, /device:TPU:5, one launch (start us, length us, event | category | flops | bytes accessed | tf_op | source)
XLA Modules:
  0.0 42.9 jit_solution(17332124453466677339)
XLA Ops:
  0.0 0.7 %collective-permute-start = (bf16[4,8,640]{2,1,0:T(8,128)(2,1)}, bf16[4,8,640]{2,1,0:T(8,128)(2,1)S(1)}, u32[]{:S(2)}, u32[]{:S(2)}) collective-permute-start(bf16[4,8,640]{2,1,0:T(8,128)(2,1)} %bitcast.26), channel_id=1, source_target_pairs={{0,1},{1,0},{2,3},{3,2},{4,5},{5,4},{6,7},{7,6},{8,9},{9,8},{10,11... | collective-permute-start | bytes 122888 | tf_op jit(solution)/shard_map/ppermute | solution.py:207
  0.7 0.8 %dynamic-slice_bitcast_fusion.4 = (bf16[8,640]{1,0:T(8,128)(2,1)S(1)}, bf16[8,640]{1,0:T(8,128)(2,1)S(1)}, bf16[8,640]{1,0:T(8,128)(2,1)S(1)}, bf16[8,640]{1,0:T(8,128)(2,1)S(1)}) fusion(bf16[4,1,8,640]{3,2,1,0:T(8,128)(2,1)} %param.6, s32[]{:T(128)S(6)} %select_n.47, s32[]{:T(128)S(6)} %select_n.46, s32[]{:T(128)S(6)} %select_n.45, s32[]{:T(128)S(6)} %select_n.44), kind=kLoop, calls=%fused_computation.9 | loop fusion | bytes 81936 | tf_op jit(solution)/shard_map/jit(dynamic_index_in_dim)/squeeze | solution.py:208
  1.4 4.2 %shard_map.64 = (bf16[4,1024,1024]{2,1,0:T(8,128)(2,1)S(1)}, bf16[1,640,1024]{2,1,0:T(8,128)(2,1)S(1)}, bf16[1,1024,640]{2,1,0:T(8,128)(2,1)S(1)}, f32[1,1024]{1,0:T(1,128)S(1)}, f32[1,1024]{1,0:T(1,128)S(1)}) custom-call(bf16[4,1024,1024]{2,1,0:T(8,128)(2,1)} %bitcast.23, bf16[1,640,1024]{2,1,0:T(8,128)(2,1)} %bitcast.24, bf16[1,1024,640]{2,1,0:T(8,128)(2,1)} %bitcast.25, ...), custom_call_target="tpu_custom_call" | custom-call | bytes 22036480 | tf_op jit(solution)/shard_map/pallas_call | solution.py:80
  5.7 0.0 collective-permute-done
  5.7 3.3 %collective-permute-start.3 = (bf16[16,640]{1,0:T(8,128)(2,1)S(1)}, bf16[16,640]{1,0:T(8,128)(2,1)S(1)}, u32[]{:S(2)}, u32[]{:S(2)}) collective-permute-start(bf16[16,640]{1,0:T(8,128)(2,1)S(1)} %pad_maximum_fusion.3), channel_id=1, source_target_pairs={{0,7},{1,6},{2,5},{3,4},{4,3},{5,2},{6,1},{7,0},{8,15},{9,14},{10,... | collective-permute-start | bytes 61448 | tf_op jit(solution)/shard_map/ppermute | solution.py:216
  9.0 0.0 collective-permute-start.2
  9.0 0.8 %collective-permute-start.1 = (bf16[16,640]{1,0:T(8,128)(2,1)S(1)}, bf16[16,640]{1,0:T(8,128)(2,1)S(1)}, u32[]{:S(2)}, u32[]{:S(2)}) collective-permute-start(bf16[16,640]{1,0:T(8,128)(2,1)S(1)} %pad_maximum_fusion.1), channel_id=1, source_target_pairs={{0,3},{1,2},{2,1},{3,0},{4,7},{5,6},{6,5},{7,4},{8,11},{9,10},{10,... | collective-permute-start | bytes 61448 | tf_op jit(solution)/shard_map/ppermute | solution.py:216
  9.8 1.0 %collective-permute-done.3.refs_3_ = bf16[16,640]{1,0:T(8,128)(2,1)S(1)} collective-permute-done((bf16[16,640]{1,0:T(8,128)(2,1)S(1)}, bf16[16,640]{1,0:T(8,128)(2,1)S(1)}, u32[]{:S(2)}, u32[]{:S(2)}) %collective-permute-start.3) | collective-permute-done | bytes 20512 | tf_op jit(solution)/shard_map/ppermute | solution.py:216
  10.8 2.5 %collective-permute-done.2.refs_2_ = bf16[16,640]{1,0:T(8,128)(2,1)S(1)} collective-permute-done((bf16[16,640]{1,0:T(8,128)(2,1)S(1)}, bf16[16,640]{1,0:T(8,128)(2,1)S(1)}, u32[]{:S(2)}, u32[]{:S(2)}) %collective-permute-start.2) | collective-permute-done | bytes 20512 | tf_op jit(solution)/shard_map/ppermute | solution.py:216
  13.2 0.0 collective-permute-done.1.refs_1_
  13.2 0.4 collective-permute-start.4
  13.6 1.0 %collective-permute-done.4.latent = bf16[64,1024]{1,0:T(8,128)(2,1)S(1)} collective-permute-done((bf16[64,1024]{1,0:T(8,128)(2,1)S(1)}, bf16[64,1024]{1,0:T(8,128)(2,1)S(1)}, u32[]{:S(2)}, u32[]{:S(2)}) %collective-permute-start.4) | collective-permute-done | bytes 131104 | tf_op jit(solution)/shard_map/ppermute | solution.py:226
  14.6 9.4 %collective-permute-start.5 = (bf16[64,1024]{1,0:T(8,128)(2,1)S(1)}, bf16[64,1024]{1,0:T(8,128)(2,1)S(1)}, u32[]{:S(2)}, u32[]{:S(2)}) collective-permute-start(bf16[64,1024]{1,0:T(8,128)(2,1)S(1)} %shard_map.66), channel_id=1, source_target_pairs={{0,1},{1,0},{2,3},{3,2},{4,5},{5,4},{6,7},{7,6},{8,16},{9,17},{10,... | collective-permute-start | bytes 393224 | tf_op jit(solution)/shard_map/ppermute | solution.py:226
  24.0 3.0 %collective-permute-done.5.latent = bf16[64,1024]{1,0:T(8,128)(2,1)S(1)} collective-permute-done((bf16[64,1024]{1,0:T(8,128)(2,1)S(1)}, bf16[64,1024]{1,0:T(8,128)(2,1)S(1)}, u32[]{:S(2)}, u32[]{:S(2)}) %collective-permute-start.5) | collective-permute-done | bytes 131104 | tf_op jit(solution)/shard_map/ppermute | solution.py:226
  27.0 2.7 %shard_map.67 = bf16[64,1024]{1,0:T(8,128)(2,1)S(1)} custom-call(bf16[64,1024]{1,0:T(8,128)(2,1)S(1)} %collective-permute-done.5.latent, bf16[4,1024,1024]{2,1,0:T(8,128)(2,1)S(1)} %get-tuple-element.23.refs_5_.weights, f32[1,1024]{1,0:T(1,128)S(1)} %get-tuple-element.24.refs_6_.gain), custom_call_target="tpu_custom_call" | custom-call | tf_op jit(solution)/shard_map/pallas_call | solution.py:125
  29.7 0.1 collective-permute-start.6
  29.8 3.8 %collective-permute-done.6.latent = bf16[64,1024]{1,0:T(8,128)(2,1)S(1)} collective-permute-done((bf16[64,1024]{1,0:T(8,128)(2,1)S(1)}, bf16[64,1024]{1,0:T(8,128)(2,1)S(1)}, u32[]{:S(2)}, u32[]{:S(2)}) %collective-permute-start.6) | collective-permute-done | bytes 131104 | tf_op jit(solution)/shard_map/ppermute | solution.py:226
  33.6 2.6 %collective-permute-start.10 = (f32[8,640]{1,0:T(8,128)S(1)}, f32[8,640]{1,0:T(8,128)S(1)}, u32[]{:S(2)}, u32[]{:S(2)}) collective-permute-start(f32[8,640]{1,0:T(8,128)S(1)} %get-tuple-element.30), channel_id=1, source_target_pairs={{0,1},{1,0},{2,26},{3,27},{4,5},{5,4},{6,7},{7,6},{8,24},{9,25},{1... | collective-permute-start | bytes 61448 | tf_op jit(solution)/shard_map/ppermute | solution.py:239
  36.2 0.6 %collective-permute-start.7 = (f32[8,640]{1,0:T(8,128)S(1)}, f32[8,640]{1,0:T(8,128)S(1)}, u32[]{:S(2)}, u32[]{:S(2)}) collective-permute-start(f32[8,640]{1,0:T(8,128)S(1)} %get-tuple-element.27), channel_id=1, source_target_pairs={{0,1},{1,0},{2,3},{3,2},{4,28},{5,29},{6,7},{7,6},{8,9},{9,8},{10,... | collective-permute-start | bytes 61448 | tf_op jit(solution)/shard_map/ppermute | solution.py:239
  36.8 2.6 %collective-permute-start.8 = (f32[8,640]{1,0:T(8,128)S(1)}, f32[8,640]{1,0:T(8,128)S(1)}, u32[]{:S(2)}, u32[]{:S(2)}) collective-permute-start(f32[8,640]{1,0:T(8,128)S(1)} %get-tuple-element.28), channel_id=1, source_target_pairs={{0,1},{1,0},{2,3},{3,2},{4,5},{5,4},{6,30},{7,31},{8,9},{9,8},{10,... | collective-permute-start | bytes 61448 | tf_op jit(solution)/shard_map/ppermute | solution.py:239
  39.4 0.0 collective-permute-start.9
  39.4 0.0 collective-permute-done.10
  39.4 2.8 %collective-permute-done.7 = f32[8,640]{1,0:T(8,128)S(1)} collective-permute-done((f32[8,640]{1,0:T(8,128)S(1)}, f32[8,640]{1,0:T(8,128)S(1)}, u32[]{:S(2)}, u32[]{:S(2)}) %collective-permute-start.7) | collective-permute-done | bytes 20512 | tf_op jit(solution)/shard_map/ppermute | solution.py:239
  42.2 0.0 collective-permute-done.8
  42.2 0.0 collective-permute-done.9
  42.3 0.6 %select_bitcast_fusion = f32[1,1,8,640]{3,2,1,0:T(8,128)} fusion(f32[8,640]{1,0:T(8,128)S(1)} %collective-permute-done.7, f32[8,640]{1,0:T(8,128)S(1)} %collective-permute-done.8, f32[8,640]{1,0:T(8,128)S(1)} %collective-permute-done.9, f32[8,640]{1,0:T(8,128)S(1)} %collective-permute-done.10, pred[]{:T(512)S(6)} %eq.11, pred[]{:T(512)S(6)} %eq.10, pred[]{:T(512)S(6)} %eq.9), kind=kLoop, calls=%fused_computation.4 | loop fusion | flops 15360 | bytes 102403 | tf_op jit(solution)/shard_map/broadcast_in_dim | solution.py:241
  (8 shorter events, 0.0 us)
Async XLA Ops:
  0.0 5.7 %collective-permute-start = (bf16[4,8,640]{2,1,0:T(8,128)(2,1)}, bf16[4,8,640]{2,1,0:T(8,128)(2,1)S(1)}, u32[]{:S(2)}, u32[]{:S(2)}) collective-permute-start(bf16[4,8,640]{2,1,0:T(8,128)(2,1)} %bitcast.26), channel_id=1, source_target_pairs={{0,1},{1,0},{2,3},{3,2},{4,5},{5,4},{6,7},{7,6},{8,9},{9,8},{10,11... | collective-permute-start | bytes 122888 | tf_op jit(solution)/shard_map/ppermute | solution.py:207
  5.7 5.1 %collective-permute-start.3 = (bf16[16,640]{1,0:T(8,128)(2,1)S(1)}, bf16[16,640]{1,0:T(8,128)(2,1)S(1)}, u32[]{:S(2)}, u32[]{:S(2)}) collective-permute-start(bf16[16,640]{1,0:T(8,128)(2,1)S(1)} %pad_maximum_fusion.3), channel_id=1, source_target_pairs={{0,7},{1,6},{2,5},{3,4},{4,3},{5,2},{6,1},{7,0},{8,15},{9,14},{10,... | collective-permute-start | bytes 61448 | tf_op jit(solution)/shard_map/ppermute | solution.py:216
  9.0 4.3 %collective-permute-start.2 = (bf16[16,640]{1,0:T(8,128)(2,1)S(1)}, bf16[16,640]{1,0:T(8,128)(2,1)S(1)}, u32[]{:S(2)}, u32[]{:S(2)}) collective-permute-start(bf16[16,640]{1,0:T(8,128)(2,1)S(1)} %pad_maximum_fusion.2), channel_id=1, source_target_pairs={{0,5},{1,4},{2,7},{3,6},{4,1},{5,0},{6,3},{7,2},{8,13},{9,12},{10,... | collective-permute-start | bytes 61448 | tf_op jit(solution)/shard_map/ppermute | solution.py:216
  9.0 4.2 %collective-permute-start.1 = (bf16[16,640]{1,0:T(8,128)(2,1)S(1)}, bf16[16,640]{1,0:T(8,128)(2,1)S(1)}, u32[]{:S(2)}, u32[]{:S(2)}) collective-permute-start(bf16[16,640]{1,0:T(8,128)(2,1)S(1)} %pad_maximum_fusion.1), channel_id=1, source_target_pairs={{0,3},{1,2},{2,1},{3,0},{4,7},{5,6},{6,5},{7,4},{8,11},{9,10},{10,... | collective-permute-start | bytes 61448 | tf_op jit(solution)/shard_map/ppermute | solution.py:216
  13.2 1.4 %collective-permute-start.4 = (bf16[64,1024]{1,0:T(8,128)(2,1)S(1)}, bf16[64,1024]{1,0:T(8,128)(2,1)S(1)}, u32[]{:S(2)}, u32[]{:S(2)}) collective-permute-start(bf16[64,1024]{1,0:T(8,128)(2,1)S(1)} %shard_map.65), channel_id=1, source_target_pairs={{0,8},{1,9},{2,10},{3,11},{4,12},{5,13},{6,14},{7,15},{8,0},{9,1},... | collective-permute-start | bytes 393224 | tf_op jit(solution)/shard_map/ppermute | solution.py:226
  14.6 12.4 %collective-permute-start.5 = (bf16[64,1024]{1,0:T(8,128)(2,1)S(1)}, bf16[64,1024]{1,0:T(8,128)(2,1)S(1)}, u32[]{:S(2)}, u32[]{:S(2)}) collective-permute-start(bf16[64,1024]{1,0:T(8,128)(2,1)S(1)} %shard_map.66), channel_id=1, source_target_pairs={{0,1},{1,0},{2,3},{3,2},{4,5},{5,4},{6,7},{7,6},{8,16},{9,17},{10,... | collective-permute-start | bytes 393224 | tf_op jit(solution)/shard_map/ppermute | solution.py:226
  29.7 3.9 %collective-permute-start.6 = (bf16[64,1024]{1,0:T(8,128)(2,1)S(1)}, bf16[64,1024]{1,0:T(8,128)(2,1)S(1)}, u32[]{:S(2)}, u32[]{:S(2)}) collective-permute-start(bf16[64,1024]{1,0:T(8,128)(2,1)S(1)} %shard_map.67), channel_id=1, source_target_pairs={{0,1},{1,0},{2,3},{3,2},{4,5},{5,4},{6,7},{7,6},{8,9},{9,8},{10,11... | collective-permute-start | bytes 393224 | tf_op jit(solution)/shard_map/ppermute | solution.py:226
  33.6 5.9 %collective-permute-start.10 = (f32[8,640]{1,0:T(8,128)S(1)}, f32[8,640]{1,0:T(8,128)S(1)}, u32[]{:S(2)}, u32[]{:S(2)}) collective-permute-start(f32[8,640]{1,0:T(8,128)S(1)} %get-tuple-element.30), channel_id=1, source_target_pairs={{0,1},{1,0},{2,26},{3,27},{4,5},{5,4},{6,7},{7,6},{8,24},{9,25},{1... | collective-permute-start | bytes 61448 | tf_op jit(solution)/shard_map/ppermute | solution.py:239
  36.2 6.0 %collective-permute-start.7 = (f32[8,640]{1,0:T(8,128)S(1)}, f32[8,640]{1,0:T(8,128)S(1)}, u32[]{:S(2)}, u32[]{:S(2)}) collective-permute-start(f32[8,640]{1,0:T(8,128)S(1)} %get-tuple-element.27), channel_id=1, source_target_pairs={{0,1},{1,0},{2,3},{3,2},{4,28},{5,29},{6,7},{7,6},{8,9},{9,8},{10,... | collective-permute-start | bytes 61448 | tf_op jit(solution)/shard_map/ppermute | solution.py:239
  36.8 5.5 %collective-permute-start.8 = (f32[8,640]{1,0:T(8,128)S(1)}, f32[8,640]{1,0:T(8,128)S(1)}, u32[]{:S(2)}, u32[]{:S(2)}) collective-permute-start(f32[8,640]{1,0:T(8,128)S(1)} %get-tuple-element.28), channel_id=1, source_target_pairs={{0,1},{1,0},{2,3},{3,2},{4,5},{5,4},{6,30},{7,31},{8,9},{9,8},{10,... | collective-permute-start | bytes 61448 | tf_op jit(solution)/shard_map/ppermute | solution.py:239
  39.4 2.8 %collective-permute-start.9 = (f32[8,640]{1,0:T(8,128)S(1)}, f32[8,640]{1,0:T(8,128)S(1)}, u32[]{:S(2)}, u32[]{:S(2)}) collective-permute-start(f32[8,640]{1,0:T(8,128)S(1)} %get-tuple-element.29), channel_id=1, source_target_pairs={{0,24},{1,25},{2,3},{3,2},{4,5},{5,4},{6,7},{7,6},{8,9},{9,8},{10,... | collective-permute-start | bytes 61448 | tf_op jit(solution)/shard_map/ppermute | solution.py:239

commit v4 on v3

--- a/solution.py
+++ b/solution.py
@@ -13,11 +13,19 @@
 BOTH = ("segment", "lon")
 HOP_POWER = 1
 OUT_POWER = 1
+LOG2_E = 1.4426950408889634
+FULL_ROWS = 128
+EARLY = 2
+HBM_SPEC = pl.BlockSpec(memory_space=pltpu.HBM)
 VMEM_SPEC = pl.BlockSpec(memory_space=pltpu.VMEM)
 
 
 def matmul(left, right):
-    return jnp.dot(left, right, preferred_element_type=jnp.float32)
+    rows = left.shape[0]
+    times = max(1, FULL_ROWS // rows)
+    if times > 1:
+        left = jnp.concatenate([left] * times, axis=0)
+    return jnp.dot(left, right, preferred_element_type=jnp.float32)[:rows]
 
 
 def norm_rows(latent, gain):
@@ -30,105 +38,139 @@
     head_size = width // HEADS
     heads = min(4, HEADS)
     lanes = heads * head_size
-    lane_head = lax.broadcasted_iota(jnp.int32, (rows, lanes), 1) // head_size
-    own = [lane_head == head for head in range(heads)]
-    row_head = lax.broadcasted_iota(jnp.int32, (heads * rows, heads * rows), 0) // rows
-    column_head = lax.broadcasted_iota(jnp.int32, (heads * rows, heads * rows), 1) // rows
-    same_head = jnp.where(row_head == column_head, 1.0, 0.0).astype(jnp.bfloat16)
+    cuts = [slice(start, start + lanes) for start in range(0, width, lanes)]
+    turned = keys.T
+    key_head = lax.broadcasted_iota(jnp.int32, (lanes, rows), 0) // head_size
+    value_head = lax.broadcasted_iota(jnp.int32, (rows, lanes), 1) // head_size
+    row_head = lax.broadcasted_iota(jnp.int32, (heads * rows, lanes), 0) // rows
+    lane_head = lax.broadcasted_iota(jnp.int32, (heads * rows, lanes), 1) // head_size
+    same_head = jnp.where(row_head == lane_head, 1.0, 0.0).astype(jnp.bfloat16)
+    scores = []
+    for cut in cuts:
+        part = turned[cut]
+        block = [jnp.where(key_head == head, part, jnp.zeros_like(part)) for head in range(heads)]
+        scores.append(
+            jnp.dot(queries[:, cut], jnp.concatenate(block, axis=1), preferred_element_type=jnp.float32)
+        )
+    capped = jnp.tanh(jnp.concatenate(scores, axis=0) * (head_size ** (-0.5) / SOFTCAP))
+    raised = jnp.exp2(capped * (SOFTCAP * LOG2_E)).astype(jnp.bfloat16)
+    total = jnp.dot(raised, same_head, preferred_element_type=jnp.float32)
     outs = []
-    for start in range(0, width, lanes):
-        cut = slice(start, start + lanes)
-        zero = jnp.zeros((rows, lanes), jnp.bfloat16)
-        key_block = jnp.concatenate([jnp.where(mask, keys[:, cut], zero) for mask in own], axis=0)
-        value_block = jnp.concatenate([jnp.where(mask, values[:, cut], zero) for mask in own], axis=0)
-        scores = lax.dot_general(
-            queries[:, cut], key_block, (((1,), (1,)), ((), ())), preferred_element_type=jnp.float32
-        )
-        raised = jnp.exp(SOFTCAP * jnp.tanh(scores * (head_size ** (-0.5) / SOFTCAP)))
-        high = raised.astype(jnp.bfloat16)
-        low = (raised - high.astype(jnp.float32)).astype(jnp.bfloat16)
-        total = matmul(high, same_head) + matmul(low, same_head)
-        probability = (raised / total).astype(jnp.bfloat16)
-        outs.append(matmul(probability, value_block).astype(jnp.bfloat16))
+    for index, cut in enumerate(cuts):
+        part = values[:, cut]
+        block = [jnp.where(value_head == head, part, jnp.zeros_like(part)) for head in range(heads)]
+        mine = slice(index * rows, (index + 1) * rows)
+        mixed = jnp.dot(raised[mine], jnp.concatenate(block, axis=0), preferred_element_type=jnp.float32)
+        outs.append((mixed / total[mine]).astype(jnp.bfloat16))
     return jnp.concatenate(outs, axis=-1)
 
 
 def layer(latent, weights, gain):
     wide = latent.astype(jnp.float32)
     normed = norm_rows(wide, gain)
-    queries, keys, values = [matmul(normed, weights[i]).astype(jnp.bfloat16) for i in range(3)]
+    queries, keys, values = [matmul(normed, weights(i)).astype(jnp.bfloat16) for i in range(3)]
     attended = attend(queries, keys, values)
-    return (wide + matmul(attended, weights[3])).astype(jnp.bfloat16)
-
-
-def load_kernel(*refs):
-    count = (len(refs) - 1) // 2
-    sources, targets, sems = refs[:count], refs[count:-1], refs[-1]
-    copies = []
-    for source, target in zip(sources, targets):
-        for part in range(source.shape[0]):
-            sem = sems.at[len(copies)]
-            copies.append(pltpu.make_async_copy(source.at[part], target.at[part], sem))
-    for copy in copies:
-        copy.start()
-    for copy in copies:
-        copy.wait()
-
-
-def load(arrays):
-    size = sum(value.size * value.dtype.itemsize for value in arrays)
+    return (wide + matmul(attended, weights(3))).astype(jnp.bfloat16)
+
+
+def load_kernel(segments, hint, weights, encoder, decoder, gain, final_gain, *rest):
+    weights_out, encoder_out, decoder_out, gain_out, final_out, sems = rest
+    segment = lax.axis_index("segment")
+
+    def move(pairs):
+        copies = [
+            pltpu.make_async_copy(source, target, sems.at[index])
+            for index, (source, target) in enumerate(pairs)
+        ]
+        for copy in copies:
+            copy.start()
+        for copy in copies:
+            copy.wait()
+
+    early = [(weights.at[i], weights_out.at[i]) for i in range(EARLY)] + [(gain, gain_out)]
+    late = [(weights.at[i], weights_out.at[i]) for i in range(EARLY, 4)]
+
+    @pl.when(segment == 0)
+    def _():
+        move([(encoder, encoder_out)] + early)
+
+    @pl.when(segment > 0)
+    def _():
+        move(early + late)
+
+    @pl.when(segment == segments - 1)
+    def _():
+        move([(decoder, decoder_out), (final_gain, final_out)])
+
+
+def load(segments, hint, arrays):
     return pl.pallas_call(
-        load_kernel,
+        functools.partial(load_kernel, segments),
         out_shape=[pltpu.VMEM(value.shape, value.dtype) for value in arrays],
-        in_specs=[pl.BlockSpec(memory_space=pltpu.HBM)] * len(arrays),
+        in_specs=[pl.BlockSpec(memory_space=pl.ANY)] + [HBM_SPEC] * len(arrays),
         out_specs=[VMEM_SPEC] * len(arrays),
-        scratch_shapes=[pltpu.SemaphoreType.DMA((sum(value.shape[0] for value in arrays),))],
+        scratch_shapes=[pltpu.SemaphoreType.DMA((6,))],
         compiler_params=pltpu.CompilerParams(vmem_limit_bytes=1024 * 1024),
-        cost_estimate=pl.CostEstimate(flops=0, bytes_accessed=2 * size, transcendentals=0),
-    )(*[pltpu.with_memory_space_constraint(value, pltpu.HBM) for value in arrays])
+        cost_estimate=pl.CostEstimate(flops=0, bytes_accessed=16 * 1024 * 1024, transcendentals=0),
+    )(hint, *[in_hbm(value) for value in arrays])
 
 
 def first_kernel(*refs):
-    pieces, (encoder, weights, gain, out) = refs[:-4], refs[-4:]
+    pieces, (encoder, weights, all_weights, gain, out, fetched, sems) = refs[:-7], refs[-7:]
 
     @pl.when(lax.axis_index("segment") == 0)
     def _():
+        copies = [
+            pltpu.make_async_copy(all_weights.at[i], fetched.at[i - EARLY], sems.at[i - EARLY])
+            for i in range(EARLY, 4)
+        ]
+        for copy in copies:
+            copy.start()
+
+        def get(i):
+            if i < EARLY:
+                return weights[i]
+            copies[i - EARLY].wait()
+            return fetched[i - EARLY]
+
         patches = jnp.concatenate([piece[...] for piece in pieces], axis=0)
-        latent = matmul(patches, encoder[0]).astype(jnp.bfloat16)
-        out[...] = layer(latent, weights, gain[...])
+        latent = matmul(patches, encoder[...]).astype(jnp.bfloat16)
+        out[...] = layer(latent, get, gain[...])
 
 
 def middle_kernel(tick, latent, weights, gain, out):
     @pl.when(lax.axis_index("segment") == tick)
     def _():
-        out[...] = layer(latent[...], weights, gain[...])
-
-
-def last_kernel(tick, group, rows, latent, weights, gain, final_gain, decoder, *rest):
-    outs, decoded = rest[:-1], rest[-1]
-
+        out[...] = layer(latent[...], lambda i: weights[i], gain[...])
+
+
+def last_kernel(tick, group, rows, latent, weights, gain, final_gain, decoder, *outs):
     @pl.when(lax.axis_index("segment") == tick)
     def _():
-        mixed = layer(latent[...], weights, gain[...])
+        mixed = layer(latent[...], lambda i: weights[i], gain[...])
         final = norm_rows(mixed.astype(jnp.float32), final_gain[...])
-        decoded[...] = matmul(final, decoder[0])
+        decoded = matmul(final, decoder[...])
         for index, out in enumerate(outs):
             start = (index * group + (index == 0)) * rows
             out[...] = decoded[start : start + rows, :]
 
 
+def in_hbm(value):
+    return pltpu.with_memory_space_constraint(value, pltpu.HBM)
+
+
 def in_vmem(value):
     return pltpu.with_memory_space_constraint(value, pltpu.VMEM)
 
 
-def call(kernel, out_shape, operands, scratch=()):
+def call(kernel, out_shape, operands, in_specs=None, scratch=()):
     return pl.pallas_call(
         kernel,
         out_shape=out_shape,
-        in_specs=[VMEM_SPEC] * len(operands),
+        in_specs=in_specs or [VMEM_SPEC] * len(operands),
         out_specs=jax.tree.map(lambda _: VMEM_SPEC, out_shape),
         scratch_shapes=list(scratch),
-        compiler_params=pltpu.CompilerParams(vmem_limit_bytes=8 * 1024 * 1024),
+        compiler_params=pltpu.CompilerParams(vmem_limit_bytes=16 * 1024 * 1024),
     )(*operands)
 
 
@@ -215,12 +257,19 @@
         piece = jnp.concatenate([picked[k], theirs], axis=0)
         pieces.append(lax.ppermute(piece, BOTH, everywhere(segments, lons, k * group + 1)) if k else piece)
 
-    loaded = load([layer_weights[0], encoder_weight[None], decoder_weight[None], layer_gains, final_gain[None]])
+    every = layer_weights[0]
+    loaded = load(segments, pieces[0], [every, encoder_weight, decoder_weight, layer_gains, final_gain[None]])
     weights, encoder, decoder, gain, final_gain = [in_vmem(value) for value in loaded]
 
     latent_shape = jax.ShapeDtypeStruct((columns, width), jnp.bfloat16)
     part_shape = jax.ShapeDtypeStruct((lon_local, out_values), jnp.float32)
-    latent = call(first_kernel, latent_shape, pieces + [encoder, weights, gain])
+    latent = call(
+        first_kernel,
+        latent_shape,
+        pieces + [encoder, weights, in_hbm(every), gain],
+        [VMEM_SPEC] * (bands + 2) + [HBM_SPEC, VMEM_SPEC],
+        [pltpu.VMEM((4 - EARLY, width, width), jnp.bfloat16), pltpu.SemaphoreType.DMA((4 - EARLY,))],
+    )
     for tick in range(1, segments):
         edges = {(tick - 1, g): (tick, g) for g in range(bands)}
         latent = lax.ppermute(latent, BOTH, full_pairs(edges, segments, bands, group, False, HOP_POWER))
@@ -230,7 +279,6 @@
         functools.partial(last_kernel, segments - 1, group, lon_local),
         [part_shape] * bands,
         [latent, weights, gain, final_gain, decoder],
-        [pltpu.VMEM((columns, out_values), jnp.float32)],
     )
     segment_id = lax.axis_index("segment")
     answer = None

time: 43.7 us -> 37.2 us (0.85); the launches traced: 42.9 us -> 36.9 us
  starting transfers between devices: 20.4 us -> 18 us
  waiting for transfers between devices: 14 us -> 12.2 us
  Pallas kernels: 6.91 us -> 5.18 us
    ppermute x3, waiting for transfers between devices: 3.48 us -> 0.05 us  [body(): lax.ppermute(piece, BOTH, everywhere(segments, lons, k * group + 1))]
    pallas_call x5, Pallas kernels: 6.91 us -> 5.18 us  [the longest x1 3.53 us: load(): pl.pallas_call(functools.partial(load_kernel, segments), out_shape=[pltpu...]
    ppermute x4, starting transfers between devices: 5.85 us -> 4.55 us  [body(): lax.ppermute(part, BOTH, full_pairs(edges, segments, bands, group, True,...]
    ppermute x3, starting transfers between devices: 9.88 us -> 8.68 us  [body(): lax.ppermute(latent, BOTH, full_pairs(edges, segments, bands, group, Fals...]
    ppermute x4, waiting for transfers between devices: 2.81 us -> 3.7 us  [body(): lax.ppermute(part, BOTH, full_pairs(edges, segments, bands, group, True,...]
  transfers between devices with their start and end apart: 11 -> 11, of which waited for: 6 -> 5; matrix products, arithmetic and copies ran while one was open for 2% -> 2% of each run, Pallas kernels for 10% -> 10%
where the time goes in v4:
time: 37.2 us; the launch traced here: 36.9 us
  starting transfers between devices  18 us (48%)
  waiting for transfers between devices  12.2 us (33%)
  Pallas kernels  5.18 us (14%)
  local copies, waits for them, and re-layouts  0.76 us (2%)
  other arithmetic  0.63 us (2%)
    ppermute x3, starting transfers between devices, body(): lax.ppermute(latent, BOTH, full_pairs(edges, segments, bands, group, Fals...  8.68 us
    ppermute x3, waiting for transfers between devices, body(): lax.ppermute(latent, BOTH, full_pairs(edges, segments, bands, group, Fals...  8.16 us
    ppermute x4, starting transfers between devices, body(): lax.ppermute(part, BOTH, full_pairs(edges, segments, bands, group, True,...  4.55 us
    ppermute x3, starting transfers between devices, body(): lax.ppermute(piece, BOTH, everywhere(segments, lons, k * group + 1))  4.13 us
    ppermute x4, waiting for transfers between devices, body(): lax.ppermute(part, BOTH, full_pairs(edges, segments, bands, group, True,...  3.7 us
    pallas_call x1, Pallas kernels, load(): pl.pallas_call(functools.partial(load_kernel, segments), out_shape=[pltpu...  3.53 us
    pallas_call x4, Pallas kernels, call(): pl.pallas_call(kernel, out_shape=out_shape, in_specs=in_specs or [VMEM_SP...  1.65 us
    squeeze x1, local copies, waits for them, and re-layouts, body(): lax.dynamic_index_in_dim(own, place ^ k ^ 1, 0, keepdims=False)  0.76 us
  transfers between devices with their start and end apart: 11, of which 5 were waited for; matrix products, arithmetic and copies ran while one was open for 2% of the time, Pallas kernels for 10%

profile of v4, /device:TPU:5, one launch (start us, length us, event | category | flops | bytes accessed | tf_op | source)
XLA Modules:
  0.0 36.9 jit_solution(9786472378803093802)
XLA Ops:
  0.0 0.7 %collective-permute-start = (bf16[4,8,640]{2,1,0:T(8,128)(2,1)}, bf16[4,8,640]{2,1,0:T(8,128)(2,1)S(1)}, u32[]{:S(2)}, u32[]{:S(2)}) collective-permute-start(bf16[4,8,640]{2,1,0:T(8,128)(2,1)} %bitcast.23), channel_id=1, source_target_pairs={{0,1},{1,0},{2,3},{3,2},{4,5},{5,4},{6,7},{7,6},{8,9},{9,8},{10,11... | collective-permute-start | bytes 122888 | tf_op jit(solution)/shard_map/ppermute | solution.py:249
  0.7 0.8 %dynamic-slice_bitcast_fusion.4 = (bf16[8,640]{1,0:T(8,128)(2,1)S(1)}, bf16[8,640]{1,0:T(8,128)(2,1)S(1)}, bf16[8,640]{1,0:T(8,128)(2,1)S(1)}, bf16[8,640]{1,0:T(8,128)(2,1)S(1)}) fusion(bf16[4,1,8,640]{3,2,1,0:T(8,128)(2,1)} %param.6, s32[]{:T(128)S(6)} %select_n.47, s32[]{:T(128)S(6)} %select_n.46, s32[]{:T(128)S(6)} %select_n.45, s32[]{:T(128)S(6)} %select_n.44), kind=kLoop, calls=%fused_computation.9 | loop fusion | bytes 81936 | tf_op jit(solution)/shard_map/jit(dynamic_index_in_dim)/squeeze | solution.py:250
  1.4 0.3 collective-permute-done
  1.8 3.6 %collective-permute-start.3 = (bf16[16,640]{1,0:T(8,128)(2,1)S(1)}, bf16[16,640]{1,0:T(8,128)(2,1)S(1)}, u32[]{:S(2)}, u32[]{:S(2)}) collective-permute-start(bf16[16,640]{1,0:T(8,128)(2,1)S(1)} %pad_maximum_fusion.3), channel_id=1, source_target_pairs={{0,7},{1,6},{2,5},{3,4},{4,3},{5,2},{6,1},{7,0},{8,15},{9,14},{10,... | collective-permute-start | bytes 61448 | tf_op jit(solution)/shard_map/ppermute | solution.py:258
  5.4 0.0 collective-permute-start.2
  5.4 0.5 %collective-permute-start.1 = (bf16[16,640]{1,0:T(8,128)(2,1)S(1)}, bf16[16,640]{1,0:T(8,128)(2,1)S(1)}, u32[]{:S(2)}, u32[]{:S(2)}) collective-permute-start(bf16[16,640]{1,0:T(8,128)(2,1)S(1)} %pad_maximum_fusion.1), channel_id=1, source_target_pairs={{0,3},{1,2},{2,1},{3,0},{4,7},{5,6},{6,5},{7,4},{8,11},{9,10},{10,... | collective-permute-start | bytes 61448 | tf_op jit(solution)/shard_map/ppermute | solution.py:258
  5.9 3.5 %shard_map.64 = (bf16[4,1024,1024]{2,1,0:T(8,128)(2,1)S(1)}, bf16[640,1024]{1,0:T(8,128)(2,1)S(1)}, bf16[1024,640]{1,0:T(8,128)(2,1)S(1)}, f32[1,1024]{1,0:T(1,128)S(1)}, f32[1,1024]{1,0:T(1,128)S(1)}) custom-call(bf16[16,640]{1,0:T(8,128)(2,1)S(1)} %pad_maximum_fusion.hint.refs_0_, bf16[4,1024,1024]{2,1,0:T(8,128)(2,1)} %bitcast.21, ...), custom_call_target="tpu_custom_call" | custom-call | bytes 16777216 | tf_op jit(solution)/shard_map/pallas_call | solution.py:107
  9.4 0.0 collective-permute-done.3.refs_3_
  9.5 0.0 collective-permute-done.2.refs_2_
  9.5 0.0 collective-permute-done.1.refs_1_
  9.5 0.3 collective-permute-start.4
  9.8 1.1 %collective-permute-done.4.latent = bf16[64,1024]{1,0:T(8,128)(2,1)S(1)} collective-permute-done((bf16[64,1024]{1,0:T(8,128)(2,1)S(1)}, bf16[64,1024]{1,0:T(8,128)(2,1)S(1)}, u32[]{:S(2)}, u32[]{:S(2)}) %collective-permute-start.4) | collective-permute-done | bytes 131104 | tf_op jit(solution)/shard_map/ppermute | solution.py:275
  10.9 8.3 %collective-permute-start.5 = (bf16[64,1024]{1,0:T(8,128)(2,1)S(1)}, bf16[64,1024]{1,0:T(8,128)(2,1)S(1)}, u32[]{:S(2)}, u32[]{:S(2)}) collective-permute-start(bf16[64,1024]{1,0:T(8,128)(2,1)S(1)} %shard_map.66), channel_id=1, source_target_pairs={{0,1},{1,0},{2,3},{3,2},{4,5},{5,4},{6,7},{7,6},{8,16},{9,17},{10,... | collective-permute-start | bytes 393224 | tf_op jit(solution)/shard_map/ppermute | solution.py:275
  19.2 3.3 %collective-permute-done.5.latent = bf16[64,1024]{1,0:T(8,128)(2,1)S(1)} collective-permute-done((bf16[64,1024]{1,0:T(8,128)(2,1)S(1)}, bf16[64,1024]{1,0:T(8,128)(2,1)S(1)}, u32[]{:S(2)}, u32[]{:S(2)}) %collective-permute-start.5) | collective-permute-done | bytes 131104 | tf_op jit(solution)/shard_map/ppermute | solution.py:275
  22.5 1.6 %shard_map.67 = bf16[64,1024]{1,0:T(8,128)(2,1)S(1)} custom-call(bf16[64,1024]{1,0:T(8,128)(2,1)S(1)} %collective-permute-done.5.latent, bf16[4,1024,1024]{2,1,0:T(8,128)(2,1)S(1)} %get-tuple-element.23.refs_5_.weights, f32[1,1024]{1,0:T(1,128)S(1)} %get-tuple-element.24.refs_7_.gain), custom_call_target="tpu_custom_call" | custom-call | tf_op jit(solution)/shard_map/pallas_call | solution.py:167
  24.1 0.1 collective-permute-start.6
  24.2 3.8 %collective-permute-done.6.latent = bf16[64,1024]{1,0:T(8,128)(2,1)S(1)} collective-permute-done((bf16[64,1024]{1,0:T(8,128)(2,1)S(1)}, bf16[64,1024]{1,0:T(8,128)(2,1)S(1)}, u32[]{:S(2)}, u32[]{:S(2)}) %collective-permute-start.6) | collective-permute-done | bytes 131104 | tf_op jit(solution)/shard_map/ppermute | solution.py:275
  28.0 2.3 %collective-permute-start.10 = (f32[8,640]{1,0:T(8,128)S(1)}, f32[8,640]{1,0:T(8,128)S(1)}, u32[]{:S(2)}, u32[]{:S(2)}) collective-permute-start(f32[8,640]{1,0:T(8,128)S(1)} %get-tuple-element.30), channel_id=1, source_target_pairs={{0,1},{1,0},{2,26},{3,27},{4,5},{5,4},{6,7},{7,6},{8,24},{9,25},{1... | collective-permute-start | bytes 61448 | tf_op jit(solution)/shard_map/ppermute | solution.py:287
  30.4 0.0 collective-permute-start.7
  30.4 2.2 %collective-permute-start.8 = (f32[8,640]{1,0:T(8,128)S(1)}, f32[8,640]{1,0:T(8,128)S(1)}, u32[]{:S(2)}, u32[]{:S(2)}) collective-permute-start(f32[8,640]{1,0:T(8,128)S(1)} %get-tuple-element.28), channel_id=1, source_target_pairs={{0,1},{1,0},{2,3},{3,2},{4,5},{5,4},{6,30},{7,31},{8,9},{9,8},{10,... | collective-permute-start | bytes 61448 | tf_op jit(solution)/shard_map/ppermute | solution.py:287
  32.6 0.0 collective-permute-start.9
  32.6 0.0 collective-permute-done.10
  32.6 3.7 %collective-permute-done.7 = f32[8,640]{1,0:T(8,128)S(1)} collective-permute-done((f32[8,640]{1,0:T(8,128)S(1)}, f32[8,640]{1,0:T(8,128)S(1)}, u32[]{:S(2)}, u32[]{:S(2)}) %collective-permute-start.7) | collective-permute-done | bytes 20512 | tf_op jit(solution)/shard_map/ppermute | solution.py:287
  36.3 0.0 collective-permute-done.8
  36.3 0.0 collective-permute-done.9
  36.3 0.6 %select_bitcast_fusion = f32[1,1,8,640]{3,2,1,0:T(8,128)} fusion(f32[8,640]{1,0:T(8,128)S(1)} %collective-permute-done.7, f32[8,640]{1,0:T(8,128)S(1)} %collective-permute-done.8, f32[8,640]{1,0:T(8,128)S(1)} %collective-permute-done.9, f32[8,640]{1,0:T(8,128)S(1)} %collective-permute-done.10, pred[]{:T(512)S(6)} %eq.11, pred[]{:T(512)S(6)} %eq.10, pred[]{:T(512)S(6)} %eq.9), kind=kLoop, calls=%fused_computation.4 | loop fusion | flops 15360 | bytes 102403 | tf_op jit(solution)/shard_map/broadcast_in_dim | solution.py:289
  (8 shorter events, 0.0 us)
Async XLA Ops:
  0.0 1.8 %collective-permute-start = (bf16[4,8,640]{2,1,0:T(8,128)(2,1)}, bf16[4,8,640]{2,1,0:T(8,128)(2,1)S(1)}, u32[]{:S(2)}, u32[]{:S(2)}) collective-permute-start(bf16[4,8,640]{2,1,0:T(8,128)(2,1)} %bitcast.23), channel_id=1, source_target_pairs={{0,1},{1,0},{2,3},{3,2},{4,5},{5,4},{6,7},{7,6},{8,9},{9,8},{10,11... | collective-permute-start | bytes 122888 | tf_op jit(solution)/shard_map/ppermute | solution.py:249
  1.8 7.7 %collective-permute-start.3 = (bf16[16,640]{1,0:T(8,128)(2,1)S(1)}, bf16[16,640]{1,0:T(8,128)(2,1)S(1)}, u32[]{:S(2)}, u32[]{:S(2)}) collective-permute-start(bf16[16,640]{1,0:T(8,128)(2,1)S(1)} %pad_maximum_fusion.3), channel_id=1, source_target_pairs={{0,7},{1,6},{2,5},{3,4},{4,3},{5,2},{6,1},{7,0},{8,15},{9,14},{10,... | collective-permute-start | bytes 61448 | tf_op jit(solution)/shard_map/ppermute | solution.py:258
  5.4 4.1 %collective-permute-start.2 = (bf16[16,640]{1,0:T(8,128)(2,1)S(1)}, bf16[16,640]{1,0:T(8,128)(2,1)S(1)}, u32[]{:S(2)}, u32[]{:S(2)}) collective-permute-start(bf16[16,640]{1,0:T(8,128)(2,1)S(1)} %pad_maximum_fusion.2), channel_id=1, source_target_pairs={{0,5},{1,4},{2,7},{3,6},{4,1},{5,0},{6,3},{7,2},{8,13},{9,12},{10,... | collective-permute-start | bytes 61448 | tf_op jit(solution)/shard_map/ppermute | solution.py:258
  5.4 4.1 %collective-permute-start.1 = (bf16[16,640]{1,0:T(8,128)(2,1)S(1)}, bf16[16,640]{1,0:T(8,128)(2,1)S(1)}, u32[]{:S(2)}, u32[]{:S(2)}) collective-permute-start(bf16[16,640]{1,0:T(8,128)(2,1)S(1)} %pad_maximum_fusion.1), channel_id=1, source_target_pairs={{0,3},{1,2},{2,1},{3,0},{4,7},{5,6},{6,5},{7,4},{8,11},{9,10},{10,... | collective-permute-start | bytes 61448 | tf_op jit(solution)/shard_map/ppermute | solution.py:258
  9.5 1.4 %collective-permute-start.4 = (bf16[64,1024]{1,0:T(8,128)(2,1)S(1)}, bf16[64,1024]{1,0:T(8,128)(2,1)S(1)}, u32[]{:S(2)}, u32[]{:S(2)}) collective-permute-start(bf16[64,1024]{1,0:T(8,128)(2,1)S(1)} %shard_map.65), channel_id=1, source_target_pairs={{0,8},{1,9},{2,10},{3,11},{4,12},{5,13},{6,14},{7,15},{8,0},{9,1},... | collective-permute-start | bytes 393224 | tf_op jit(solution)/shard_map/ppermute | solution.py:275
  10.9 11.5 %collective-permute-start.5 = (bf16[64,1024]{1,0:T(8,128)(2,1)S(1)}, bf16[64,1024]{1,0:T(8,128)(2,1)S(1)}, u32[]{:S(2)}, u32[]{:S(2)}) collective-permute-start(bf16[64,1024]{1,0:T(8,128)(2,1)S(1)} %shard_map.66), channel_id=1, source_target_pairs={{0,1},{1,0},{2,3},{3,2},{4,5},{5,4},{6,7},{7,6},{8,16},{9,17},{10,... | collective-permute-start | bytes 393224 | tf_op jit(solution)/shard_map/ppermute | solution.py:275
  24.1 3.9 %collective-permute-start.6 = (bf16[64,1024]{1,0:T(8,128)(2,1)S(1)}, bf16[64,1024]{1,0:T(8,128)(2,1)S(1)}, u32[]{:S(2)}, u32[]{:S(2)}) collective-permute-start(bf16[64,1024]{1,0:T(8,128)(2,1)S(1)} %shard_map.67), channel_id=1, source_target_pairs={{0,1},{1,0},{2,3},{3,2},{4,5},{5,4},{6,7},{7,6},{8,9},{9,8},{10,11... | collective-permute-start | bytes 393224 | tf_op jit(solution)/shard_map/ppermute | solution.py:275
  28.0 4.6 %collective-permute-start.10 = (f32[8,640]{1,0:T(8,128)S(1)}, f32[8,640]{1,0:T(8,128)S(1)}, u32[]{:S(2)}, u32[]{:S(2)}) collective-permute-start(f32[8,640]{1,0:T(8,128)S(1)} %get-tuple-element.30), channel_id=1, source_target_pairs={{0,1},{1,0},{2,26},{3,27},{4,5},{5,4},{6,7},{7,6},{8,24},{9,25},{1... | collective-permute-start | bytes 61448 | tf_op jit(solution)/shard_map/ppermute | solution.py:287
  30.4 5.9 %collective-permute-start.7 = (f32[8,640]{1,0:T(8,128)S(1)}, f32[8,640]{1,0:T(8,128)S(1)}, u32[]{:S(2)}, u32[]{:S(2)}) collective-permute-start(f32[8,640]{1,0:T(8,128)S(1)} %get-tuple-element.27), channel_id=1, source_target_pairs={{0,1},{1,0},{2,3},{3,2},{4,28},{5,29},{6,7},{7,6},{8,9},{9,8},{10,... | collective-permute-start | bytes 61448 | tf_op jit(solution)/shard_map/ppermute | solution.py:287
  30.4 5.9 %collective-permute-start.8 = (f32[8,640]{1,0:T(8,128)S(1)}, f32[8,640]{1,0:T(8,128)S(1)}, u32[]{:S(2)}, u32[]{:S(2)}) collective-permute-start(f32[8,640]{1,0:T(8,128)S(1)} %get-tuple-element.28), channel_id=1, source_target_pairs={{0,1},{1,0},{2,3},{3,2},{4,5},{5,4},{6,30},{7,31},{8,9},{9,8},{10,... | collective-permute-start | bytes 61448 | tf_op jit(solution)/shard_map/ppermute | solution.py:287
  32.6 3.7 %collective-permute-start.9 = (f32[8,640]{1,0:T(8,128)S(1)}, f32[8,640]{1,0:T(8,128)S(1)}, u32[]{:S(2)}, u32[]{:S(2)}) collective-permute-start(f32[8,640]{1,0:T(8,128)S(1)} %get-tuple-element.29), channel_id=1, source_target_pairs={{0,24},{1,25},{2,3},{3,2},{4,5},{5,4},{6,7},{7,6},{8,9},{9,8},{10,... | collective-permute-start | bytes 61448 | tf_op jit(solution)/shard_map/ppermute | solution.py:287

commit v5 on v4

--- a/solution.py
+++ b/solution.py
@@ -11,10 +11,9 @@
 SOFTCAP = 5.0
 EPSILON = 1e-06
 BOTH = ("segment", "lon")
-HOP_POWER = 1
-OUT_POWER = 1
 LOG2_E = 1.4426950408889634
 FULL_ROWS = 128
+EXCHANGE_FLOPS = 5 * 10**9
 EARLY = 2
 HBM_SPEC = pl.BlockSpec(memory_space=pltpu.HBM)
 VMEM_SPEC = pl.BlockSpec(memory_space=pltpu.VMEM)
@@ -73,9 +72,14 @@
     return (wide + matmul(attended, weights(3))).astype(jnp.bfloat16)
 
 
-def load_kernel(segments, hint, weights, encoder, decoder, gain, final_gain, *rest):
-    weights_out, encoder_out, decoder_out, gain_out, final_out, sems = rest
+def leads(group, segment):
+    return (lax.axis_index("segment") == segment) & (lax.rem(lax.axis_index("lon"), group) == 0)
+
+
+def load_kernel(segments, group, hint, weights, decoder, gain, final_gain, *rest):
+    weights_out, decoder_out, gain_out, final_out, sems = rest
     segment = lax.axis_index("segment")
+    leader = (lax.rem(lax.axis_index("lon"), group) == 0) | (segment == segments - 1)
 
     def move(pairs):
         copies = [
@@ -87,25 +91,18 @@
         for copy in copies:
             copy.wait()
 
-    early = [(weights.at[i], weights_out.at[i]) for i in range(EARLY)] + [(gain, gain_out)]
-    late = [(weights.at[i], weights_out.at[i]) for i in range(EARLY, 4)]
-
-    @pl.when(segment == 0)
-    def _():
-        move([(encoder, encoder_out)] + early)
-
-    @pl.when(segment > 0)
-    def _():
-        move(early + late)
-
-    @pl.when(segment == segments - 1)
+    @pl.when(leader & (segment > 0))
+    def _():
+        move([(weights.at[i], weights_out.at[i]) for i in range(4)] + [(gain, gain_out)])
+
+    @pl.when(leader & (segment == segments - 1))
     def _():
         move([(decoder, decoder_out), (final_gain, final_out)])
 
 
-def load(segments, hint, arrays):
+def load(segments, group, hint, arrays):
     return pl.pallas_call(
-        functools.partial(load_kernel, segments),
+        functools.partial(load_kernel, segments, group),
         out_shape=[pltpu.VMEM(value.shape, value.dtype) for value in arrays],
         in_specs=[pl.BlockSpec(memory_space=pl.ANY)] + [HBM_SPEC] * len(arrays),
         out_specs=[VMEM_SPEC] * len(arrays),
@@ -115,44 +112,63 @@
     )(hint, *[in_hbm(value) for value in arrays])
 
 
-def first_kernel(*refs):
-    pieces, (encoder, weights, all_weights, gain, out, fetched, sems) = refs[:-7], refs[-7:]
-
-    @pl.when(lax.axis_index("segment") == 0)
-    def _():
-        copies = [
-            pltpu.make_async_copy(all_weights.at[i], fetched.at[i - EARLY], sems.at[i - EARLY])
-            for i in range(EARLY, 4)
-        ]
-        for copy in copies:
-            copy.start()
-
-        def get(i):
-            if i < EARLY:
-                return weights[i]
-            copies[i - EARLY].wait()
-            return fetched[i - EARLY]
-
+def piece_kernel(group, table, *refs):
+    picked, other, outs = refs[: len(table)], refs[len(table)], refs[len(table) + 1 :]
+    place, member = lax.axis_index("lon") // group, lax.rem(lax.axis_index("lon"), group)
+    for row, mine, out in zip(table, picked, outs):
+        out[...] = jnp.concatenate([mine[...], other[place ^ sent_way(row, member) ^ 1]], axis=0)
+
+
+def sent_way(row, member):
+    way = row[1]
+    for c in range(1, len(row)):
+        way = jnp.where(member == c, row[c ^ 1], way)
+    return way
+
+
+def exchange_table(groups, group):
+    count = -(-(groups - 1) // group)
+    table = [[0] * group for _ in range(count)]
+    ways = list(range(1, groups))
+    for step in reversed(range(count)):
+        for c in range(group if step == 0 else min(group, len(ways) - step * group)):
+            if ways:
+                table[step][c] = ways.pop(0)
+    return table
+
+
+def first_kernel(group, *refs):
+    pieces, (encoder, weights, gain, out) = refs[:-4], refs[-4:]
+
+    @pl.when(leads(group, 0))
+    def _():
         patches = jnp.concatenate([piece[...] for piece in pieces], axis=0)
         latent = matmul(patches, encoder[...]).astype(jnp.bfloat16)
-        out[...] = layer(latent, get, gain[...])
-
-
-def middle_kernel(tick, latent, weights, gain, out):
+        out[...] = layer(latent, lambda i: weights[i], gain[...])
+
+
+def middle_kernel(tick, group, latent, weights, gain, out):
+    @pl.when(leads(group, tick))
+    def _():
+        out[...] = layer(latent[...], lambda i: weights[i], gain[...])
+
+
+def last_kernel(tick, group, rows, turns, *refs):
+    latents, (weights, gain, final_gain, decoder) = refs[:group], refs[group : group + 4]
+    outs, decoded = refs[group + 4 : -1], refs[-1]
+    member = lax.rem(lax.axis_index("lon"), group)
+
     @pl.when(lax.axis_index("segment") == tick)
     def _():
-        out[...] = layer(latent[...], lambda i: weights[i], gain[...])
-
-
-def last_kernel(tick, group, rows, latent, weights, gain, final_gain, decoder, *outs):
-    @pl.when(lax.axis_index("segment") == tick)
-    def _():
-        mixed = layer(latent[...], lambda i: weights[i], gain[...])
+        latent = latents[0][...]
+        for c in range(1, group):
+            latent = jnp.where(member == c, latents[c][...], latent)
+        mixed = layer(latent, lambda i: weights[i], gain[...])
         final = norm_rows(mixed.astype(jnp.float32), final_gain[...])
-        decoded = matmul(final, decoder[...])
-        for index, out in enumerate(outs):
-            start = (index * group + (index == 0)) * rows
-            out[...] = decoded[start : start + rows, :]
+        decoded[...] = matmul(final, decoder[...])
+        for block, out in enumerate(outs):
+            start = pl.multiple_of((block * group + (member ^ turns[block])) * rows, 8)
+            out[...] = decoded[pl.ds(start, rows), :]
 
 
 def in_hbm(value):
@@ -209,22 +225,33 @@
     return bin(one[0] ^ two[0]).count("1") + abs(one[1] - two[1])
 
 
-def full_pairs(edges, segments, groups, group, cross, power):
-    nodes = [(s, g) for s in range(segments) for g in range(groups)]
+def full_pairs(edges, segments, groups, group, extra={}):
+    devices = [(s, g, c) for s in range(segments) for g in range(groups) for c in range(group)]
+    edges = extra | edges
     targets = set(edges.values())
-    senders = [node for node in nodes if node not in edges]
-    takers = [node for node in nodes if node not in targets]
-    table = [
-        [apart(one, two) ** power + 0.01 if one != two else 0.0 for two in takers] for one in senders
-    ]
-    filled = {one: takers[column] for one, column in zip(senders, assign(table))}
-    pairs = []
-    for one in nodes:
-        two = edges.get(one) or filled[one]
-        flip = 1 if one == two or (cross and one in edges) else 0
-        for c in range(group):
-            pairs.append(((one[0] * groups + one[1]) * group + c, (two[0] * groups + two[1]) * group + (c ^ flip)))
-    return pairs
+    givers = [one for one in devices if one in targets and one not in edges]
+    takers = [one for one in devices if one in edges and one not in targets]
+    chosen = assign([[apart(one, two) + 0.0 for two in takers] for one in givers])
+    links = edges | {one: takers[column] for one, column in zip(givers, chosen)}
+    idle = [one for one in devices if one not in links]
+    for s, g, c in idle:
+        if (s, g, c ^ 1) in idle:
+            links[(s, g, c)] = (s, g, c ^ 1)
+    rest = [one for one in idle if one not in links]
+    while rest:
+        ring = rest[:2] if len(rest) != 3 else rest
+        rest = rest[len(ring) :]
+        for one, two in zip(ring, ring[1:] + ring[:1]):
+            links[one] = two
+    number = {one: index for index, one in enumerate(devices)}
+    return [(number[one], number[two]) for one, two in links.items()]
+
+
+def detour(tick, groups):
+    links = {}
+    for g in range(groups):
+        links |= {(tick, g, 0): (tick, g, 1), (tick, g, 1): (tick - 1, g, 1), (tick - 1, g, 1): (tick - 1, g, 0)}
+    return links
 
 
 def everywhere(segments, lons, mask):
@@ -236,55 +263,73 @@
     lons = lax.axis_size("lon")
     bands, band_rows, lon_local, patch_values = patches.shape
     assert band_rows == 1 and bands == segments and lons % bands == 0
-    assert lons & (lons - 1) == 0 and bands & (bands - 1) == 0 and 1 < bands < lons
+    assert lons & (lons - 1) == 0 and bands & (bands - 1) == 0 and 2 < bands < lons
     group = lons // bands
     columns = lons * lon_local
     width = encoder_weight.shape[1]
     out_values = decoder_weight.shape[1]
 
-    place = lax.axis_index("lon") // group
+    place, member = lax.axis_index("lon") // group, lax.axis_index("lon") % group
+    table = exchange_table(bands, group)
+    rows_sent = [[0] * group] + table
     own = patches[:, 0]
     step = 1
     while step < group:
         other = lax.ppermute(own, BOTH, everywhere(segments, lons, step))
-        picked = [lax.dynamic_index_in_dim(own, place ^ k ^ 1, 0, keepdims=False) for k in range(bands)]
+        picked = [
+            lax.dynamic_index_in_dim(own, place ^ sent_way(row, member) ^ 1, 0, keepdims=False) for row in rows_sent
+        ]
         picked = lax.optimization_barrier(picked) if step == 1 else picked
         own = jnp.concatenate([own, other], axis=1)
         step *= 2
-    pieces = []
-    for k in range(bands):
-        theirs = lax.dynamic_index_in_dim(other, place ^ k ^ 1, 0, keepdims=False)
-        piece = jnp.concatenate([picked[k], theirs], axis=0)
-        pieces.append(lax.ppermute(piece, BOTH, everywhere(segments, lons, k * group + 1)) if k else piece)
-
-    every = layer_weights[0]
-    loaded = load(segments, pieces[0], [every, encoder_weight, decoder_weight, layer_gains, final_gain[None]])
-    weights, encoder, decoder, gain, final_gain = [in_vmem(value) for value in loaded]
+    sent = pl.pallas_call(
+        functools.partial(piece_kernel, group, rows_sent),
+        out_shape=[jax.ShapeDtypeStruct((group * lon_local, patch_values), jnp.bfloat16)] * len(rows_sent),
+        in_specs=[VMEM_SPEC] * (len(rows_sent) + 1),
+        out_specs=[VMEM_SPEC] * len(rows_sent),
+        compiler_params=pltpu.CompilerParams(vmem_limit_bytes=2 * 1024 * 1024),
+        cost_estimate=pl.CostEstimate(flops=EXCHANGE_FLOPS, bytes_accessed=10**6, transcendentals=0),
+    )(*picked, other)
+    pieces = [sent[0]] + [None] * (bands - 1)
+    turns = [1] + [0] * (bands - 1)
+    for row, piece in zip(table, sent[1:]):
+        pairs = [
+            ((s * bands + g) * group + c, (s * bands + (g ^ row[c ^ 1])) * group + (c ^ 1))
+            for s in range(segments)
+            for g in range(bands)
+            for c in range(group)
+        ]
+        taken = lax.ppermute(piece, BOTH, pairs)
+        for c in range(group):
+            if row[c]:
+                pieces[row[c]] = lax.ppermute(taken, BOTH, everywhere(segments, lons, c)) if c else taken
+                turns[row[c]] = c
+    loaded = load(segments, group, pieces[0], [layer_weights[0], decoder_weight, layer_gains, final_gain[None]])
+    weights, decoder, gain, final_gain = [in_vmem(value) for value in loaded]
 
     latent_shape = jax.ShapeDtypeStruct((columns, width), jnp.bfloat16)
     part_shape = jax.ShapeDtypeStruct((lon_local, out_values), jnp.float32)
-    latent = call(
-        first_kernel,
-        latent_shape,
-        pieces + [encoder, weights, in_hbm(every), gain],
-        [VMEM_SPEC] * (bands + 2) + [HBM_SPEC, VMEM_SPEC],
-        [pltpu.VMEM((4 - EARLY, width, width), jnp.bfloat16), pltpu.SemaphoreType.DMA((4 - EARLY,))],
-    )
-    for tick in range(1, segments):
-        edges = {(tick - 1, g): (tick, g) for g in range(bands)}
-        latent = lax.ppermute(latent, BOTH, full_pairs(edges, segments, bands, group, False, HOP_POWER))
-        if tick < segments - 1:
-            latent = call(functools.partial(middle_kernel, tick), latent_shape, [latent, weights, gain])
+    first = [in_vmem(value) for value in (encoder_weight, layer_weights[0], layer_gains)]
+    latent = call(functools.partial(first_kernel, group), latent_shape, pieces + first)
+    for tick in range(1, segments - 1):
+        edges = {(tick - 1, g, 0): (tick, g, 0) for g in range(bands)}
+        latent = lax.ppermute(latent, BOTH, full_pairs(edges, segments, bands, group, detour(tick, bands)))
+        latent = call(functools.partial(middle_kernel, tick, group), latent_shape, [latent, weights, gain])
+    last = segments - 1
+    edges = {(last - 1, g, 0): (last, g, 0) for g in range(bands)}
+    latents = [lax.ppermute(latent, BOTH, full_pairs(edges, segments, bands, group, detour(last, bands)))]
+    latents += [lax.ppermute(latents[0], BOTH, everywhere(segments, lons, c)) for c in range(1, group)]
     parts = call(
-        functools.partial(last_kernel, segments - 1, group, lon_local),
+        functools.partial(last_kernel, last, group, lon_local, turns),
         [part_shape] * bands,
-        [latent, weights, gain, final_gain, decoder],
+        latents + [weights, gain, final_gain, decoder],
+        scratch=[pltpu.VMEM((columns, out_values), jnp.float32)],
     )
     segment_id = lax.axis_index("segment")
     answer = None
     for k, part in enumerate(parts):
-        edges = {(segments - 1, g): (g ^ 1, g ^ k) for g in range(bands)}
-        taken = lax.ppermute(part, BOTH, full_pairs(edges, segments, bands, group, True, OUT_POWER))
+        edges = {(last, g, c): (g ^ 1, g ^ k, c ^ 1) for g in range(bands) for c in range(group)}
+        taken = lax.ppermute(part, BOTH, full_pairs(edges, segments, bands, group))
         answer = taken if k == 0 else jnp.where(place ^ segment_id ^ 1 == k, taken, answer)
     return answer[None, None]
 

time: 37.2 us -> 35.4 us (0.952)
  Pallas kernels: 5.18 us -> 0.09 us
  starting transfers between devices: 18 us -> 21.2 us
    pallas_call x1 -> x2, Pallas kernels: 3.53 us -> 0.07 us  [the longest x1 0.05 us: load(): pl.pallas_call(functools.partial(load_kernel, segments, group), out_shape...]
    ppermute x10 -> x11, starting transfers between devices: 17.4 us -> 20.5 us  [the longest x3 10.9 us: body(): lax.ppermute(latent, BOTH, full_pairs(edges, segments, bands, group, deto...]
    pallas_call x4, Pallas kernels: 1.65 us -> 0.02 us  [call(): pl.pallas_call(kernel, out_shape=out_shape, in_specs=in_specs or [VMEM_SP...]
    ppermute x10 -> x11, waiting for transfers between devices: 11.9 us -> 12.1 us  [the longest x3 3.86 us: body(): lax.ppermute(latent, BOTH, full_pairs(edges, segments, bands, group, deto...]
    squeeze x2 -> x1, local copies, waits for them, and re-layouts: 0.76 us -> 0.74 us  [body(): lax.dynamic_index_in_dim(own, place ^ sent_way(row, member) ^ 1, 0, keepd...]
  transfers between devices with their start and end apart: 11 -> 12, of which waited for: 5 -> 8; matrix products, arithmetic and copies ran while one was open for 2% -> 2% of each run, Pallas kernels for 10% -> 0%
where the time goes in v5:
time: 35.4 us; the launch traced here: 35.1 us
  starting transfers between devices  21.2 us (60%)
  waiting for transfers between devices  12.4 us (35%)
  local copies, waits for them, and re-layouts  0.76 us (2%)
  other arithmetic  0.62 us (2%)
    ppermute x3, starting transfers between devices, body(): lax.ppermute(latent, BOTH, full_pairs(edges, segments, bands, group, deto...  10.9 us
    ppermute x4, starting transfers between devices, body(): taken = lax.ppermute(part, BOTH, full_pairs(edges, segments, bands, group))  5.07 us
    ppermute x3, waiting for transfers between devices, body(): lax.ppermute(latent, BOTH, full_pairs(edges, segments, bands, group, deto...  3.86 us
    ppermute x4, waiting for transfers between devices, body(): taken = lax.ppermute(part, BOTH, full_pairs(edges, segments, bands, group))  3.85 us
    ppermute x2, starting transfers between devices, body(): taken = lax.ppermute(piece, BOTH, pairs)  2.92 us
    ppermute x2, waiting for transfers between devices, body(): taken = lax.ppermute(piece, BOTH, pairs)  2.28 us
    ppermute x1, starting transfers between devices, body(): lax.ppermute(latents[0], BOTH, everywhere(segments, lons, c))  1.54 us
    ppermute x1, waiting for transfers between devices, body(): lax.ppermute(taken, BOTH, everywhere(segments, lons, c))  1.14 us
  transfers between devices with their start and end apart: 12, of which 8 were waited for; matrix products, arithmetic and copies ran while one was open for 2% of the time, Pallas kernels for 0%

profile of v5, /device:TPU:5, one launch (start us, length us, event | category | flops | bytes accessed | tf_op | source)
XLA Modules:
  0.0 35.1 jit_solution(6512584072305040446)
XLA Ops:
  0.0 0.7 %collective-permute-start = (bf16[4,8,640]{2,1,0:T(8,128)(2,1)}, bf16[4,8,640]{2,1,0:T(8,128)(2,1)S(1)}, u32[]{:S(2)}, u32[]{:S(2)}) collective-permute-start(bf16[4,8,640]{2,1,0:T(8,128)(2,1)} %bitcast.15), channel_id=1, source_target_pairs={{0,1},{1,0},{2,3},{3,2},{4,5},{5,4},{6,7},{7,6},{8,9},{9,8},{10,11... | collective-permute-start | bytes 122888 | tf_op jit(solution)/shard_map/ppermute | solution.py:278
  0.7 0.7 %dynamic-slice_bitcast_fusion = (bf16[8,640]{1,0:T(8,128)(2,1)S(1)}, bf16[8,640]{1,0:T(8,128)(2,1)S(1)}, bf16[8,640]{1,0:T(8,128)(2,1)S(1)}) fusion(bf16[4,1,8,640]{3,2,1,0:T(8,128)(2,1)} %param.6, s32[]{:T(128)S(6)} %select_n.56, s32[]{:T(128)S(6)} %select_n.54, s32[]{:T(128)S(6)} %select_n.51), kind=kLoop, calls=%fused_computation.1 | loop fusion | bytes 61452 | tf_op jit(solution)/shard_map/jit(dynamic_index_in_dim)/squeeze | solution.py:280
  1.4 0.0 copy-start.1
  1.4 0.3 collective-permute-done.refs_3_
  1.8 2.6 %collective-permute-start.2 = (bf16[16,640]{1,0:T(8,128)(2,1)S(1)}, bf16[16,640]{1,0:T(8,128)(2,1)S(1)}, u32[]{:S(2)}, u32[]{:S(2)}) collective-permute-start(bf16[16,640]{1,0:T(8,128)(2,1)S(1)} %get-tuple-element.24), channel_id=1, source_target_pairs={{0,7},{1,4},{2,5},{3,6},{4,3},{5,0},{6,1},{7,2},{8,15},{9,12},{10,... | collective-permute-start | bytes 61448 | tf_op jit(solution)/shard_map/ppermute | solution.py:302
  4.4 0.3 collective-permute-start.1
  4.7 2.3 %collective-permute-done.2.refs_2_ = bf16[16,640]{1,0:T(8,128)(2,1)S(1)} collective-permute-done((bf16[16,640]{1,0:T(8,128)(2,1)S(1)}, bf16[16,640]{1,0:T(8,128)(2,1)S(1)}, u32[]{:S(2)}, u32[]{:S(2)}) %collective-permute-start.2) | collective-permute-done | bytes 20512 | tf_op jit(solution)/shard_map/ppermute | solution.py:302
  7.0 0.0 collective-permute-start.3
  7.0 0.0 collective-permute-done.1.refs_1_
  7.0 1.1 %collective-permute-done.3.refs_3_ = bf16[16,640]{1,0:T(8,128)(2,1)S(1)} collective-permute-done((bf16[16,640]{1,0:T(8,128)(2,1)S(1)}, bf16[16,640]{1,0:T(8,128)(2,1)S(1)}, u32[]{:S(2)}, u32[]{:S(2)}) %collective-permute-start.3) | collective-permute-done | bytes 20512 | tf_op jit(solution)/shard_map/ppermute | solution.py:305
  8.2 0.0 slice-done
  8.2 0.0 slice-done.1
  8.2 0.0 copy-done
  8.2 0.0 copy-done.1
  8.2 0.6 %collective-permute-start.4 = (bf16[64,1024]{1,0:T(8,128)(2,1)S(1)}, bf16[64,1024]{1,0:T(8,128)(2,1)S(1)}, u32[]{:S(2)}, u32[]{:S(2)}) collective-permute-start(bf16[64,1024]{1,0:T(8,128)(2,1)S(1)} %shard_map.65), channel_id=1, source_target_pairs={{8,9},{9,1},{1,0},{10,11},{11,3},{3,2},{12,13},{13,5},{5,4},{14,15... | collective-permute-start | bytes 393224 | tf_op jit(solution)/shard_map/ppermute | solution.py:316
  8.9 0.1 shard_map.66
  8.9 0.9 %collective-permute-done.4.latent = bf16[64,1024]{1,0:T(8,128)(2,1)S(1)} collective-permute-done((bf16[64,1024]{1,0:T(8,128)(2,1)S(1)}, bf16[64,1024]{1,0:T(8,128)(2,1)S(1)}, u32[]{:S(2)}, u32[]{:S(2)}) %collective-permute-start.4) | collective-permute-done | bytes 131104 | tf_op jit(solution)/shard_map/ppermute | solution.py:316
  9.9 1.8 %collective-permute-start.5 = (bf16[64,1024]{1,0:T(8,128)(2,1)S(1)}, bf16[64,1024]{1,0:T(8,128)(2,1)S(1)}, u32[]{:S(2)}, u32[]{:S(2)}) collective-permute-start(bf16[64,1024]{1,0:T(8,128)(2,1)S(1)} %shard_map.67), channel_id=1, source_target_pairs={{16,17},{17,9},{9,8},{18,19},{19,11},{11,10},{20,21},{21,13},{13,1... | collective-permute-start | bytes 393224 | tf_op jit(solution)/shard_map/ppermute | solution.py:316
  11.6 1.9 %collective-permute-done.5.latent = bf16[64,1024]{1,0:T(8,128)(2,1)S(1)} collective-permute-done((bf16[64,1024]{1,0:T(8,128)(2,1)S(1)}, bf16[64,1024]{1,0:T(8,128)(2,1)S(1)}, u32[]{:S(2)}, u32[]{:S(2)}) %collective-permute-start.5) | collective-permute-done | bytes 131104 | tf_op jit(solution)/shard_map/ppermute | solution.py:316
  13.6 8.5 %collective-permute-start.6 = (bf16[64,1024]{1,0:T(8,128)(2,1)S(1)}, bf16[64,1024]{1,0:T(8,128)(2,1)S(1)}, u32[]{:S(2)}, u32[]{:S(2)}) collective-permute-start(bf16[64,1024]{1,0:T(8,128)(2,1)S(1)} %shard_map.68), channel_id=1, source_target_pairs={{24,25},{25,17},{17,16},{26,27},{27,19},{19,18},{28,29},{29,21},{2... | collective-permute-start | bytes 393224 | tf_op jit(solution)/shard_map/ppermute | solution.py:320
  22.1 1.0 %collective-permute-done.6.refs_0_ = bf16[64,1024]{1,0:T(8,128)(2,1)S(1)} collective-permute-done((bf16[64,1024]{1,0:T(8,128)(2,1)S(1)}, bf16[64,1024]{1,0:T(8,128)(2,1)S(1)}, u32[]{:S(2)}, u32[]{:S(2)}) %collective-permute-start.6) | collective-permute-done | bytes 131104 | tf_op jit(solution)/shard_map/ppermute | solution.py:320
  23.1 1.5 %collective-permute-start.7 = (bf16[64,1024]{1,0:T(8,128)(2,1)S(1)}, bf16[64,1024]{1,0:T(8,128)(2,1)S(1)}, u32[]{:S(2)}, u32[]{:S(2)}) collective-permute-start(bf16[64,1024]{1,0:T(8,128)(2,1)S(1)} %collective-permute-done.6.refs_0_), channel_id=1, source_target_pairs={{0,1},{1,0},{2,3},{3,2},{4,5},{5,4},{6,7},{7,6},{8,9},{9,8},{10,11... | collective-permute-start | bytes 393224 | tf_op jit(solution)/shard_map/ppermute | solution.py:321
  24.6 1.0 %collective-permute-done.7.refs_1_ = bf16[64,1024]{1,0:T(8,128)(2,1)S(1)} collective-permute-done((bf16[64,1024]{1,0:T(8,128)(2,1)S(1)}, bf16[64,1024]{1,0:T(8,128)(2,1)S(1)}, u32[]{:S(2)}, u32[]{:S(2)}) %collective-permute-start.7) | collective-permute-done | bytes 131104 | tf_op jit(solution)/shard_map/ppermute | solution.py:321
  25.6 0.4 %collective-permute-start.10 = (f32[8,640]{1,0:T(8,128)S(1)}, f32[8,640]{1,0:T(8,128)S(1)}, u32[]{:S(2)}, u32[]{:S(2)}) collective-permute-start(f32[8,640]{1,0:T(8,128)S(1)} %get-tuple-element.31), channel_id=1, source_target_pairs={{24,11},{25,10},{26,1},{27,0},{28,31},{29,30},{30,21},{31,20},{0,2... | collective-permute-start | bytes 61448 | tf_op jit(solution)/shard_map/ppermute | solution.py:332
  26.0 0.1 collective-permute-start.11
  26.1 3.9 %collective-permute-start.8 = (f32[8,640]{1,0:T(8,128)S(1)}, f32[8,640]{1,0:T(8,128)S(1)}, u32[]{:S(2)}, u32[]{:S(2)}) collective-permute-start(f32[8,640]{1,0:T(8,128)S(1)} %get-tuple-element.29), channel_id=1, source_target_pairs={{24,15},{25,14},{26,5},{27,4},{28,27},{29,26},{30,17},{31,16},{4,2... | collective-permute-start | bytes 61448 | tf_op jit(solution)/shard_map/ppermute | solution.py:332
  30.0 0.6 %collective-permute-start.9 = (f32[8,640]{1,0:T(8,128)S(1)}, f32[8,640]{1,0:T(8,128)S(1)}, u32[]{:S(2)}, u32[]{:S(2)}) collective-permute-start(f32[8,640]{1,0:T(8,128)S(1)} %get-tuple-element.30), channel_id=1, source_target_pairs={{24,13},{25,12},{26,7},{27,6},{28,25},{29,24},{30,19},{31,18},{6,3... | collective-permute-start | bytes 61448 | tf_op jit(solution)/shard_map/ppermute | solution.py:332
  30.7 0.0 collective-permute-done.10
  30.7 0.0 collective-permute-done.11
  30.7 3.8 %collective-permute-done.8 = f32[8,640]{1,0:T(8,128)S(1)} collective-permute-done((f32[8,640]{1,0:T(8,128)S(1)}, f32[8,640]{1,0:T(8,128)S(1)}, u32[]{:S(2)}, u32[]{:S(2)}) %collective-permute-start.8) | collective-permute-done | bytes 20512 | tf_op jit(solution)/shard_map/ppermute | solution.py:332
  34.5 0.0 collective-permute-done.9
  34.5 0.6 %select_bitcast_fusion = f32[1,1,8,640]{3,2,1,0:T(8,128)} fusion(f32[8,640]{1,0:T(8,128)S(1)} %collective-permute-done.8, f32[8,640]{1,0:T(8,128)S(1)} %collective-permute-done.9, f32[8,640]{1,0:T(8,128)S(1)} %collective-permute-done.10, f32[8,640]{1,0:T(8,128)S(1)} %collective-permute-done.11, pred[]{:T(512)S(6)} %eq.19, pred[]{:T(512)S(6)} %eq.18, pred[]{:T(512)S(6)} %eq.16), kind=kLoop, calls=%fused_computation | loop fusion | flops 15360 | bytes 102403 | tf_op jit(solution)/shard_map/broadcast_in_dim | solution.py:334
  (9 shorter events, 0.0 us)
Async XLA Ops:
  0.0 1.8 %collective-permute-start = (bf16[4,8,640]{2,1,0:T(8,128)(2,1)}, bf16[4,8,640]{2,1,0:T(8,128)(2,1)S(1)}, u32[]{:S(2)}, u32[]{:S(2)}) collective-permute-start(bf16[4,8,640]{2,1,0:T(8,128)(2,1)} %bitcast.15), channel_id=1, source_target_pairs={{0,1},{1,0},{2,3},{3,2},{4,5},{5,4},{6,7},{7,6},{8,9},{9,8},{10,11... | collective-permute-start | bytes 122888 | tf_op jit(solution)/shard_map/ppermute | solution.py:278
  1.4 6.8 %slice-start = ((s8[8388608]{0:T(1024)(128)(4,1)}), s8[4194304]{0:T(1024)(128)(4,1)S(1)}, s32[]{:S(2)}) async-start(s8[8388608]{0:T(1024)(128)(4,1)} %bitcast.12), calls=%async_computation | async-start | bytes 8388608
  1.4 6.8 %slice-start.1 = ((s8[8388608]{0:T(1024)(128)(4,1)}), s8[4194304]{0:T(1024)(128)(4,1)S(1)}, s32[]{:S(2)}) async-start(s8[8388608]{0:T(1024)(128)(4,1)} %bitcast.12), calls=%async_computation.1 | async-start | bytes 8388608
  1.4 6.8 %copy-start = (bf16[640,1024]{1,0:T(8,128)(2,1)S(1)}, bf16[640,1024]{1,0:T(8,128)(2,1)}, u32[]{:S(2)}) copy-start(bf16[640,1024]{1,0:T(8,128)(2,1)} %refs_4_.1) | copy-start | bytes 3932164
  1.4 6.8 %copy-start.1 = (f32[1,1024]{1,0:T(1,128)S(1)}, f32[1,1024]{1,0:T(1,128)}, u32[]{:S(2)}) copy-start(f32[1,1024]{1,0:T(1,128)} %gain.1) | copy-start | bytes 12292
  1.8 5.2 %collective-permute-start.2 = (bf16[16,640]{1,0:T(8,128)(2,1)S(1)}, bf16[16,640]{1,0:T(8,128)(2,1)S(1)}, u32[]{:S(2)}, u32[]{:S(2)}) collective-permute-start(bf16[16,640]{1,0:T(8,128)(2,1)S(1)} %get-tuple-element.24), channel_id=1, source_target_pairs={{0,7},{1,4},{2,5},{3,6},{4,3},{5,0},{6,1},{7,2},{8,15},{9,12},{10,... | collective-permute-start | bytes 61448 | tf_op jit(solution)/shard_map/ppermute | solution.py:302
  4.4 2.7 %collective-permute-start.1 = (bf16[16,640]{1,0:T(8,128)(2,1)S(1)}, bf16[16,640]{1,0:T(8,128)(2,1)S(1)}, u32[]{:S(2)}, u32[]{:S(2)}) collective-permute-start(bf16[16,640]{1,0:T(8,128)(2,1)S(1)} %get-tuple-element.23), channel_id=1, source_target_pairs={{0,1},{1,2},{2,3},{3,0},{4,5},{5,6},{6,7},{7,4},{8,9},{9,10},{10,1... | collective-permute-start | bytes 61448 | tf_op jit(solution)/shard_map/ppermute | solution.py:302
  7.0 1.2 %collective-permute-start.3 = (bf16[16,640]{1,0:T(8,128)(2,1)S(1)}, bf16[16,640]{1,0:T(8,128)(2,1)S(1)}, u32[]{:S(2)}, u32[]{:S(2)}) collective-permute-start(bf16[16,640]{1,0:T(8,128)(2,1)S(1)} %collective-permute-done.2.refs_2_), channel_id=1, source_target_pairs={{0,1},{1,0},{2,3},{3,2},{4,5},{5,4},{6,7},{7,6},{8,9},{9,8},{10,11... | collective-permute-start | bytes 61448 | tf_op jit(solution)/shard_map/ppermute | solution.py:305
  8.2 1.6 %collective-permute-start.4 = (bf16[64,1024]{1,0:T(8,128)(2,1)S(1)}, bf16[64,1024]{1,0:T(8,128)(2,1)S(1)}, u32[]{:S(2)}, u32[]{:S(2)}) collective-permute-start(bf16[64,1024]{1,0:T(8,128)(2,1)S(1)} %shard_map.65), channel_id=1, source_target_pairs={{8,9},{9,1},{1,0},{10,11},{11,3},{3,2},{12,13},{13,5},{5,4},{14,15... | collective-permute-start | bytes 393224 | tf_op jit(solution)/shard_map/ppermute | solution.py:316
  9.9 3.7 %collective-permute-start.5 = (bf16[64,1024]{1,0:T(8,128)(2,1)S(1)}, bf16[64,1024]{1,0:T(8,128)(2,1)S(1)}, u32[]{:S(2)}, u32[]{:S(2)}) collective-permute-start(bf16[64,1024]{1,0:T(8,128)(2,1)S(1)} %shard_map.67), channel_id=1, source_target_pairs={{16,17},{17,9},{9,8},{18,19},{19,11},{11,10},{20,21},{21,13},{13,1... | collective-permute-start | bytes 393224 | tf_op jit(solution)/shard_map/ppermute | solution.py:316
  13.6 9.5 %collective-permute-start.6 = (bf16[64,1024]{1,0:T(8,128)(2,1)S(1)}, bf16[64,1024]{1,0:T(8,128)(2,1)S(1)}, u32[]{:S(2)}, u32[]{:S(2)}) collective-permute-start(bf16[64,1024]{1,0:T(8,128)(2,1)S(1)} %shard_map.68), channel_id=1, source_target_pairs={{24,25},{25,17},{17,16},{26,27},{27,19},{19,18},{28,29},{29,21},{2... | collective-permute-start | bytes 393224 | tf_op jit(solution)/shard_map/ppermute | solution.py:320
  23.1 2.5 %collective-permute-start.7 = (bf16[64,1024]{1,0:T(8,128)(2,1)S(1)}, bf16[64,1024]{1,0:T(8,128)(2,1)S(1)}, u32[]{:S(2)}, u32[]{:S(2)}) collective-permute-start(bf16[64,1024]{1,0:T(8,128)(2,1)S(1)} %collective-permute-done.6.refs_0_), channel_id=1, source_target_pairs={{0,1},{1,0},{2,3},{3,2},{4,5},{5,4},{6,7},{7,6},{8,9},{9,8},{10,11... | collective-permute-start | bytes 393224 | tf_op jit(solution)/shard_map/ppermute | solution.py:321
  25.6 5.1 %collective-permute-start.10 = (f32[8,640]{1,0:T(8,128)S(1)}, f32[8,640]{1,0:T(8,128)S(1)}, u32[]{:S(2)}, u32[]{:S(2)}) collective-permute-start(f32[8,640]{1,0:T(8,128)S(1)} %get-tuple-element.31), channel_id=1, source_target_pairs={{24,11},{25,10},{26,1},{27,0},{28,31},{29,30},{30,21},{31,20},{0,2... | collective-permute-start | bytes 61448 | tf_op jit(solution)/shard_map/ppermute | solution.py:332
  26.0 4.7 %collective-permute-start.11 = (f32[8,640]{1,0:T(8,128)S(1)}, f32[8,640]{1,0:T(8,128)S(1)}, u32[]{:S(2)}, u32[]{:S(2)}) collective-permute-start(f32[8,640]{1,0:T(8,128)S(1)} %get-tuple-element.32), channel_id=1, source_target_pairs={{24,9},{25,8},{26,3},{27,2},{28,29},{29,28},{30,23},{31,22},{2,26}... | collective-permute-start | bytes 61448 | tf_op jit(solution)/shard_map/ppermute | solution.py:332
  26.1 8.4 %collective-permute-start.8 = (f32[8,640]{1,0:T(8,128)S(1)}, f32[8,640]{1,0:T(8,128)S(1)}, u32[]{:S(2)}, u32[]{:S(2)}) collective-permute-start(f32[8,640]{1,0:T(8,128)S(1)} %get-tuple-element.29), channel_id=1, source_target_pairs={{24,15},{25,14},{26,5},{27,4},{28,27},{29,26},{30,17},{31,16},{4,2... | collective-permute-start | bytes 61448 | tf_op jit(solution)/shard_map/ppermute | solution.py:332
  30.0 4.5 %collective-permute-start.9 = (f32[8,640]{1,0:T(8,128)S(1)}, f32[8,640]{1,0:T(8,128)S(1)}, u32[]{:S(2)}, u32[]{:S(2)}) collective-permute-start(f32[8,640]{1,0:T(8,128)S(1)} %get-tuple-element.30), channel_id=1, source_target_pairs={{24,13},{25,12},{26,7},{27,6},{28,25},{29,24},{30,19},{31,18},{6,3... | collective-permute-start | bytes 61448 | tf_op jit(solution)/shard_map/ppermute | solution.py:332

commit v6 on v5

--- a/solution.py
+++ b/solution.py
@@ -79,7 +79,7 @@
 def load_kernel(segments, group, hint, weights, decoder, gain, final_gain, *rest):
     weights_out, decoder_out, gain_out, final_out, sems = rest
     segment = lax.axis_index("segment")
-    leader = (lax.rem(lax.axis_index("lon"), group) == 0) | (segment == segments - 1)
+    leader = lax.rem(lax.axis_index("lon"), group) == 0
 
     def move(pairs):
         copies = [
@@ -127,14 +127,9 @@
 
 
 def exchange_table(groups, group):
-    count = -(-(groups - 1) // group)
-    table = [[0] * group for _ in range(count)]
-    ways = list(range(1, groups))
-    for step in reversed(range(count)):
-        for c in range(group if step == 0 else min(group, len(ways) - step * group)):
-            if ways:
-                table[step][c] = ways.pop(0)
-    return table
+    ways = [2, 1, *range(3, groups)]
+    ways += [0] * (-len(ways) % group)
+    return [ways[start : start + group] for start in range(0, len(ways), group)]
 
 
 def first_kernel(group, *refs):
@@ -153,22 +148,16 @@
         out[...] = layer(latent[...], lambda i: weights[i], gain[...])
 
 
-def last_kernel(tick, group, rows, turns, *refs):
-    latents, (weights, gain, final_gain, decoder) = refs[:group], refs[group : group + 4]
-    outs, decoded = refs[group + 4 : -1], refs[-1]
-    member = lax.rem(lax.axis_index("lon"), group)
-
-    @pl.when(lax.axis_index("segment") == tick)
-    def _():
-        latent = latents[0][...]
-        for c in range(1, group):
-            latent = jnp.where(member == c, latents[c][...], latent)
-        mixed = layer(latent, lambda i: weights[i], gain[...])
+def last_kernel(tick, group, rows, turns, latent, weights, gain, final_gain, decoder, *outs):
+    @pl.when(leads(group, tick))
+    def _():
+        mixed = layer(latent[...], lambda i: weights[i], gain[...])
         final = norm_rows(mixed.astype(jnp.float32), final_gain[...])
-        decoded[...] = matmul(final, decoder[...])
+        decoded = matmul(final, decoder[...])
         for block, out in enumerate(outs):
-            start = pl.multiple_of((block * group + (member ^ turns[block])) * rows, 8)
-            out[...] = decoded[pl.ds(start, rows), :]
+            turn = turns[block] ^ 1 if block else 0
+            starts = [(block * group + (c ^ turn)) * rows for c in range(group)]
+            out[...] = jnp.concatenate([decoded[start : start + rows] for start in starts], axis=0).astype(out.dtype)
 
 
 def in_hbm(value):
@@ -252,6 +241,55 @@
     for g in range(groups):
         links |= {(tick, g, 0): (tick, g, 1), (tick, g, 1): (tick - 1, g, 1), (tick - 1, g, 1): (tick - 1, g, 0)}
     return links
+
+
+def ring_up(devices, links):
+    alone = []
+    for one in devices:
+        mate = (one[0], one[1], one[2] ^ 1)
+        if mate in devices:
+            links[one] = mate
+        else:
+            alone.append(one)
+    while len(alone) > 1:
+        one, two = min(
+            ((one, two) for index, one in enumerate(alone) for two in alone[index + 1 :]), key=lambda pair: apart(*pair)
+        )
+        links[one], links[two] = two, one
+        alone = [three for three in alone if three not in (one, two)]
+    for one in alone:
+        two = min((two for two in devices if two != one and two[2] == 1), key=lambda two: apart(one, two))
+        after = links[two]
+        links[one], links[two], links[after] = two, after, one
+
+
+def fan_pairs(k, segments, groups, group, late):
+    last = segments - 1
+    devices = [(s, g, c) for s in range(segments) for g in range(groups) for c in range(group)]
+    links = {(last, g, 0): (g ^ 1, g ^ k, 1) for g in range(groups)}
+    taken = list(links.values())
+    outside = [one for one in taken if one[0] != last]
+    inside = [one for one in taken if one[0] == last]
+    for s, g, c in inside:
+        links[(s, g, 1)] = (s, g, 0)
+    for s, g, c in outside:
+        links[(s, g, 1)] = (s, g, 0)
+    givers = [(s, g, 0) for s, g, c in outside]
+    takers = [(last, g, 0) for g in range(groups) if (last, g, 1) not in inside]
+    waiting = [one for one in late if one[0] == last and one not in links]
+    if len(waiting) % 2 and len(waiting) < groups - 1:
+        one = waiting[0]
+        links[one] = (last, one[1], 0)
+        takers[takers.index(links[one])] = one
+    for one, column in zip(givers, assign([[apart(one, two) + 0.0 for two in takers] for one in givers])):
+        links[one] = takers[column]
+    idle = [one for one in devices if one not in links]
+    ring_up([one for one in idle if one not in late], links)
+    ring_up([one for one in idle if one in late], links)
+    late |= {(s, g, c) for s, g, _ in taken for c in range(2)} - {(last, g, 0) for g in range(groups)}
+    number = {one: index for index, one in enumerate(devices)}
+    assert len(set(links.values())) == len(links) == len(devices)
+    return [(number[one], number[two]) for one, two in links.items()]
 
 
 def everywhere(segments, lons, mask):
@@ -308,7 +346,7 @@
     weights, decoder, gain, final_gain = [in_vmem(value) for value in loaded]
 
     latent_shape = jax.ShapeDtypeStruct((columns, width), jnp.bfloat16)
-    part_shape = jax.ShapeDtypeStruct((lon_local, out_values), jnp.float32)
+    part_shape = jax.ShapeDtypeStruct((group * lon_local, out_values), jnp.bfloat16)
     first = [in_vmem(value) for value in (encoder_weight, layer_weights[0], layer_gains)]
     latent = call(functools.partial(first_kernel, group), latent_shape, pieces + first)
     for tick in range(1, segments - 1):
@@ -317,21 +355,24 @@
         latent = call(functools.partial(middle_kernel, tick, group), latent_shape, [latent, weights, gain])
     last = segments - 1
     edges = {(last - 1, g, 0): (last, g, 0) for g in range(bands)}
-    latents = [lax.ppermute(latent, BOTH, full_pairs(edges, segments, bands, group, detour(last, bands)))]
-    latents += [lax.ppermute(latents[0], BOTH, everywhere(segments, lons, c)) for c in range(1, group)]
+    latent = lax.ppermute(latent, BOTH, full_pairs(edges, segments, bands, group, detour(last, bands)))
     parts = call(
         functools.partial(last_kernel, last, group, lon_local, turns),
         [part_shape] * bands,
-        latents + [weights, gain, final_gain, decoder],
-        scratch=[pltpu.VMEM((columns, out_values), jnp.float32)],
+        [latent, weights, gain, final_gain, decoder],
     )
     segment_id = lax.axis_index("segment")
-    answer = None
-    for k, part in enumerate(parts):
-        edges = {(last, g, c): (g ^ 1, g ^ k, c ^ 1) for g in range(bands) for c in range(group)}
-        taken = lax.ppermute(part, BOTH, full_pairs(edges, segments, bands, group))
-        answer = taken if k == 0 else jnp.where(place ^ segment_id ^ 1 == k, taken, answer)
-    return answer[None, None]
+    late, picked = set(), None
+    ways = {k: fan_pairs(k, segments, bands, group, late) for k in range(bands - 1, -1, -1)}
+    for k in (bands - 1, *range(bands - 1)):
+        taken = lax.ppermute(parts[k], BOTH, ways[k])
+        picked = taken if picked is None else jnp.where(place ^ segment_id ^ 1 == k, taken, picked)
+    rows = [picked[c * lon_local : (c + 1) * lon_local] for c in range(group)]
+    answer = rows[1]
+    for e in range(1, group):
+        handed = lax.ppermute(rows[1 ^ e], BOTH, everywhere(segments, lons, e))
+        answer = jnp.where(member == 1 ^ e, handed, answer)
+    return answer.astype(jnp.float32)[None, None]
 
 
 def solution(mesh):

time: 35.4 us -> 34.4 us (0.972)
  waiting for transfers between devices: 12.4 us -> 9.35 us
  starting transfers between devices: 21.2 us -> 23 us
    ppermute x2, waiting for transfers between devices: 2.28 us -> 0.23 us  [body(): taken = lax.ppermute(piece, BOTH, pairs)]
    ppermute x5, waiting for transfers between devices: 4.83 us -> 3.78 us  [the longest x4 2.62 us: body(): taken = lax.ppermute(parts[k], BOTH, ways[k])]
    ppermute x2, starting transfers between devices: 2.92 us -> 3.82 us  [body(): taken = lax.ppermute(piece, BOTH, pairs)]
    ppermute x1, starting transfers between devices: 0.04 us -> 0.68 us  [body(): lax.ppermute(taken, BOTH, everywhere(segments, lons, c))]
    ppermute x3, waiting for transfers between devices: 3.86 us -> 4.41 us  [body(): lax.ppermute(latent, BOTH, full_pairs(edges, segments, bands, group, deto...]
    ppermute x1, waiting for transfers between devices: 1.14 us -> 0.62 us  [body(): lax.ppermute(taken, BOTH, everywhere(segments, lons, c))]
where the time goes in v6:
time: 34.4 us; the launch traced here: 34 us
  starting transfers between devices  23 us (67%)
  waiting for transfers between devices  9.35 us (27%)
  local copies, waits for them, and re-layouts  0.76 us (2%)
  other arithmetic  0.63 us (2%)
    ppermute x3, starting transfers between devices, body(): lax.ppermute(latent, BOTH, full_pairs(edges, segments, bands, group, deto...  11.2 us
    ppermute x4, starting transfers between devices, body(): taken = lax.ppermute(parts[k], BOTH, ways[k])  6.6 us
    ppermute x3, waiting for transfers between devices, body(): lax.ppermute(latent, BOTH, full_pairs(edges, segments, bands, group, deto...  4.41 us
    ppermute x2, starting transfers between devices, body(): taken = lax.ppermute(piece, BOTH, pairs)  3.82 us
    ppermute x4, waiting for transfers between devices, body(): taken = lax.ppermute(parts[k], BOTH, ways[k])  2.62 us
    ppermute x1, waiting for transfers between devices, body(): handed = lax.ppermute(rows[1 ^ e], BOTH, everywhere(segments, lons, e))  1.16 us
    squeeze x1, local copies, waits for them, and re-layouts, body(): lax.dynamic_index_in_dim(own, place ^ sent_way(row, member) ^ 1, 0, keepd...  0.74 us
  transfers between devices with their start and end apart: 12, of which 8 were waited for; matrix products, arithmetic and copies ran while one was open for 2% of the time, Pallas kernels for 0%

profile of v6, /device:TPU:5, one launch (start us, length us, event | category | flops | bytes accessed | tf_op | source)
XLA Modules:
  0.0 34.0 jit_solution(14227971343133299723)
XLA Ops:
  0.0 0.7 %collective-permute-start = (bf16[4,8,640]{2,1,0:T(8,128)(2,1)}, bf16[4,8,640]{2,1,0:T(8,128)(2,1)S(1)}, u32[]{:S(2)}, u32[]{:S(2)}) collective-permute-start(bf16[4,8,640]{2,1,0:T(8,128)(2,1)} %bitcast.18), channel_id=1, source_target_pairs={{0,1},{1,0},{2,3},{3,2},{4,5},{5,4},{6,7},{7,6},{8,9},{9,8},{10,11... | collective-permute-start | bytes 122888 | tf_op jit(solution)/shard_map/ppermute | solution.py:316
  0.7 0.7 %dynamic-slice_bitcast_fusion = (bf16[8,640]{1,0:T(8,128)(2,1)S(1)}, bf16[8,640]{1,0:T(8,128)(2,1)S(1)}, bf16[8,640]{1,0:T(8,128)(2,1)S(1)}) fusion(bf16[4,1,8,640]{3,2,1,0:T(8,128)(2,1)} %param.6, s32[]{:T(128)S(6)} %select_n.65, s32[]{:T(128)S(6)} %select_n.63, s32[]{:T(128)S(6)} %select_n.61), kind=kLoop, calls=%fused_computation.4 | loop fusion | bytes 61452 | tf_op jit(solution)/shard_map/jit(dynamic_index_in_dim)/squeeze | solution.py:318
  1.4 0.0 copy-start.1
  1.4 0.3 collective-permute-done.refs_3_
  1.8 2.6 %collective-permute-start.1 = (bf16[16,640]{1,0:T(8,128)(2,1)S(1)}, bf16[16,640]{1,0:T(8,128)(2,1)S(1)}, u32[]{:S(2)}, u32[]{:S(2)}) collective-permute-start(bf16[16,640]{1,0:T(8,128)(2,1)S(1)} %get-tuple-element.23), channel_id=1, source_target_pairs={{0,3},{1,4},{2,1},{3,6},{4,7},{5,0},{6,5},{7,2},{8,11},{9,12},{10,... | collective-permute-start | bytes 61448 | tf_op jit(solution)/shard_map/ppermute | solution.py:340
  4.4 1.2 %collective-permute-start.3 = (bf16[16,640]{1,0:T(8,128)(2,1)S(1)}, bf16[16,640]{1,0:T(8,128)(2,1)S(1)}, u32[]{:S(2)}, u32[]{:S(2)}) collective-permute-start(bf16[16,640]{1,0:T(8,128)(2,1)S(1)} %get-tuple-element.24), channel_id=1, source_target_pairs={{0,1},{1,6},{2,3},{3,4},{4,5},{5,2},{6,7},{7,0},{8,9},{9,14},{10,1... | collective-permute-start | bytes 61448 | tf_op jit(solution)/shard_map/ppermute | solution.py:340
  5.6 0.0 collective-permute-done.1.refs_2_
  5.6 0.7 %collective-permute-start.2 = (bf16[16,640]{1,0:T(8,128)(2,1)S(1)}, bf16[16,640]{1,0:T(8,128)(2,1)S(1)}, u32[]{:S(2)}, u32[]{:S(2)}) collective-permute-start(bf16[16,640]{1,0:T(8,128)(2,1)S(1)} %collective-permute-done.1.refs_2_), channel_id=1, source_target_pairs={{0,1},{1,0},{2,3},{3,2},{4,5},{5,4},{6,7},{7,6},{8,9},{9,8},{10,11... | collective-permute-start | bytes 61448 | tf_op jit(solution)/shard_map/ppermute | solution.py:343
  6.3 0.2 collective-permute-done.3.refs_3_
  6.5 0.6 %collective-permute-done.2.refs_1_ = bf16[16,640]{1,0:T(8,128)(2,1)S(1)} collective-permute-done((bf16[16,640]{1,0:T(8,128)(2,1)S(1)}, bf16[16,640]{1,0:T(8,128)(2,1)S(1)}, u32[]{:S(2)}, u32[]{:S(2)}) %collective-permute-start.2) | collective-permute-done | bytes 20512 | tf_op jit(solution)/shard_map/ppermute | solution.py:343
  7.1 0.0 slice-done
  7.1 0.0 slice-done.1
  7.1 0.0 copy-done
  7.1 0.0 copy-done.1
  7.2 1.5 %collective-permute-start.4 = (bf16[64,1024]{1,0:T(8,128)(2,1)S(1)}, bf16[64,1024]{1,0:T(8,128)(2,1)S(1)}, u32[]{:S(2)}, u32[]{:S(2)}) collective-permute-start(bf16[64,1024]{1,0:T(8,128)(2,1)S(1)} %shard_map.65), channel_id=1, source_target_pairs={{8,9},{9,1},{1,0},{10,11},{11,3},{3,2},{12,13},{13,5},{5,4},{14,15... | collective-permute-start | bytes 393224 | tf_op jit(solution)/shard_map/ppermute | solution.py:354
  8.6 0.1 shard_map.66
  8.7 0.9 %collective-permute-done.4.latent = bf16[64,1024]{1,0:T(8,128)(2,1)S(1)} collective-permute-done((bf16[64,1024]{1,0:T(8,128)(2,1)S(1)}, bf16[64,1024]{1,0:T(8,128)(2,1)S(1)}, u32[]{:S(2)}, u32[]{:S(2)}) %collective-permute-start.4) | collective-permute-done | bytes 131104 | tf_op jit(solution)/shard_map/ppermute | solution.py:354
  9.6 1.0 %collective-permute-start.5 = (bf16[64,1024]{1,0:T(8,128)(2,1)S(1)}, bf16[64,1024]{1,0:T(8,128)(2,1)S(1)}, u32[]{:S(2)}, u32[]{:S(2)}) collective-permute-start(bf16[64,1024]{1,0:T(8,128)(2,1)S(1)} %shard_map.67), channel_id=1, source_target_pairs={{16,17},{17,9},{9,8},{18,19},{19,11},{11,10},{20,21},{21,13},{13,1... | collective-permute-start | bytes 393224 | tf_op jit(solution)/shard_map/ppermute | solution.py:354
  10.6 2.5 %collective-permute-done.5.latent = bf16[64,1024]{1,0:T(8,128)(2,1)S(1)} collective-permute-done((bf16[64,1024]{1,0:T(8,128)(2,1)S(1)}, bf16[64,1024]{1,0:T(8,128)(2,1)S(1)}, u32[]{:S(2)}, u32[]{:S(2)}) %collective-permute-start.5) | collective-permute-done | bytes 131104 | tf_op jit(solution)/shard_map/ppermute | solution.py:354
  13.1 8.7 %collective-permute-start.6 = (bf16[64,1024]{1,0:T(8,128)(2,1)S(1)}, bf16[64,1024]{1,0:T(8,128)(2,1)S(1)}, u32[]{:S(2)}, u32[]{:S(2)}) collective-permute-start(bf16[64,1024]{1,0:T(8,128)(2,1)S(1)} %shard_map.68), channel_id=1, source_target_pairs={{24,25},{25,17},{17,16},{26,27},{27,19},{19,18},{28,29},{29,21},{2... | collective-permute-start | bytes 393224 | tf_op jit(solution)/shard_map/ppermute | solution.py:358
  21.9 1.0 %collective-permute-done.6.latent = bf16[64,1024]{1,0:T(8,128)(2,1)S(1)} collective-permute-done((bf16[64,1024]{1,0:T(8,128)(2,1)S(1)}, bf16[64,1024]{1,0:T(8,128)(2,1)S(1)}, u32[]{:S(2)}, u32[]{:S(2)}) %collective-permute-start.6) | collective-permute-done | bytes 131104 | tf_op jit(solution)/shard_map/ppermute | solution.py:358
  22.9 1.5 %collective-permute-start.10 = (bf16[16,640]{1,0:T(8,128)(2,1)S(1)}, bf16[16,640]{1,0:T(8,128)(2,1)S(1)}, u32[]{:S(2)}, u32[]{:S(2)}) collective-permute-start(bf16[16,640]{1,0:T(8,128)(2,1)S(1)} %get-tuple-element.32), channel_id=1, source_target_pairs={{24,15},{26,5},{28,27},{30,17},{27,26},{15,14},{5,4},{17,16},{14,3... | collective-permute-start | bytes 61448 | tf_op jit(solution)/shard_map/ppermute | solution.py:368
  24.4 4.5 %collective-permute-start.7 = (bf16[16,640]{1,0:T(8,128)(2,1)S(1)}, bf16[16,640]{1,0:T(8,128)(2,1)S(1)}, u32[]{:S(2)}, u32[]{:S(2)}) collective-permute-start(bf16[16,640]{1,0:T(8,128)(2,1)S(1)} %get-tuple-element.29), channel_id=1, source_target_pairs={{24,13},{26,7},{28,25},{30,19},{25,24},{13,12},{7,6},{19,18},{27,2... | collective-permute-start | bytes 61448 | tf_op jit(solution)/shard_map/ppermute | solution.py:368
  28.9 0.0 collective-permute-start.8
  28.9 0.5 %collective-permute-start.9 = (bf16[16,640]{1,0:T(8,128)(2,1)S(1)}, bf16[16,640]{1,0:T(8,128)(2,1)S(1)}, u32[]{:S(2)}, u32[]{:S(2)}) collective-permute-start(bf16[16,640]{1,0:T(8,128)(2,1)S(1)} %get-tuple-element.31), channel_id=1, source_target_pairs={{24,9},{26,3},{28,29},{30,23},{29,28},{9,8},{3,2},{23,22},{8,24},{... | collective-permute-start | bytes 61448 | tf_op jit(solution)/shard_map/ppermute | solution.py:368
  29.5 2.6 %collective-permute-done.10 = bf16[16,640]{1,0:T(8,128)(2,1)S(1)} collective-permute-done((bf16[16,640]{1,0:T(8,128)(2,1)S(1)}, bf16[16,640]{1,0:T(8,128)(2,1)S(1)}, u32[]{:S(2)}, u32[]{:S(2)}) %collective-permute-start.10) | collective-permute-done | bytes 20512 | tf_op jit(solution)/shard_map/ppermute | solution.py:368
  32.1 0.0 collective-permute-done.7
  32.1 0.0 collective-permute-done.8
  32.1 0.0 collective-permute-done.9
  32.1 0.1 collective-permute-start.11
  32.2 1.2 %collective-permute-done.11 = bf16[8,640]{1,0:T(8,128)(2,1)S(1)} collective-permute-done((bf16[8,640]{1,0:T(8,128)(2,1)S(1)}, bf16[8,640]{1,0:T(8,128)(2,1)S(1)}, u32[]{:S(2)}, u32[]{:S(2)}) %collective-permute-start.11) | collective-permute-done | bytes 10272 | tf_op jit(solution)/shard_map/ppermute | solution.py:373
  33.4 0.6 %fusion.1 = f32[1,1,8,640]{3,2,1,0:T(8,128)} fusion(bf16[8,640]{1,0:T(8,128)(2,1)S(1)} %collective-permute-done.11, bf16[16,640]{1,0:T(8,128)(2,1)S(1)} %select_select_fusion, pred[]{:T(512)S(6)} %eq.19), kind=kLoop, calls=%fused_computation.3 | loop fusion | flops 10240 | bytes 40961 | tf_op jit(solution)/shard_map/broadcast_in_dim | solution.py:375
  (11 shorter events, 0.1 us)
Async XLA Ops:
  0.0 1.8 %collective-permute-start = (bf16[4,8,640]{2,1,0:T(8,128)(2,1)}, bf16[4,8,640]{2,1,0:T(8,128)(2,1)S(1)}, u32[]{:S(2)}, u32[]{:S(2)}) collective-permute-start(bf16[4,8,640]{2,1,0:T(8,128)(2,1)} %bitcast.18), channel_id=1, source_target_pairs={{0,1},{1,0},{2,3},{3,2},{4,5},{5,4},{6,7},{7,6},{8,9},{9,8},{10,11... | collective-permute-start | bytes 122888 | tf_op jit(solution)/shard_map/ppermute | solution.py:316
  1.4 5.7 %slice-start = ((s8[8388608]{0:T(1024)(128)(4,1)}), s8[4194304]{0:T(1024)(128)(4,1)S(1)}, s32[]{:S(2)}) async-start(s8[8388608]{0:T(1024)(128)(4,1)} %bitcast.15), calls=%async_computation | async-start | bytes 8388608
  1.4 5.7 %slice-start.1 = ((s8[8388608]{0:T(1024)(128)(4,1)}), s8[4194304]{0:T(1024)(128)(4,1)S(1)}, s32[]{:S(2)}) async-start(s8[8388608]{0:T(1024)(128)(4,1)} %bitcast.15), calls=%async_computation.1 | async-start | bytes 8388608
  1.4 5.7 %copy-start = (bf16[640,1024]{1,0:T(8,128)(2,1)S(1)}, bf16[640,1024]{1,0:T(8,128)(2,1)}, u32[]{:S(2)}) copy-start(bf16[640,1024]{1,0:T(8,128)(2,1)} %refs_4_.1) | copy-start | bytes 3932164
  1.4 5.7 %copy-start.1 = (f32[1,1024]{1,0:T(1,128)S(1)}, f32[1,1024]{1,0:T(1,128)}, u32[]{:S(2)}) copy-start(f32[1,1024]{1,0:T(1,128)} %gain.1) | copy-start | bytes 12292
  1.8 3.8 %collective-permute-start.1 = (bf16[16,640]{1,0:T(8,128)(2,1)S(1)}, bf16[16,640]{1,0:T(8,128)(2,1)S(1)}, u32[]{:S(2)}, u32[]{:S(2)}) collective-permute-start(bf16[16,640]{1,0:T(8,128)(2,1)S(1)} %get-tuple-element.23), channel_id=1, source_target_pairs={{0,3},{1,4},{2,1},{3,6},{4,7},{5,0},{6,5},{7,2},{8,11},{9,12},{10,... | collective-permute-start | bytes 61448 | tf_op jit(solution)/shard_map/ppermute | solution.py:340
  4.4 2.1 %collective-permute-start.3 = (bf16[16,640]{1,0:T(8,128)(2,1)S(1)}, bf16[16,640]{1,0:T(8,128)(2,1)S(1)}, u32[]{:S(2)}, u32[]{:S(2)}) collective-permute-start(bf16[16,640]{1,0:T(8,128)(2,1)S(1)} %get-tuple-element.24), channel_id=1, source_target_pairs={{0,1},{1,6},{2,3},{3,4},{4,5},{5,2},{6,7},{7,0},{8,9},{9,14},{10,1... | collective-permute-start | bytes 61448 | tf_op jit(solution)/shard_map/ppermute | solution.py:340
  5.6 1.5 %collective-permute-start.2 = (bf16[16,640]{1,0:T(8,128)(2,1)S(1)}, bf16[16,640]{1,0:T(8,128)(2,1)S(1)}, u32[]{:S(2)}, u32[]{:S(2)}) collective-permute-start(bf16[16,640]{1,0:T(8,128)(2,1)S(1)} %collective-permute-done.1.refs_2_), channel_id=1, source_target_pairs={{0,1},{1,0},{2,3},{3,2},{4,5},{5,4},{6,7},{7,6},{8,9},{9,8},{10,11... | collective-permute-start | bytes 61448 | tf_op jit(solution)/shard_map/ppermute | solution.py:343
  7.2 2.5 %collective-permute-start.4 = (bf16[64,1024]{1,0:T(8,128)(2,1)S(1)}, bf16[64,1024]{1,0:T(8,128)(2,1)S(1)}, u32[]{:S(2)}, u32[]{:S(2)}) collective-permute-start(bf16[64,1024]{1,0:T(8,128)(2,1)S(1)} %shard_map.65), channel_id=1, source_target_pairs={{8,9},{9,1},{1,0},{10,11},{11,3},{3,2},{12,13},{13,5},{5,4},{14,15... | collective-permute-start | bytes 393224 | tf_op jit(solution)/shard_map/ppermute | solution.py:354
  9.6 3.5 %collective-permute-start.5 = (bf16[64,1024]{1,0:T(8,128)(2,1)S(1)}, bf16[64,1024]{1,0:T(8,128)(2,1)S(1)}, u32[]{:S(2)}, u32[]{:S(2)}) collective-permute-start(bf16[64,1024]{1,0:T(8,128)(2,1)S(1)} %shard_map.67), channel_id=1, source_target_pairs={{16,17},{17,9},{9,8},{18,19},{19,11},{11,10},{20,21},{21,13},{13,1... | collective-permute-start | bytes 393224 | tf_op jit(solution)/shard_map/ppermute | solution.py:354
  13.1 9.7 %collective-permute-start.6 = (bf16[64,1024]{1,0:T(8,128)(2,1)S(1)}, bf16[64,1024]{1,0:T(8,128)(2,1)S(1)}, u32[]{:S(2)}, u32[]{:S(2)}) collective-permute-start(bf16[64,1024]{1,0:T(8,128)(2,1)S(1)} %shard_map.68), channel_id=1, source_target_pairs={{24,25},{25,17},{17,16},{26,27},{27,19},{19,18},{28,29},{29,21},{2... | collective-permute-start | bytes 393224 | tf_op jit(solution)/shard_map/ppermute | solution.py:358
  22.9 9.2 %collective-permute-start.10 = (bf16[16,640]{1,0:T(8,128)(2,1)S(1)}, bf16[16,640]{1,0:T(8,128)(2,1)S(1)}, u32[]{:S(2)}, u32[]{:S(2)}) collective-permute-start(bf16[16,640]{1,0:T(8,128)(2,1)S(1)} %get-tuple-element.32), channel_id=1, source_target_pairs={{24,15},{26,5},{28,27},{30,17},{27,26},{15,14},{5,4},{17,16},{14,3... | collective-permute-start | bytes 61448 | tf_op jit(solution)/shard_map/ppermute | solution.py:368
  24.4 7.7 %collective-permute-start.7 = (bf16[16,640]{1,0:T(8,128)(2,1)S(1)}, bf16[16,640]{1,0:T(8,128)(2,1)S(1)}, u32[]{:S(2)}, u32[]{:S(2)}) collective-permute-start(bf16[16,640]{1,0:T(8,128)(2,1)S(1)} %get-tuple-element.29), channel_id=1, source_target_pairs={{24,13},{26,7},{28,25},{30,19},{25,24},{13,12},{7,6},{19,18},{27,2... | collective-permute-start | bytes 61448 | tf_op jit(solution)/shard_map/ppermute | solution.py:368
  28.9 3.1 %collective-permute-start.8 = (bf16[16,640]{1,0:T(8,128)(2,1)S(1)}, bf16[16,640]{1,0:T(8,128)(2,1)S(1)}, u32[]{:S(2)}, u32[]{:S(2)}) collective-permute-start(bf16[16,640]{1,0:T(8,128)(2,1)S(1)} %get-tuple-element.30), channel_id=1, source_target_pairs={{24,11},{26,1},{28,31},{30,21},{31,30},{11,10},{1,0},{21,20},{10,2... | collective-permute-start | bytes 61448 | tf_op jit(solution)/shard_map/ppermute | solution.py:368
  28.9 3.1 %collective-permute-start.9 = (bf16[16,640]{1,0:T(8,128)(2,1)S(1)}, bf16[16,640]{1,0:T(8,128)(2,1)S(1)}, u32[]{:S(2)}, u32[]{:S(2)}) collective-permute-start(bf16[16,640]{1,0:T(8,128)(2,1)S(1)} %get-tuple-element.31), channel_id=1, source_target_pairs={{24,9},{26,3},{28,29},{30,23},{29,28},{9,8},{3,2},{23,22},{8,24},{... | collective-permute-start | bytes 61448 | tf_op jit(solution)/shard_map/ppermute | solution.py:368
  32.1 1.2 %collective-permute-start.11 = (bf16[8,640]{1,0:T(8,128)(2,1)S(1)}, bf16[8,640]{1,0:T(8,128)(2,1)S(1)}, u32[]{:S(2)}, u32[]{:S(2)}) collective-permute-start(bf16[8,640]{1,0:T(8,128)(2,1)S(1)} %slice.8), channel_id=1, source_target_pairs={{0,1},{1,0},{2,3},{3,2},{4,5},{5,4},{6,7},{7,6},{8,9},{9,8},{10,11... | collective-permute-start | bytes 30728 | tf_op jit(solution)/shard_map/ppermute | solution.py:373

commit v7 on v6

--- a/solution.py
+++ b/solution.py
@@ -73,13 +73,13 @@
 
 
 def leads(group, segment):
-    return (lax.axis_index("segment") == segment) & (lax.rem(lax.axis_index("lon"), group) == 0)
+    return (lax.axis_index("segment") == segment) & (lax.rem(lax.axis_index("lon"), group) == segment % 2)
 
 
 def load_kernel(segments, group, hint, weights, decoder, gain, final_gain, *rest):
     weights_out, decoder_out, gain_out, final_out, sems = rest
     segment = lax.axis_index("segment")
-    leader = lax.rem(lax.axis_index("lon"), group) == 0
+    leader = lax.rem(lax.axis_index("lon"), group) == lax.rem(segment, 2)
 
     def move(pairs):
         copies = [
@@ -238,12 +238,14 @@
 
 def detour(tick, groups):
     links = {}
+    here, there = tick % 2, (tick - 1) % 2
     for g in range(groups):
-        links |= {(tick, g, 0): (tick, g, 1), (tick, g, 1): (tick - 1, g, 1), (tick - 1, g, 1): (tick - 1, g, 0)}
+        links |= {(tick, g, here): (tick, g, here ^ 1), (tick, g, here ^ 1): (tick - 1, g, there ^ 1)}
+        links |= {(tick - 1, g, there ^ 1): (tick - 1, g, there)}
     return links
 
 
-def ring_up(devices, links):
+def ring_up(devices, links, free):
     alone = []
     for one in devices:
         mate = (one[0], one[1], one[2] ^ 1)
@@ -258,35 +260,34 @@
         links[one], links[two] = two, one
         alone = [three for three in alone if three not in (one, two)]
     for one in alone:
-        two = min((two for two in devices if two != one and two[2] == 1), key=lambda two: apart(one, two))
+        two = min((two for two in devices if two != one and two[2] == free), key=lambda two: apart(one, two))
         after = links[two]
         links[one], links[two], links[after] = two, after, one
 
 
 def fan_pairs(k, segments, groups, group, late):
     last = segments - 1
+    work = last % 2
+    free = work ^ 1
     devices = [(s, g, c) for s in range(segments) for g in range(groups) for c in range(group)]
-    links = {(last, g, 0): (g ^ 1, g ^ k, 1) for g in range(groups)}
+    links = {(last, g, work): (g ^ 1, g ^ k, free) for g in range(groups)}
     taken = list(links.values())
-    outside = [one for one in taken if one[0] != last]
-    inside = [one for one in taken if one[0] == last]
-    for s, g, c in inside:
-        links[(s, g, 1)] = (s, g, 0)
-    for s, g, c in outside:
-        links[(s, g, 1)] = (s, g, 0)
-    givers = [(s, g, 0) for s, g, c in outside]
-    takers = [(last, g, 0) for g in range(groups) if (last, g, 1) not in inside]
-    waiting = [one for one in late if one[0] == last and one not in links]
+    for s, g, _ in taken:
+        links[(s, g, free)] = (s, g, work)
+    inside = [g for s, g, _ in taken if s == last]
+    givers = [(s, g, work) for s, g, _ in taken if s != last]
+    takers = [(last, g, work) for g in range(groups) if g not in inside]
+    waiting = [one for one in sorted(late) if one[0] == last and one not in links]
     if len(waiting) % 2 and len(waiting) < groups - 1:
         one = waiting[0]
-        links[one] = (last, one[1], 0)
+        links[one] = (last, one[1], work)
         takers[takers.index(links[one])] = one
     for one, column in zip(givers, assign([[apart(one, two) + 0.0 for two in takers] for one in givers])):
         links[one] = takers[column]
     idle = [one for one in devices if one not in links]
-    ring_up([one for one in idle if one not in late], links)
-    ring_up([one for one in idle if one in late], links)
-    late |= {(s, g, c) for s, g, _ in taken for c in range(2)} - {(last, g, 0) for g in range(groups)}
+    ring_up([one for one in idle if one not in late], links, free)
+    ring_up([one for one in idle if one in late], links, free)
+    late |= {(s, g, c) for s, g, _ in taken for c in range(2)} - {(last, g, work) for g in range(groups)}
     number = {one: index for index, one in enumerate(devices)}
     assert len(set(links.values())) == len(links) == len(devices)
     return [(number[one], number[two]) for one, two in links.items()]
@@ -350,17 +351,18 @@
     first = [in_vmem(value) for value in (encoder_weight, layer_weights[0], layer_gains)]
     latent = call(functools.partial(first_kernel, group), latent_shape, pieces + first)
     for tick in range(1, segments - 1):
-        edges = {(tick - 1, g, 0): (tick, g, 0) for g in range(bands)}
+        edges = {(tick - 1, g, (tick - 1) % 2): (tick, g, tick % 2) for g in range(bands)}
         latent = lax.ppermute(latent, BOTH, full_pairs(edges, segments, bands, group, detour(tick, bands)))
         latent = call(functools.partial(middle_kernel, tick, group), latent_shape, [latent, weights, gain])
     last = segments - 1
-    edges = {(last - 1, g, 0): (last, g, 0) for g in range(bands)}
+    edges = {(last - 1, g, (last - 1) % 2): (last, g, last % 2) for g in range(bands)}
     latent = lax.ppermute(latent, BOTH, full_pairs(edges, segments, bands, group, detour(last, bands)))
     parts = call(
         functools.partial(last_kernel, last, group, lon_local, turns),
         [part_shape] * bands,
         [latent, weights, gain, final_gain, decoder],
     )
+    first = last % 2 ^ 1
     segment_id = lax.axis_index("segment")
     late, picked = set(), None
     ways = {k: fan_pairs(k, segments, bands, group, late) for k in range(bands - 1, -1, -1)}
@@ -368,10 +370,10 @@
         taken = lax.ppermute(parts[k], BOTH, ways[k])
         picked = taken if picked is None else jnp.where(place ^ segment_id ^ 1 == k, taken, picked)
     rows = [picked[c * lon_local : (c + 1) * lon_local] for c in range(group)]
-    answer = rows[1]
+    answer = rows[first]
     for e in range(1, group):
-        handed = lax.ppermute(rows[1 ^ e], BOTH, everywhere(segments, lons, e))
-        answer = jnp.where(member == 1 ^ e, handed, answer)
+        handed = lax.ppermute(rows[first ^ e], BOTH, everywhere(segments, lons, e))
+        answer = jnp.where(member == first ^ e, handed, answer)
     return answer.astype(jnp.float32)[None, None]
 
 

time: 34.4 us -> 32.9 us (0.956)
  waiting for transfers between devices: 9.35 us -> 7.04 us
  starting transfers between devices: 23 us -> 24 us
    ppermute x1, starting transfers between devices: 0.07 us -> 2.32 us  [body(): handed = lax.ppermute(rows[first ^ e], BOTH, everywhere(segments, lons, e))]
    ppermute x4, waiting for transfers between devices: 2.62 us -> 1.19 us  [body(): taken = lax.ppermute(parts[k], BOTH, ways[k])]
    ppermute x4, starting transfers between devices: 6.6 us -> 5.64 us  [body(): taken = lax.ppermute(parts[k], BOTH, ways[k])]
    ppermute x3, waiting for transfers between devices: 4.41 us -> 3.86 us  [body(): lax.ppermute(latent, BOTH, full_pairs(edges, segments, bands, group, deto...]
    ppermute x3, starting transfers between devices: 11.2 us -> 10.9 us  [body(): lax.ppermute(latent, BOTH, full_pairs(edges, segments, bands, group, deto...]
  transfers between devices with their start and end apart: 12 -> 12, of which waited for: 8 -> 11; matrix products, arithmetic and copies ran while one was open for 2% -> 2% of each run, Pallas kernels for 0% -> 0%
where the time goes in v7:
time: 32.9 us; the launch traced here: 32.6 us
  starting transfers between devices  24 us (73%)
  waiting for transfers between devices  7.04 us (21%)
  local copies, waits for them, and re-layouts  0.76 us (2%)
  other arithmetic  0.63 us (2%)
    ppermute x3, starting transfers between devices, body(): lax.ppermute(latent, BOTH, full_pairs(edges, segments, bands, group, deto...  10.9 us
    ppermute x4, starting transfers between devices, body(): taken = lax.ppermute(parts[k], BOTH, ways[k])  5.64 us
    ppermute x3, waiting for transfers between devices, body(): lax.ppermute(latent, BOTH, full_pairs(edges, segments, bands, group, deto...  3.86 us
    ppermute x2, starting transfers between devices, body(): taken = lax.ppermute(piece, BOTH, pairs)  3.82 us
    ppermute x1, starting transfers between devices, body(): handed = lax.ppermute(rows[first ^ e], BOTH, everywhere(segments, lons, e))  2.32 us
    ppermute x4, waiting for transfers between devices, body(): taken = lax.ppermute(parts[k], BOTH, ways[k])  1.19 us
    ppermute x1, waiting for transfers between devices, body(): handed = lax.ppermute(rows[first ^ e], BOTH, everywhere(segments, lons, e))  0.83 us
    squeeze x1, local copies, waits for them, and re-layouts, body(): lax.dynamic_index_in_dim(own, place ^ sent_way(row, member) ^ 1, 0, keepd...  0.74 us
  transfers between devices with their start and end apart: 12, of which 11 were waited for; matrix products, arithmetic and copies ran while one was open for 2% of the time, Pallas kernels for 0%

profile of v7, /device:TPU:5, one launch (start us, length us, event | category | flops | bytes accessed | tf_op | source)
XLA Modules:
  0.0 32.6 jit_solution(3301949869819984736)
XLA Ops:
  0.0 0.7 %collective-permute-start = (bf16[4,8,640]{2,1,0:T(8,128)(2,1)}, bf16[4,8,640]{2,1,0:T(8,128)(2,1)S(1)}, u32[]{:S(2)}, u32[]{:S(2)}) collective-permute-start(bf16[4,8,640]{2,1,0:T(8,128)(2,1)} %bitcast.18), channel_id=1, source_target_pairs={{0,1},{1,0},{2,3},{3,2},{4,5},{5,4},{6,7},{7,6},{8,9},{9,8},{10,11... | collective-permute-start | bytes 122888 | tf_op jit(solution)/shard_map/ppermute | solution.py:317
  0.7 0.7 %dynamic-slice_bitcast_fusion = (bf16[8,640]{1,0:T(8,128)(2,1)S(1)}, bf16[8,640]{1,0:T(8,128)(2,1)S(1)}, bf16[8,640]{1,0:T(8,128)(2,1)S(1)}) fusion(bf16[4,1,8,640]{3,2,1,0:T(8,128)(2,1)} %param.6, s32[]{:T(128)S(6)} %select_n.65, s32[]{:T(128)S(6)} %select_n.63, s32[]{:T(128)S(6)} %select_n.61), kind=kLoop, calls=%fused_computation.4 | loop fusion | bytes 61452 | tf_op jit(solution)/shard_map/jit(dynamic_index_in_dim)/squeeze | solution.py:319
  1.4 0.0 copy-start.1
  1.4 0.3 collective-permute-done.refs_3_
  1.8 2.6 %collective-permute-start.1 = (bf16[16,640]{1,0:T(8,128)(2,1)S(1)}, bf16[16,640]{1,0:T(8,128)(2,1)S(1)}, u32[]{:S(2)}, u32[]{:S(2)}) collective-permute-start(bf16[16,640]{1,0:T(8,128)(2,1)S(1)} %get-tuple-element.23), channel_id=1, source_target_pairs={{0,3},{1,4},{2,1},{3,6},{4,7},{5,0},{6,5},{7,2},{8,11},{9,12},{10,... | collective-permute-start | bytes 61448 | tf_op jit(solution)/shard_map/ppermute | solution.py:341
  4.4 1.2 %collective-permute-start.3 = (bf16[16,640]{1,0:T(8,128)(2,1)S(1)}, bf16[16,640]{1,0:T(8,128)(2,1)S(1)}, u32[]{:S(2)}, u32[]{:S(2)}) collective-permute-start(bf16[16,640]{1,0:T(8,128)(2,1)S(1)} %get-tuple-element.24), channel_id=1, source_target_pairs={{0,1},{1,6},{2,3},{3,4},{4,5},{5,2},{6,7},{7,0},{8,9},{9,14},{10,1... | collective-permute-start | bytes 61448 | tf_op jit(solution)/shard_map/ppermute | solution.py:341
  5.6 0.0 collective-permute-done.1.refs_2_
  5.6 0.7 %collective-permute-start.2 = (bf16[16,640]{1,0:T(8,128)(2,1)S(1)}, bf16[16,640]{1,0:T(8,128)(2,1)S(1)}, u32[]{:S(2)}, u32[]{:S(2)}) collective-permute-start(bf16[16,640]{1,0:T(8,128)(2,1)S(1)} %collective-permute-done.1.refs_2_), channel_id=1, source_target_pairs={{0,1},{1,0},{2,3},{3,2},{4,5},{5,4},{6,7},{7,6},{8,9},{9,8},{10,11... | collective-permute-start | bytes 61448 | tf_op jit(solution)/shard_map/ppermute | solution.py:344
  6.3 0.2 collective-permute-done.3.refs_3_
  6.5 0.6 %collective-permute-done.2.refs_1_ = bf16[16,640]{1,0:T(8,128)(2,1)S(1)} collective-permute-done((bf16[16,640]{1,0:T(8,128)(2,1)S(1)}, bf16[16,640]{1,0:T(8,128)(2,1)S(1)}, u32[]{:S(2)}, u32[]{:S(2)}) %collective-permute-start.2) | collective-permute-done | bytes 20512 | tf_op jit(solution)/shard_map/ppermute | solution.py:344
  7.1 0.0 slice-done
  7.1 0.0 slice-done.1
  7.1 0.0 copy-done
  7.1 0.0 copy-done.1
  7.2 1.5 %collective-permute-start.4 = (bf16[64,1024]{1,0:T(8,128)(2,1)S(1)}, bf16[64,1024]{1,0:T(8,128)(2,1)S(1)}, u32[]{:S(2)}, u32[]{:S(2)}) collective-permute-start(bf16[64,1024]{1,0:T(8,128)(2,1)S(1)} %shard_map.65), channel_id=1, source_target_pairs={{9,8},{8,1},{1,0},{11,10},{10,3},{3,2},{13,12},{12,5},{5,4},{15,14... | collective-permute-start | bytes 393224 | tf_op jit(solution)/shard_map/ppermute | solution.py:355
  8.6 0.1 shard_map.66
  8.7 0.9 %collective-permute-done.4.latent = bf16[64,1024]{1,0:T(8,128)(2,1)S(1)} collective-permute-done((bf16[64,1024]{1,0:T(8,128)(2,1)S(1)}, bf16[64,1024]{1,0:T(8,128)(2,1)S(1)}, u32[]{:S(2)}, u32[]{:S(2)}) %collective-permute-start.4) | collective-permute-done | bytes 131104 | tf_op jit(solution)/shard_map/ppermute | solution.py:355
  9.6 2.6 %collective-permute-start.5 = (bf16[64,1024]{1,0:T(8,128)(2,1)S(1)}, bf16[64,1024]{1,0:T(8,128)(2,1)S(1)}, u32[]{:S(2)}, u32[]{:S(2)}) collective-permute-start(bf16[64,1024]{1,0:T(8,128)(2,1)S(1)} %shard_map.67), channel_id=1, source_target_pairs={{16,17},{17,8},{8,9},{18,19},{19,10},{10,11},{20,21},{21,12},{12,1... | collective-permute-start | bytes 393224 | tf_op jit(solution)/shard_map/ppermute | solution.py:355
  12.2 1.9 %collective-permute-done.5.latent = bf16[64,1024]{1,0:T(8,128)(2,1)S(1)} collective-permute-done((bf16[64,1024]{1,0:T(8,128)(2,1)S(1)}, bf16[64,1024]{1,0:T(8,128)(2,1)S(1)}, u32[]{:S(2)}, u32[]{:S(2)}) %collective-permute-start.5) | collective-permute-done | bytes 131104 | tf_op jit(solution)/shard_map/ppermute | solution.py:355
  14.2 6.8 %collective-permute-start.6 = (bf16[64,1024]{1,0:T(8,128)(2,1)S(1)}, bf16[64,1024]{1,0:T(8,128)(2,1)S(1)}, u32[]{:S(2)}, u32[]{:S(2)}) collective-permute-start(bf16[64,1024]{1,0:T(8,128)(2,1)S(1)} %shard_map.68), channel_id=1, source_target_pairs={{25,24},{24,17},{17,16},{27,26},{26,19},{19,18},{29,28},{28,21},{2... | collective-permute-start | bytes 393224 | tf_op jit(solution)/shard_map/ppermute | solution.py:359
  21.0 1.0 %collective-permute-done.6.latent = bf16[64,1024]{1,0:T(8,128)(2,1)S(1)} collective-permute-done((bf16[64,1024]{1,0:T(8,128)(2,1)S(1)}, bf16[64,1024]{1,0:T(8,128)(2,1)S(1)}, u32[]{:S(2)}, u32[]{:S(2)}) %collective-permute-start.6) | collective-permute-done | bytes 131104 | tf_op jit(solution)/shard_map/ppermute | solution.py:359
  22.0 5.1 %collective-permute-start.10 = (bf16[16,640]{1,0:T(8,128)(2,1)S(1)}, bf16[16,640]{1,0:T(8,128)(2,1)S(1)}, u32[]{:S(2)}, u32[]{:S(2)}) collective-permute-start(bf16[16,640]{1,0:T(8,128)(2,1)S(1)} %get-tuple-element.32), channel_id=1, source_target_pairs={{25,14},{27,4},{29,26},{31,16},{14,15},{4,5},{26,27},{16,17},{15,3... | collective-permute-start | bytes 61448 | tf_op jit(solution)/shard_map/ppermute | solution.py:370
  27.1 0.0 collective-permute-start.7
  27.1 0.5 %collective-permute-start.8 = (bf16[16,640]{1,0:T(8,128)(2,1)S(1)}, bf16[16,640]{1,0:T(8,128)(2,1)S(1)}, u32[]{:S(2)}, u32[]{:S(2)}) collective-permute-start(bf16[16,640]{1,0:T(8,128)(2,1)S(1)} %get-tuple-element.30), channel_id=1, source_target_pairs={{25,10},{27,0},{29,30},{31,20},{10,11},{0,1},{30,31},{20,21},{11,2... | collective-permute-start | bytes 61448 | tf_op jit(solution)/shard_map/ppermute | solution.py:370
  27.6 0.0 collective-permute-start.9
  27.6 0.4 %collective-permute-done.10 = bf16[16,640]{1,0:T(8,128)(2,1)S(1)} collective-permute-done((bf16[16,640]{1,0:T(8,128)(2,1)S(1)}, bf16[16,640]{1,0:T(8,128)(2,1)S(1)}, u32[]{:S(2)}, u32[]{:S(2)}) %collective-permute-start.10) | collective-permute-done | bytes 20512 | tf_op jit(solution)/shard_map/ppermute | solution.py:370
  28.0 0.3 collective-permute-done.7
  28.3 0.2 collective-permute-done.8
  28.4 0.3 %collective-permute-done.9 = bf16[16,640]{1,0:T(8,128)(2,1)S(1)} collective-permute-done((bf16[16,640]{1,0:T(8,128)(2,1)S(1)}, bf16[16,640]{1,0:T(8,128)(2,1)S(1)}, u32[]{:S(2)}, u32[]{:S(2)}) %collective-permute-start.9) | collective-permute-done | bytes 20512 | tf_op jit(solution)/shard_map/ppermute | solution.py:370
  28.8 2.3 %collective-permute-start.11 = (bf16[8,640]{1,0:T(8,128)(2,1)S(1)}, bf16[8,640]{1,0:T(8,128)(2,1)S(1)}, u32[]{:S(2)}, u32[]{:S(2)}) collective-permute-start(bf16[8,640]{1,0:T(8,128)(2,1)S(1)} %slice.8), channel_id=1, source_target_pairs={{0,1},{1,0},{2,3},{3,2},{4,5},{5,4},{6,7},{7,6},{8,9},{9,8},{10,11... | collective-permute-start | bytes 30728 | tf_op jit(solution)/shard_map/ppermute | solution.py:375
  31.1 0.8 %collective-permute-done.11 = bf16[8,640]{1,0:T(8,128)(2,1)S(1)} collective-permute-done((bf16[8,640]{1,0:T(8,128)(2,1)S(1)}, bf16[8,640]{1,0:T(8,128)(2,1)S(1)}, u32[]{:S(2)}, u32[]{:S(2)}) %collective-permute-start.11) | collective-permute-done | bytes 10272 | tf_op jit(solution)/shard_map/ppermute | solution.py:375
  32.0 0.6 %fusion.1 = f32[1,1,8,640]{3,2,1,0:T(8,128)} fusion(bf16[8,640]{1,0:T(8,128)(2,1)S(1)} %collective-permute-done.11, bf16[16,640]{1,0:T(8,128)(2,1)S(1)} %select_select_fusion, pred[]{:T(512)S(6)} %eq.17), kind=kLoop, calls=%fused_computation.3 | loop fusion | flops 10240 | bytes 40961 | tf_op jit(solution)/shard_map/broadcast_in_dim | solution.py:377
  (11 shorter events, 0.1 us)
Async XLA Ops:
  0.0 1.8 %collective-permute-start = (bf16[4,8,640]{2,1,0:T(8,128)(2,1)}, bf16[4,8,640]{2,1,0:T(8,128)(2,1)S(1)}, u32[]{:S(2)}, u32[]{:S(2)}) collective-permute-start(bf16[4,8,640]{2,1,0:T(8,128)(2,1)} %bitcast.18), channel_id=1, source_target_pairs={{0,1},{1,0},{2,3},{3,2},{4,5},{5,4},{6,7},{7,6},{8,9},{9,8},{10,11... | collective-permute-start | bytes 122888 | tf_op jit(solution)/shard_map/ppermute | solution.py:317
  1.4 5.7 %slice-start = ((s8[8388608]{0:T(1024)(128)(4,1)}), s8[4194304]{0:T(1024)(128)(4,1)S(1)}, s32[]{:S(2)}) async-start(s8[8388608]{0:T(1024)(128)(4,1)} %bitcast.15), calls=%async_computation | async-start | bytes 8388608
  1.4 5.7 %slice-start.1 = ((s8[8388608]{0:T(1024)(128)(4,1)}), s8[4194304]{0:T(1024)(128)(4,1)S(1)}, s32[]{:S(2)}) async-start(s8[8388608]{0:T(1024)(128)(4,1)} %bitcast.15), calls=%async_computation.1 | async-start | bytes 8388608
  1.4 5.7 %copy-start = (bf16[640,1024]{1,0:T(8,128)(2,1)S(1)}, bf16[640,1024]{1,0:T(8,128)(2,1)}, u32[]{:S(2)}) copy-start(bf16[640,1024]{1,0:T(8,128)(2,1)} %refs_4_.1) | copy-start | bytes 3932164
  1.4 5.7 %copy-start.1 = (f32[1,1024]{1,0:T(1,128)S(1)}, f32[1,1024]{1,0:T(1,128)}, u32[]{:S(2)}) copy-start(f32[1,1024]{1,0:T(1,128)} %gain.1) | copy-start | bytes 12292
  1.8 3.8 %collective-permute-start.1 = (bf16[16,640]{1,0:T(8,128)(2,1)S(1)}, bf16[16,640]{1,0:T(8,128)(2,1)S(1)}, u32[]{:S(2)}, u32[]{:S(2)}) collective-permute-start(bf16[16,640]{1,0:T(8,128)(2,1)S(1)} %get-tuple-element.23), channel_id=1, source_target_pairs={{0,3},{1,4},{2,1},{3,6},{4,7},{5,0},{6,5},{7,2},{8,11},{9,12},{10,... | collective-permute-start | bytes 61448 | tf_op jit(solution)/shard_map/ppermute | solution.py:341
  4.4 2.1 %collective-permute-start.3 = (bf16[16,640]{1,0:T(8,128)(2,1)S(1)}, bf16[16,640]{1,0:T(8,128)(2,1)S(1)}, u32[]{:S(2)}, u32[]{:S(2)}) collective-permute-start(bf16[16,640]{1,0:T(8,128)(2,1)S(1)} %get-tuple-element.24), channel_id=1, source_target_pairs={{0,1},{1,6},{2,3},{3,4},{4,5},{5,2},{6,7},{7,0},{8,9},{9,14},{10,1... | collective-permute-start | bytes 61448 | tf_op jit(solution)/shard_map/ppermute | solution.py:341
  5.6 1.5 %collective-permute-start.2 = (bf16[16,640]{1,0:T(8,128)(2,1)S(1)}, bf16[16,640]{1,0:T(8,128)(2,1)S(1)}, u32[]{:S(2)}, u32[]{:S(2)}) collective-permute-start(bf16[16,640]{1,0:T(8,128)(2,1)S(1)} %collective-permute-done.1.refs_2_), channel_id=1, source_target_pairs={{0,1},{1,0},{2,3},{3,2},{4,5},{5,4},{6,7},{7,6},{8,9},{9,8},{10,11... | collective-permute-start | bytes 61448 | tf_op jit(solution)/shard_map/ppermute | solution.py:344
  7.2 2.4 %collective-permute-start.4 = (bf16[64,1024]{1,0:T(8,128)(2,1)S(1)}, bf16[64,1024]{1,0:T(8,128)(2,1)S(1)}, u32[]{:S(2)}, u32[]{:S(2)}) collective-permute-start(bf16[64,1024]{1,0:T(8,128)(2,1)S(1)} %shard_map.65), channel_id=1, source_target_pairs={{9,8},{8,1},{1,0},{11,10},{10,3},{3,2},{13,12},{12,5},{5,4},{15,14... | collective-permute-start | bytes 393224 | tf_op jit(solution)/shard_map/ppermute | solution.py:355
  9.6 4.5 %collective-permute-start.5 = (bf16[64,1024]{1,0:T(8,128)(2,1)S(1)}, bf16[64,1024]{1,0:T(8,128)(2,1)S(1)}, u32[]{:S(2)}, u32[]{:S(2)}) collective-permute-start(bf16[64,1024]{1,0:T(8,128)(2,1)S(1)} %shard_map.67), channel_id=1, source_target_pairs={{16,17},{17,8},{8,9},{18,19},{19,10},{10,11},{20,21},{21,12},{12,1... | collective-permute-start | bytes 393224 | tf_op jit(solution)/shard_map/ppermute | solution.py:355
  14.2 7.8 %collective-permute-start.6 = (bf16[64,1024]{1,0:T(8,128)(2,1)S(1)}, bf16[64,1024]{1,0:T(8,128)(2,1)S(1)}, u32[]{:S(2)}, u32[]{:S(2)}) collective-permute-start(bf16[64,1024]{1,0:T(8,128)(2,1)S(1)} %shard_map.68), channel_id=1, source_target_pairs={{25,24},{24,17},{17,16},{27,26},{26,19},{19,18},{29,28},{28,21},{2... | collective-permute-start | bytes 393224 | tf_op jit(solution)/shard_map/ppermute | solution.py:359
  22.0 6.0 %collective-permute-start.10 = (bf16[16,640]{1,0:T(8,128)(2,1)S(1)}, bf16[16,640]{1,0:T(8,128)(2,1)S(1)}, u32[]{:S(2)}, u32[]{:S(2)}) collective-permute-start(bf16[16,640]{1,0:T(8,128)(2,1)S(1)} %get-tuple-element.32), channel_id=1, source_target_pairs={{25,14},{27,4},{29,26},{31,16},{14,15},{4,5},{26,27},{16,17},{15,3... | collective-permute-start | bytes 61448 | tf_op jit(solution)/shard_map/ppermute | solution.py:370
  27.1 1.2 %collective-permute-start.7 = (bf16[16,640]{1,0:T(8,128)(2,1)S(1)}, bf16[16,640]{1,0:T(8,128)(2,1)S(1)}, u32[]{:S(2)}, u32[]{:S(2)}) collective-permute-start(bf16[16,640]{1,0:T(8,128)(2,1)S(1)} %get-tuple-element.29), channel_id=1, source_target_pairs={{25,12},{27,6},{29,24},{31,18},{12,13},{6,7},{24,25},{18,19},{26,2... | collective-permute-start | bytes 61448 | tf_op jit(solution)/shard_map/ppermute | solution.py:370
  27.1 1.4 %collective-permute-start.8 = (bf16[16,640]{1,0:T(8,128)(2,1)S(1)}, bf16[16,640]{1,0:T(8,128)(2,1)S(1)}, u32[]{:S(2)}, u32[]{:S(2)}) collective-permute-start(bf16[16,640]{1,0:T(8,128)(2,1)S(1)} %get-tuple-element.30), channel_id=1, source_target_pairs={{25,10},{27,0},{29,30},{31,20},{10,11},{0,1},{30,31},{20,21},{11,2... | collective-permute-start | bytes 61448 | tf_op jit(solution)/shard_map/ppermute | solution.py:370
  27.6 1.2 %collective-permute-start.9 = (bf16[16,640]{1,0:T(8,128)(2,1)S(1)}, bf16[16,640]{1,0:T(8,128)(2,1)S(1)}, u32[]{:S(2)}, u32[]{:S(2)}) collective-permute-start(bf16[16,640]{1,0:T(8,128)(2,1)S(1)} %get-tuple-element.31), channel_id=1, source_target_pairs={{25,8},{27,2},{29,28},{31,22},{8,9},{2,3},{28,29},{22,23},{9,25},{... | collective-permute-start | bytes 61448 | tf_op jit(solution)/shard_map/ppermute | solution.py:370
  28.8 3.1 %collective-permute-start.11 = (bf16[8,640]{1,0:T(8,128)(2,1)S(1)}, bf16[8,640]{1,0:T(8,128)(2,1)S(1)}, u32[]{:S(2)}, u32[]{:S(2)}) collective-permute-start(bf16[8,640]{1,0:T(8,128)(2,1)S(1)} %slice.8), channel_id=1, source_target_pairs={{0,1},{1,0},{2,3},{3,2},{4,5},{5,4},{6,7},{7,6},{8,9},{9,8},{10,11... | collective-permute-start | bytes 30728 | tf_op jit(solution)/shard_map/ppermute | solution.py:375

commit v8 on v7

--- a/solution.py
+++ b/solution.py
@@ -13,7 +13,7 @@
 BOTH = ("segment", "lon")
 LOG2_E = 1.4426950408889634
 FULL_ROWS = 128
-EXCHANGE_FLOPS = 5 * 10**9
+EXCHANGE_FLOPS = 8 * 10**9
 EARLY = 2
 HBM_SPEC = pl.BlockSpec(memory_space=pltpu.HBM)
 VMEM_SPEC = pl.BlockSpec(memory_space=pltpu.VMEM)
@@ -138,7 +138,7 @@
     @pl.when(leads(group, 0))
     def _():
         patches = jnp.concatenate([piece[...] for piece in pieces], axis=0)
-        latent = matmul(patches, encoder[...]).astype(jnp.bfloat16)
+        latent = jnp.dot(patches, encoder[...], preferred_element_type=jnp.float32).astype(jnp.bfloat16)
         out[...] = layer(latent, lambda i: weights[i], gain[...])
 
 
@@ -153,7 +153,7 @@
     def _():
         mixed = layer(latent[...], lambda i: weights[i], gain[...])
         final = norm_rows(mixed.astype(jnp.float32), final_gain[...])
-        decoded = matmul(final, decoder[...])
+        decoded = jnp.dot(final, decoder[...], preferred_element_type=jnp.float32)
         for block, out in enumerate(outs):
             turn = turns[block] ^ 1 if block else 0
             starts = [(block * group + (c ^ turn)) * rows for c in range(group)]
@@ -277,11 +277,6 @@
     inside = [g for s, g, _ in taken if s == last]
     givers = [(s, g, work) for s, g, _ in taken if s != last]
     takers = [(last, g, work) for g in range(groups) if g not in inside]
-    waiting = [one for one in sorted(late) if one[0] == last and one not in links]
-    if len(waiting) % 2 and len(waiting) < groups - 1:
-        one = waiting[0]
-        links[one] = (last, one[1], work)
-        takers[takers.index(links[one])] = one
     for one, column in zip(givers, assign([[apart(one, two) + 0.0 for two in takers] for one in givers])):
         links[one] = takers[column]
     idle = [one for one in devices if one not in links]

time: 32.9 us -> 32.9 us (level)
  waiting for transfers between devices: 7.04 us -> 6.7 us
    ppermute x4, waiting for transfers between devices: 1.19 us -> 0.84 us  [body(): taken = lax.ppermute(parts[k], BOTH, ways[k])]
  transfers between devices with their start and end apart: 12 -> 12, of which waited for: 11 -> 10; matrix products, arithmetic and copies ran while one was open for 2% -> 2% of each run, Pallas kernels for 0% -> 0%
where the time goes in v8:
time: 32.9 us; the launch traced here: 32.6 us
  starting transfers between devices  24.3 us (74%)
  waiting for transfers between devices  6.7 us (20%)
  local copies, waits for them, and re-layouts  0.76 us (2%)
  other arithmetic  0.63 us (2%)
    ppermute x3, starting transfers between devices, body(): lax.ppermute(latent, BOTH, full_pairs(edges, segments, bands, group, deto...  10.9 us
    ppermute x4, starting transfers between devices, body(): taken = lax.ppermute(parts[k], BOTH, ways[k])  5.95 us
    ppermute x3, waiting for transfers between devices, body(): lax.ppermute(latent, BOTH, full_pairs(edges, segments, bands, group, deto...  3.86 us
    ppermute x2, starting transfers between devices, body(): taken = lax.ppermute(piece, BOTH, pairs)  3.82 us
    ppermute x1, starting transfers between devices, body(): handed = lax.ppermute(rows[first ^ e], BOTH, everywhere(segments, lons, e))  2.31 us
    ppermute x4, waiting for transfers between devices, body(): taken = lax.ppermute(parts[k], BOTH, ways[k])  0.84 us
    ppermute x1, waiting for transfers between devices, body(): handed = lax.ppermute(rows[first ^ e], BOTH, everywhere(segments, lons, e))  0.83 us
    squeeze x1, local copies, waits for them, and re-layouts, body(): lax.dynamic_index_in_dim(own, place ^ sent_way(row, member) ^ 1, 0, keepd...  0.74 us
  transfers between devices with their start and end apart: 12, of which 10 were waited for; matrix products, arithmetic and copies ran while one was open for 2% of the time, Pallas kernels for 0%

profile of v8, /device:TPU:5, one launch (start us, length us, event | category | flops | bytes accessed | tf_op | source)
XLA Modules:
  0.0 32.6 jit_solution(341535623599286879)
XLA Ops:
  0.0 0.7 %collective-permute-start = (bf16[4,8,640]{2,1,0:T(8,128)(2,1)}, bf16[4,8,640]{2,1,0:T(8,128)(2,1)S(1)}, u32[]{:S(2)}, u32[]{:S(2)}) collective-permute-start(bf16[4,8,640]{2,1,0:T(8,128)(2,1)} %bitcast.18), channel_id=1, source_target_pairs={{0,1},{1,0},{2,3},{3,2},{4,5},{5,4},{6,7},{7,6},{8,9},{9,8},{10,11... | collective-permute-start | bytes 122888 | tf_op jit(solution)/shard_map/ppermute | solution.py:312
  0.7 0.7 %dynamic-slice_bitcast_fusion = (bf16[8,640]{1,0:T(8,128)(2,1)S(1)}, bf16[8,640]{1,0:T(8,128)(2,1)S(1)}, bf16[8,640]{1,0:T(8,128)(2,1)S(1)}) fusion(bf16[4,1,8,640]{3,2,1,0:T(8,128)(2,1)} %param.6, s32[]{:T(128)S(6)} %select_n.65, s32[]{:T(128)S(6)} %select_n.63, s32[]{:T(128)S(6)} %select_n.61), kind=kLoop, calls=%fused_computation.4 | loop fusion | bytes 61452 | tf_op jit(solution)/shard_map/jit(dynamic_index_in_dim)/squeeze | solution.py:314
  1.4 0.0 copy-start.1
  1.4 0.3 collective-permute-done.refs_3_
  1.8 2.6 %collective-permute-start.1 = (bf16[16,640]{1,0:T(8,128)(2,1)S(1)}, bf16[16,640]{1,0:T(8,128)(2,1)S(1)}, u32[]{:S(2)}, u32[]{:S(2)}) collective-permute-start(bf16[16,640]{1,0:T(8,128)(2,1)S(1)} %get-tuple-element.23), channel_id=1, source_target_pairs={{0,3},{1,4},{2,1},{3,6},{4,7},{5,0},{6,5},{7,2},{8,11},{9,12},{10,... | collective-permute-start | bytes 61448 | tf_op jit(solution)/shard_map/ppermute | solution.py:336
  4.4 1.2 %collective-permute-start.3 = (bf16[16,640]{1,0:T(8,128)(2,1)S(1)}, bf16[16,640]{1,0:T(8,128)(2,1)S(1)}, u32[]{:S(2)}, u32[]{:S(2)}) collective-permute-start(bf16[16,640]{1,0:T(8,128)(2,1)S(1)} %get-tuple-element.24), channel_id=1, source_target_pairs={{0,1},{1,6},{2,3},{3,4},{4,5},{5,2},{6,7},{7,0},{8,9},{9,14},{10,1... | collective-permute-start | bytes 61448 | tf_op jit(solution)/shard_map/ppermute | solution.py:336
  5.6 0.0 collective-permute-done.1.refs_2_
  5.6 0.7 %collective-permute-start.2 = (bf16[16,640]{1,0:T(8,128)(2,1)S(1)}, bf16[16,640]{1,0:T(8,128)(2,1)S(1)}, u32[]{:S(2)}, u32[]{:S(2)}) collective-permute-start(bf16[16,640]{1,0:T(8,128)(2,1)S(1)} %collective-permute-done.1.refs_2_), channel_id=1, source_target_pairs={{0,1},{1,0},{2,3},{3,2},{4,5},{5,4},{6,7},{7,6},{8,9},{9,8},{10,11... | collective-permute-start | bytes 61448 | tf_op jit(solution)/shard_map/ppermute | solution.py:339
  6.3 0.2 collective-permute-done.3.refs_3_
  6.5 0.6 %collective-permute-done.2.refs_1_ = bf16[16,640]{1,0:T(8,128)(2,1)S(1)} collective-permute-done((bf16[16,640]{1,0:T(8,128)(2,1)S(1)}, bf16[16,640]{1,0:T(8,128)(2,1)S(1)}, u32[]{:S(2)}, u32[]{:S(2)}) %collective-permute-start.2) | collective-permute-done | bytes 20512 | tf_op jit(solution)/shard_map/ppermute | solution.py:339
  7.1 0.0 slice-done
  7.1 0.0 slice-done.1
  7.1 0.0 copy-done
  7.1 0.0 copy-done.1
  7.2 1.5 %collective-permute-start.4 = (bf16[64,1024]{1,0:T(8,128)(2,1)S(1)}, bf16[64,1024]{1,0:T(8,128)(2,1)S(1)}, u32[]{:S(2)}, u32[]{:S(2)}) collective-permute-start(bf16[64,1024]{1,0:T(8,128)(2,1)S(1)} %shard_map.65), channel_id=1, source_target_pairs={{9,8},{8,1},{1,0},{11,10},{10,3},{3,2},{13,12},{12,5},{5,4},{15,14... | collective-permute-start | bytes 393224 | tf_op jit(solution)/shard_map/ppermute | solution.py:350
  8.6 0.1 shard_map.66
  8.7 0.9 %collective-permute-done.4.latent = bf16[64,1024]{1,0:T(8,128)(2,1)S(1)} collective-permute-done((bf16[64,1024]{1,0:T(8,128)(2,1)S(1)}, bf16[64,1024]{1,0:T(8,128)(2,1)S(1)}, u32[]{:S(2)}, u32[]{:S(2)}) %collective-permute-start.4) | collective-permute-done | bytes 131104 | tf_op jit(solution)/shard_map/ppermute | solution.py:350
  9.6 2.6 %collective-permute-start.5 = (bf16[64,1024]{1,0:T(8,128)(2,1)S(1)}, bf16[64,1024]{1,0:T(8,128)(2,1)S(1)}, u32[]{:S(2)}, u32[]{:S(2)}) collective-permute-start(bf16[64,1024]{1,0:T(8,128)(2,1)S(1)} %shard_map.67), channel_id=1, source_target_pairs={{16,17},{17,8},{8,9},{18,19},{19,10},{10,11},{20,21},{21,12},{12,1... | collective-permute-start | bytes 393224 | tf_op jit(solution)/shard_map/ppermute | solution.py:350
  12.2 1.9 %collective-permute-done.5.latent = bf16[64,1024]{1,0:T(8,128)(2,1)S(1)} collective-permute-done((bf16[64,1024]{1,0:T(8,128)(2,1)S(1)}, bf16[64,1024]{1,0:T(8,128)(2,1)S(1)}, u32[]{:S(2)}, u32[]{:S(2)}) %collective-permute-start.5) | collective-permute-done | bytes 131104 | tf_op jit(solution)/shard_map/ppermute | solution.py:350
  14.2 6.8 %collective-permute-start.6 = (bf16[64,1024]{1,0:T(8,128)(2,1)S(1)}, bf16[64,1024]{1,0:T(8,128)(2,1)S(1)}, u32[]{:S(2)}, u32[]{:S(2)}) collective-permute-start(bf16[64,1024]{1,0:T(8,128)(2,1)S(1)} %shard_map.68), channel_id=1, source_target_pairs={{25,24},{24,17},{17,16},{27,26},{26,19},{19,18},{29,28},{28,21},{2... | collective-permute-start | bytes 393224 | tf_op jit(solution)/shard_map/ppermute | solution.py:354
  21.0 1.0 %collective-permute-done.6.latent = bf16[64,1024]{1,0:T(8,128)(2,1)S(1)} collective-permute-done((bf16[64,1024]{1,0:T(8,128)(2,1)S(1)}, bf16[64,1024]{1,0:T(8,128)(2,1)S(1)}, u32[]{:S(2)}, u32[]{:S(2)}) %collective-permute-start.6) | collective-permute-done | bytes 131104 | tf_op jit(solution)/shard_map/ppermute | solution.py:354
  22.0 5.1 %collective-permute-start.10 = (bf16[16,640]{1,0:T(8,128)(2,1)S(1)}, bf16[16,640]{1,0:T(8,128)(2,1)S(1)}, u32[]{:S(2)}, u32[]{:S(2)}) collective-permute-start(bf16[16,640]{1,0:T(8,128)(2,1)S(1)} %get-tuple-element.32), channel_id=1, source_target_pairs={{25,14},{27,4},{29,26},{31,16},{14,15},{4,5},{26,27},{16,17},{15,3... | collective-permute-start | bytes 61448 | tf_op jit(solution)/shard_map/ppermute | solution.py:365
  27.1 0.3 %collective-permute-start.7 = (bf16[16,640]{1,0:T(8,128)(2,1)S(1)}, bf16[16,640]{1,0:T(8,128)(2,1)S(1)}, u32[]{:S(2)}, u32[]{:S(2)}) collective-permute-start(bf16[16,640]{1,0:T(8,128)(2,1)S(1)} %get-tuple-element.29), channel_id=1, source_target_pairs={{25,12},{27,6},{29,24},{31,18},{12,13},{6,7},{24,25},{18,19},{13,2... | collective-permute-start | bytes 61448 | tf_op jit(solution)/shard_map/ppermute | solution.py:365
  27.4 0.2 collective-permute-start.8
  27.6 0.3 %collective-permute-start.9 = (bf16[16,640]{1,0:T(8,128)(2,1)S(1)}, bf16[16,640]{1,0:T(8,128)(2,1)S(1)}, u32[]{:S(2)}, u32[]{:S(2)}) collective-permute-start(bf16[16,640]{1,0:T(8,128)(2,1)S(1)} %get-tuple-element.31), channel_id=1, source_target_pairs={{25,8},{27,2},{29,28},{31,22},{8,9},{2,3},{28,29},{22,23},{9,25},{... | collective-permute-start | bytes 61448 | tf_op jit(solution)/shard_map/ppermute | solution.py:365
  27.9 0.0 collective-permute-done.10
  28.0 0.3 %collective-permute-done.7 = bf16[16,640]{1,0:T(8,128)(2,1)S(1)} collective-permute-done((bf16[16,640]{1,0:T(8,128)(2,1)S(1)}, bf16[16,640]{1,0:T(8,128)(2,1)S(1)}, u32[]{:S(2)}, u32[]{:S(2)}) %collective-permute-start.7) | collective-permute-done | bytes 20512 | tf_op jit(solution)/shard_map/ppermute | solution.py:365
  28.3 0.3 collective-permute-done.8
  28.6 0.2 collective-permute-done.9
  28.8 2.3 %collective-permute-start.11 = (bf16[8,640]{1,0:T(8,128)(2,1)S(1)}, bf16[8,640]{1,0:T(8,128)(2,1)S(1)}, u32[]{:S(2)}, u32[]{:S(2)}) collective-permute-start(bf16[8,640]{1,0:T(8,128)(2,1)S(1)} %slice.8), channel_id=1, source_target_pairs={{0,1},{1,0},{2,3},{3,2},{4,5},{5,4},{6,7},{7,6},{8,9},{9,8},{10,11... | collective-permute-start | bytes 30728 | tf_op jit(solution)/shard_map/ppermute | solution.py:370
  31.1 0.8 %collective-permute-done.11 = bf16[8,640]{1,0:T(8,128)(2,1)S(1)} collective-permute-done((bf16[8,640]{1,0:T(8,128)(2,1)S(1)}, bf16[8,640]{1,0:T(8,128)(2,1)S(1)}, u32[]{:S(2)}, u32[]{:S(2)}) %collective-permute-start.11) | collective-permute-done | bytes 10272 | tf_op jit(solution)/shard_map/ppermute | solution.py:370
  31.9 0.6 %fusion.1 = f32[1,1,8,640]{3,2,1,0:T(8,128)} fusion(bf16[8,640]{1,0:T(8,128)(2,1)S(1)} %collective-permute-done.11, bf16[16,640]{1,0:T(8,128)(2,1)S(1)} %select_select_fusion, pred[]{:T(512)S(6)} %eq.17), kind=kLoop, calls=%fused_computation.3 | loop fusion | flops 10240 | bytes 40961 | tf_op jit(solution)/shard_map/broadcast_in_dim | solution.py:372
  (11 shorter events, 0.1 us)
Async XLA Ops:
  0.0 1.8 %collective-permute-start = (bf16[4,8,640]{2,1,0:T(8,128)(2,1)}, bf16[4,8,640]{2,1,0:T(8,128)(2,1)S(1)}, u32[]{:S(2)}, u32[]{:S(2)}) collective-permute-start(bf16[4,8,640]{2,1,0:T(8,128)(2,1)} %bitcast.18), channel_id=1, source_target_pairs={{0,1},{1,0},{2,3},{3,2},{4,5},{5,4},{6,7},{7,6},{8,9},{9,8},{10,11... | collective-permute-start | bytes 122888 | tf_op jit(solution)/shard_map/ppermute | solution.py:312
  1.4 5.7 %slice-start = ((s8[8388608]{0:T(1024)(128)(4,1)}), s8[4194304]{0:T(1024)(128)(4,1)S(1)}, s32[]{:S(2)}) async-start(s8[8388608]{0:T(1024)(128)(4,1)} %bitcast.15), calls=%async_computation | async-start | bytes 8388608
  1.4 5.7 %slice-start.1 = ((s8[8388608]{0:T(1024)(128)(4,1)}), s8[4194304]{0:T(1024)(128)(4,1)S(1)}, s32[]{:S(2)}) async-start(s8[8388608]{0:T(1024)(128)(4,1)} %bitcast.15), calls=%async_computation.1 | async-start | bytes 8388608
  1.4 5.7 %copy-start = (bf16[640,1024]{1,0:T(8,128)(2,1)S(1)}, bf16[640,1024]{1,0:T(8,128)(2,1)}, u32[]{:S(2)}) copy-start(bf16[640,1024]{1,0:T(8,128)(2,1)} %refs_4_.1) | copy-start | bytes 3932164
  1.4 5.7 %copy-start.1 = (f32[1,1024]{1,0:T(1,128)S(1)}, f32[1,1024]{1,0:T(1,128)}, u32[]{:S(2)}) copy-start(f32[1,1024]{1,0:T(1,128)} %gain.1) | copy-start | bytes 12292
  1.8 3.8 %collective-permute-start.1 = (bf16[16,640]{1,0:T(8,128)(2,1)S(1)}, bf16[16,640]{1,0:T(8,128)(2,1)S(1)}, u32[]{:S(2)}, u32[]{:S(2)}) collective-permute-start(bf16[16,640]{1,0:T(8,128)(2,1)S(1)} %get-tuple-element.23), channel_id=1, source_target_pairs={{0,3},{1,4},{2,1},{3,6},{4,7},{5,0},{6,5},{7,2},{8,11},{9,12},{10,... | collective-permute-start | bytes 61448 | tf_op jit(solution)/shard_map/ppermute | solution.py:336
  4.4 2.1 %collective-permute-start.3 = (bf16[16,640]{1,0:T(8,128)(2,1)S(1)}, bf16[16,640]{1,0:T(8,128)(2,1)S(1)}, u32[]{:S(2)}, u32[]{:S(2)}) collective-permute-start(bf16[16,640]{1,0:T(8,128)(2,1)S(1)} %get-tuple-element.24), channel_id=1, source_target_pairs={{0,1},{1,6},{2,3},{3,4},{4,5},{5,2},{6,7},{7,0},{8,9},{9,14},{10,1... | collective-permute-start | bytes 61448 | tf_op jit(solution)/shard_map/ppermute | solution.py:336
  5.6 1.5 %collective-permute-start.2 = (bf16[16,640]{1,0:T(8,128)(2,1)S(1)}, bf16[16,640]{1,0:T(8,128)(2,1)S(1)}, u32[]{:S(2)}, u32[]{:S(2)}) collective-permute-start(bf16[16,640]{1,0:T(8,128)(2,1)S(1)} %collective-permute-done.1.refs_2_), channel_id=1, source_target_pairs={{0,1},{1,0},{2,3},{3,2},{4,5},{5,4},{6,7},{7,6},{8,9},{9,8},{10,11... | collective-permute-start | bytes 61448 | tf_op jit(solution)/shard_map/ppermute | solution.py:339
  7.2 2.4 %collective-permute-start.4 = (bf16[64,1024]{1,0:T(8,128)(2,1)S(1)}, bf16[64,1024]{1,0:T(8,128)(2,1)S(1)}, u32[]{:S(2)}, u32[]{:S(2)}) collective-permute-start(bf16[64,1024]{1,0:T(8,128)(2,1)S(1)} %shard_map.65), channel_id=1, source_target_pairs={{9,8},{8,1},{1,0},{11,10},{10,3},{3,2},{13,12},{12,5},{5,4},{15,14... | collective-permute-start | bytes 393224 | tf_op jit(solution)/shard_map/ppermute | solution.py:350
  9.6 4.5 %collective-permute-start.5 = (bf16[64,1024]{1,0:T(8,128)(2,1)S(1)}, bf16[64,1024]{1,0:T(8,128)(2,1)S(1)}, u32[]{:S(2)}, u32[]{:S(2)}) collective-permute-start(bf16[64,1024]{1,0:T(8,128)(2,1)S(1)} %shard_map.67), channel_id=1, source_target_pairs={{16,17},{17,8},{8,9},{18,19},{19,10},{10,11},{20,21},{21,12},{12,1... | collective-permute-start | bytes 393224 | tf_op jit(solution)/shard_map/ppermute | solution.py:350
  14.2 7.8 %collective-permute-start.6 = (bf16[64,1024]{1,0:T(8,128)(2,1)S(1)}, bf16[64,1024]{1,0:T(8,128)(2,1)S(1)}, u32[]{:S(2)}, u32[]{:S(2)}) collective-permute-start(bf16[64,1024]{1,0:T(8,128)(2,1)S(1)} %shard_map.68), channel_id=1, source_target_pairs={{25,24},{24,17},{17,16},{27,26},{26,19},{19,18},{29,28},{28,21},{2... | collective-permute-start | bytes 393224 | tf_op jit(solution)/shard_map/ppermute | solution.py:354
  22.0 6.0 %collective-permute-start.10 = (bf16[16,640]{1,0:T(8,128)(2,1)S(1)}, bf16[16,640]{1,0:T(8,128)(2,1)S(1)}, u32[]{:S(2)}, u32[]{:S(2)}) collective-permute-start(bf16[16,640]{1,0:T(8,128)(2,1)S(1)} %get-tuple-element.32), channel_id=1, source_target_pairs={{25,14},{27,4},{29,26},{31,16},{14,15},{4,5},{26,27},{16,17},{15,3... | collective-permute-start | bytes 61448 | tf_op jit(solution)/shard_map/ppermute | solution.py:365
  27.1 1.3 %collective-permute-start.7 = (bf16[16,640]{1,0:T(8,128)(2,1)S(1)}, bf16[16,640]{1,0:T(8,128)(2,1)S(1)}, u32[]{:S(2)}, u32[]{:S(2)}) collective-permute-start(bf16[16,640]{1,0:T(8,128)(2,1)S(1)} %get-tuple-element.29), channel_id=1, source_target_pairs={{25,12},{27,6},{29,24},{31,18},{12,13},{6,7},{24,25},{18,19},{13,2... | collective-permute-start | bytes 61448 | tf_op jit(solution)/shard_map/ppermute | solution.py:365
  27.4 1.2 %collective-permute-start.8 = (bf16[16,640]{1,0:T(8,128)(2,1)S(1)}, bf16[16,640]{1,0:T(8,128)(2,1)S(1)}, u32[]{:S(2)}, u32[]{:S(2)}) collective-permute-start(bf16[16,640]{1,0:T(8,128)(2,1)S(1)} %get-tuple-element.30), channel_id=1, source_target_pairs={{25,10},{27,0},{29,30},{31,20},{10,11},{0,1},{30,31},{20,21},{11,2... | collective-permute-start | bytes 61448 | tf_op jit(solution)/shard_map/ppermute | solution.py:365
  27.6 1.2 %collective-permute-start.9 = (bf16[16,640]{1,0:T(8,128)(2,1)S(1)}, bf16[16,640]{1,0:T(8,128)(2,1)S(1)}, u32[]{:S(2)}, u32[]{:S(2)}) collective-permute-start(bf16[16,640]{1,0:T(8,128)(2,1)S(1)} %get-tuple-element.31), channel_id=1, source_target_pairs={{25,8},{27,2},{29,28},{31,22},{8,9},{2,3},{28,29},{22,23},{9,25},{... | collective-permute-start | bytes 61448 | tf_op jit(solution)/shard_map/ppermute | solution.py:365
  28.8 3.1 %collective-permute-start.11 = (bf16[8,640]{1,0:T(8,128)(2,1)S(1)}, bf16[8,640]{1,0:T(8,128)(2,1)S(1)}, u32[]{:S(2)}, u32[]{:S(2)}) collective-permute-start(bf16[8,640]{1,0:T(8,128)(2,1)S(1)} %slice.8), channel_id=1, source_target_pairs={{0,1},{1,0},{2,3},{3,2},{4,5},{5,4},{6,7},{7,6},{8,9},{9,8},{10,11... | collective-permute-start | bytes 30728 | tf_op jit(solution)/shard_map/ppermute | solution.py:370

commit v9 on v7

--- a/solution.py
+++ b/solution.py
@@ -67,7 +67,7 @@
 def layer(latent, weights, gain):
     wide = latent.astype(jnp.float32)
     normed = norm_rows(wide, gain)
-    queries, keys, values = [matmul(normed, weights(i)).astype(jnp.bfloat16) for i in range(3)]
+    keys, queries, values = [matmul(normed, weights(i)).astype(jnp.bfloat16) for i in (1, 0, 2)]
     attended = attend(queries, keys, values)
     return (wide + matmul(attended, weights(3))).astype(jnp.bfloat16)
 

time: 32.9 us -> 32.9 us (level)
  no operation moved by 1% of the time
where the time goes in v9:
time: 32.9 us; the launch traced here: 32.6 us
  starting transfers between devices  24 us (73%)
  waiting for transfers between devices  7.04 us (21%)
  local copies, waits for them, and re-layouts  0.76 us (2%)
  other arithmetic  0.63 us (2%)
    ppermute x3, starting transfers between devices, body(): lax.ppermute(latent, BOTH, full_pairs(edges, segments, bands, group, deto...  10.9 us
    ppermute x4, starting transfers between devices, body(): taken = lax.ppermute(parts[k], BOTH, ways[k])  5.63 us
    ppermute x3, waiting for transfers between devices, body(): lax.ppermute(latent, BOTH, full_pairs(edges, segments, bands, group, deto...  3.86 us
    ppermute x2, starting transfers between devices, body(): taken = lax.ppermute(piece, BOTH, pairs)  3.82 us
    ppermute x1, starting transfers between devices, body(): handed = lax.ppermute(rows[first ^ e], BOTH, everywhere(segments, lons, e))  2.35 us
    ppermute x4, waiting for transfers between devices, body(): taken = lax.ppermute(parts[k], BOTH, ways[k])  1.19 us
    ppermute x1, waiting for transfers between devices, body(): handed = lax.ppermute(rows[first ^ e], BOTH, everywhere(segments, lons, e))  0.83 us
    squeeze x1, local copies, waits for them, and re-layouts, body(): lax.dynamic_index_in_dim(own, place ^ sent_way(row, member) ^ 1, 0, keepd...  0.74 us
  transfers between devices with their start and end apart: 12, of which 11 were waited for; matrix products, arithmetic and copies ran while one was open for 2% of the time, Pallas kernels for 0%

profile of v9, /device:TPU:5, one launch (start us, length us, event | category | flops | bytes accessed | tf_op | source)
XLA Modules:
  0.0 32.6 jit_solution(2173905269701159893)
XLA Ops:
  0.0 0.7 %collective-permute-start = (bf16[4,8,640]{2,1,0:T(8,128)(2,1)}, bf16[4,8,640]{2,1,0:T(8,128)(2,1)S(1)}, u32[]{:S(2)}, u32[]{:S(2)}) collective-permute-start(bf16[4,8,640]{2,1,0:T(8,128)(2,1)} %bitcast.18), channel_id=1, source_target_pairs={{0,1},{1,0},{2,3},{3,2},{4,5},{5,4},{6,7},{7,6},{8,9},{9,8},{10,11... | collective-permute-start | bytes 122888 | tf_op jit(solution)/shard_map/ppermute | solution.py:317
  0.7 0.7 %dynamic-slice_bitcast_fusion = (bf16[8,640]{1,0:T(8,128)(2,1)S(1)}, bf16[8,640]{1,0:T(8,128)(2,1)S(1)}, bf16[8,640]{1,0:T(8,128)(2,1)S(1)}) fusion(bf16[4,1,8,640]{3,2,1,0:T(8,128)(2,1)} %param.6, s32[]{:T(128)S(6)} %select_n.65, s32[]{:T(128)S(6)} %select_n.63, s32[]{:T(128)S(6)} %select_n.61), kind=kLoop, calls=%fused_computation.4 | loop fusion | bytes 61452 | tf_op jit(solution)/shard_map/jit(dynamic_index_in_dim)/squeeze | solution.py:319
  1.4 0.0 copy-start.1
  1.4 0.3 collective-permute-done.refs_3_
  1.8 2.6 %collective-permute-start.1 = (bf16[16,640]{1,0:T(8,128)(2,1)S(1)}, bf16[16,640]{1,0:T(8,128)(2,1)S(1)}, u32[]{:S(2)}, u32[]{:S(2)}) collective-permute-start(bf16[16,640]{1,0:T(8,128)(2,1)S(1)} %get-tuple-element.23), channel_id=1, source_target_pairs={{0,3},{1,4},{2,1},{3,6},{4,7},{5,0},{6,5},{7,2},{8,11},{9,12},{10,... | collective-permute-start | bytes 61448 | tf_op jit(solution)/shard_map/ppermute | solution.py:341
  4.4 1.2 %collective-permute-start.3 = (bf16[16,640]{1,0:T(8,128)(2,1)S(1)}, bf16[16,640]{1,0:T(8,128)(2,1)S(1)}, u32[]{:S(2)}, u32[]{:S(2)}) collective-permute-start(bf16[16,640]{1,0:T(8,128)(2,1)S(1)} %get-tuple-element.24), channel_id=1, source_target_pairs={{0,1},{1,6},{2,3},{3,4},{4,5},{5,2},{6,7},{7,0},{8,9},{9,14},{10,1... | collective-permute-start | bytes 61448 | tf_op jit(solution)/shard_map/ppermute | solution.py:341
  5.6 0.0 collective-permute-done.1.refs_2_
  5.6 0.7 %collective-permute-start.2 = (bf16[16,640]{1,0:T(8,128)(2,1)S(1)}, bf16[16,640]{1,0:T(8,128)(2,1)S(1)}, u32[]{:S(2)}, u32[]{:S(2)}) collective-permute-start(bf16[16,640]{1,0:T(8,128)(2,1)S(1)} %collective-permute-done.1.refs_2_), channel_id=1, source_target_pairs={{0,1},{1,0},{2,3},{3,2},{4,5},{5,4},{6,7},{7,6},{8,9},{9,8},{10,11... | collective-permute-start | bytes 61448 | tf_op jit(solution)/shard_map/ppermute | solution.py:344
  6.3 0.2 collective-permute-done.3.refs_3_
  6.5 0.6 %collective-permute-done.2.refs_1_ = bf16[16,640]{1,0:T(8,128)(2,1)S(1)} collective-permute-done((bf16[16,640]{1,0:T(8,128)(2,1)S(1)}, bf16[16,640]{1,0:T(8,128)(2,1)S(1)}, u32[]{:S(2)}, u32[]{:S(2)}) %collective-permute-start.2) | collective-permute-done | bytes 20512 | tf_op jit(solution)/shard_map/ppermute | solution.py:344
  7.1 0.0 slice-done
  7.1 0.0 slice-done.1
  7.1 0.0 copy-done
  7.1 0.0 copy-done.1
  7.2 1.5 %collective-permute-start.4 = (bf16[64,1024]{1,0:T(8,128)(2,1)S(1)}, bf16[64,1024]{1,0:T(8,128)(2,1)S(1)}, u32[]{:S(2)}, u32[]{:S(2)}) collective-permute-start(bf16[64,1024]{1,0:T(8,128)(2,1)S(1)} %shard_map.65), channel_id=1, source_target_pairs={{9,8},{8,1},{1,0},{11,10},{10,3},{3,2},{13,12},{12,5},{5,4},{15,14... | collective-permute-start | bytes 393224 | tf_op jit(solution)/shard_map/ppermute | solution.py:355
  8.6 0.1 shard_map.66
  8.7 0.9 %collective-permute-done.4.latent = bf16[64,1024]{1,0:T(8,128)(2,1)S(1)} collective-permute-done((bf16[64,1024]{1,0:T(8,128)(2,1)S(1)}, bf16[64,1024]{1,0:T(8,128)(2,1)S(1)}, u32[]{:S(2)}, u32[]{:S(2)}) %collective-permute-start.4) | collective-permute-done | bytes 131104 | tf_op jit(solution)/shard_map/ppermute | solution.py:355
  9.6 2.6 %collective-permute-start.5 = (bf16[64,1024]{1,0:T(8,128)(2,1)S(1)}, bf16[64,1024]{1,0:T(8,128)(2,1)S(1)}, u32[]{:S(2)}, u32[]{:S(2)}) collective-permute-start(bf16[64,1024]{1,0:T(8,128)(2,1)S(1)} %shard_map.67), channel_id=1, source_target_pairs={{16,17},{17,8},{8,9},{18,19},{19,10},{10,11},{20,21},{21,12},{12,1... | collective-permute-start | bytes 393224 | tf_op jit(solution)/shard_map/ppermute | solution.py:355
  12.2 1.9 %collective-permute-done.5.latent = bf16[64,1024]{1,0:T(8,128)(2,1)S(1)} collective-permute-done((bf16[64,1024]{1,0:T(8,128)(2,1)S(1)}, bf16[64,1024]{1,0:T(8,128)(2,1)S(1)}, u32[]{:S(2)}, u32[]{:S(2)}) %collective-permute-start.5) | collective-permute-done | bytes 131104 | tf_op jit(solution)/shard_map/ppermute | solution.py:355
  14.2 6.8 %collective-permute-start.6 = (bf16[64,1024]{1,0:T(8,128)(2,1)S(1)}, bf16[64,1024]{1,0:T(8,128)(2,1)S(1)}, u32[]{:S(2)}, u32[]{:S(2)}) collective-permute-start(bf16[64,1024]{1,0:T(8,128)(2,1)S(1)} %shard_map.68), channel_id=1, source_target_pairs={{25,24},{24,17},{17,16},{27,26},{26,19},{19,18},{29,28},{28,21},{2... | collective-permute-start | bytes 393224 | tf_op jit(solution)/shard_map/ppermute | solution.py:359
  21.0 1.0 %collective-permute-done.6.latent = bf16[64,1024]{1,0:T(8,128)(2,1)S(1)} collective-permute-done((bf16[64,1024]{1,0:T(8,128)(2,1)S(1)}, bf16[64,1024]{1,0:T(8,128)(2,1)S(1)}, u32[]{:S(2)}, u32[]{:S(2)}) %collective-permute-start.6) | collective-permute-done | bytes 131104 | tf_op jit(solution)/shard_map/ppermute | solution.py:359
  22.0 5.1 %collective-permute-start.10 = (bf16[16,640]{1,0:T(8,128)(2,1)S(1)}, bf16[16,640]{1,0:T(8,128)(2,1)S(1)}, u32[]{:S(2)}, u32[]{:S(2)}) collective-permute-start(bf16[16,640]{1,0:T(8,128)(2,1)S(1)} %get-tuple-element.32), channel_id=1, source_target_pairs={{25,14},{27,4},{29,26},{31,16},{14,15},{4,5},{26,27},{16,17},{15,3... | collective-permute-start | bytes 61448 | tf_op jit(solution)/shard_map/ppermute | solution.py:370
  27.1 0.0 collective-permute-start.7
  27.1 0.5 %collective-permute-start.8 = (bf16[16,640]{1,0:T(8,128)(2,1)S(1)}, bf16[16,640]{1,0:T(8,128)(2,1)S(1)}, u32[]{:S(2)}, u32[]{:S(2)}) collective-permute-start(bf16[16,640]{1,0:T(8,128)(2,1)S(1)} %get-tuple-element.30), channel_id=1, source_target_pairs={{25,10},{27,0},{29,30},{31,20},{10,11},{0,1},{30,31},{20,21},{11,2... | collective-permute-start | bytes 61448 | tf_op jit(solution)/shard_map/ppermute | solution.py:370
  27.6 0.0 collective-permute-start.9
  27.6 0.4 %collective-permute-done.10 = bf16[16,640]{1,0:T(8,128)(2,1)S(1)} collective-permute-done((bf16[16,640]{1,0:T(8,128)(2,1)S(1)}, bf16[16,640]{1,0:T(8,128)(2,1)S(1)}, u32[]{:S(2)}, u32[]{:S(2)}) %collective-permute-start.10) | collective-permute-done | bytes 20512 | tf_op jit(solution)/shard_map/ppermute | solution.py:370
  28.0 0.3 collective-permute-done.7
  28.3 0.2 collective-permute-done.8
  28.4 0.3 %collective-permute-done.9 = bf16[16,640]{1,0:T(8,128)(2,1)S(1)} collective-permute-done((bf16[16,640]{1,0:T(8,128)(2,1)S(1)}, bf16[16,640]{1,0:T(8,128)(2,1)S(1)}, u32[]{:S(2)}, u32[]{:S(2)}) %collective-permute-start.9) | collective-permute-done | bytes 20512 | tf_op jit(solution)/shard_map/ppermute | solution.py:370
  28.8 2.3 %collective-permute-start.11 = (bf16[8,640]{1,0:T(8,128)(2,1)S(1)}, bf16[8,640]{1,0:T(8,128)(2,1)S(1)}, u32[]{:S(2)}, u32[]{:S(2)}) collective-permute-start(bf16[8,640]{1,0:T(8,128)(2,1)S(1)} %slice.8), channel_id=1, source_target_pairs={{0,1},{1,0},{2,3},{3,2},{4,5},{5,4},{6,7},{7,6},{8,9},{9,8},{10,11... | collective-permute-start | bytes 30728 | tf_op jit(solution)/shard_map/ppermute | solution.py:375
  31.1 0.8 %collective-permute-done.11 = bf16[8,640]{1,0:T(8,128)(2,1)S(1)} collective-permute-done((bf16[8,640]{1,0:T(8,128)(2,1)S(1)}, bf16[8,640]{1,0:T(8,128)(2,1)S(1)}, u32[]{:S(2)}, u32[]{:S(2)}) %collective-permute-start.11) | collective-permute-done | bytes 10272 | tf_op jit(solution)/shard_map/ppermute | solution.py:375
  32.0 0.6 %fusion.1 = f32[1,1,8,640]{3,2,1,0:T(8,128)} fusion(bf16[8,640]{1,0:T(8,128)(2,1)S(1)} %collective-permute-done.11, bf16[16,640]{1,0:T(8,128)(2,1)S(1)} %select_select_fusion, pred[]{:T(512)S(6)} %eq.17), kind=kLoop, calls=%fused_computation.3 | loop fusion | flops 10240 | bytes 40961 | tf_op jit(solution)/shard_map/broadcast_in_dim | solution.py:377
  (11 shorter events, 0.1 us)
Async XLA Ops:
  0.0 1.8 %collective-permute-start = (bf16[4,8,640]{2,1,0:T(8,128)(2,1)}, bf16[4,8,640]{2,1,0:T(8,128)(2,1)S(1)}, u32[]{:S(2)}, u32[]{:S(2)}) collective-permute-start(bf16[4,8,640]{2,1,0:T(8,128)(2,1)} %bitcast.18), channel_id=1, source_target_pairs={{0,1},{1,0},{2,3},{3,2},{4,5},{5,4},{6,7},{7,6},{8,9},{9,8},{10,11... | collective-permute-start | bytes 122888 | tf_op jit(solution)/shard_map/ppermute | solution.py:317
  1.4 5.7 %slice-start = ((s8[8388608]{0:T(1024)(128)(4,1)}), s8[4194304]{0:T(1024)(128)(4,1)S(1)}, s32[]{:S(2)}) async-start(s8[8388608]{0:T(1024)(128)(4,1)} %bitcast.15), calls=%async_computation | async-start | bytes 8388608
  1.4 5.7 %slice-start.1 = ((s8[8388608]{0:T(1024)(128)(4,1)}), s8[4194304]{0:T(1024)(128)(4,1)S(1)}, s32[]{:S(2)}) async-start(s8[8388608]{0:T(1024)(128)(4,1)} %bitcast.15), calls=%async_computation.1 | async-start | bytes 8388608
  1.4 5.7 %copy-start = (bf16[640,1024]{1,0:T(8,128)(2,1)S(1)}, bf16[640,1024]{1,0:T(8,128)(2,1)}, u32[]{:S(2)}) copy-start(bf16[640,1024]{1,0:T(8,128)(2,1)} %refs_4_.1) | copy-start | bytes 3932164
  1.4 5.7 %copy-start.1 = (f32[1,1024]{1,0:T(1,128)S(1)}, f32[1,1024]{1,0:T(1,128)}, u32[]{:S(2)}) copy-start(f32[1,1024]{1,0:T(1,128)} %gain.1) | copy-start | bytes 12292
  1.8 3.8 %collective-permute-start.1 = (bf16[16,640]{1,0:T(8,128)(2,1)S(1)}, bf16[16,640]{1,0:T(8,128)(2,1)S(1)}, u32[]{:S(2)}, u32[]{:S(2)}) collective-permute-start(bf16[16,640]{1,0:T(8,128)(2,1)S(1)} %get-tuple-element.23), channel_id=1, source_target_pairs={{0,3},{1,4},{2,1},{3,6},{4,7},{5,0},{6,5},{7,2},{8,11},{9,12},{10,... | collective-permute-start | bytes 61448 | tf_op jit(solution)/shard_map/ppermute | solution.py:341
  4.4 2.1 %collective-permute-start.3 = (bf16[16,640]{1,0:T(8,128)(2,1)S(1)}, bf16[16,640]{1,0:T(8,128)(2,1)S(1)}, u32[]{:S(2)}, u32[]{:S(2)}) collective-permute-start(bf16[16,640]{1,0:T(8,128)(2,1)S(1)} %get-tuple-element.24), channel_id=1, source_target_pairs={{0,1},{1,6},{2,3},{3,4},{4,5},{5,2},{6,7},{7,0},{8,9},{9,14},{10,1... | collective-permute-start | bytes 61448 | tf_op jit(solution)/shard_map/ppermute | solution.py:341
  5.6 1.5 %collective-permute-start.2 = (bf16[16,640]{1,0:T(8,128)(2,1)S(1)}, bf16[16,640]{1,0:T(8,128)(2,1)S(1)}, u32[]{:S(2)}, u32[]{:S(2)}) collective-permute-start(bf16[16,640]{1,0:T(8,128)(2,1)S(1)} %collective-permute-done.1.refs_2_), channel_id=1, source_target_pairs={{0,1},{1,0},{2,3},{3,2},{4,5},{5,4},{6,7},{7,6},{8,9},{9,8},{10,11... | collective-permute-start | bytes 61448 | tf_op jit(solution)/shard_map/ppermute | solution.py:344
  7.2 2.4 %collective-permute-start.4 = (bf16[64,1024]{1,0:T(8,128)(2,1)S(1)}, bf16[64,1024]{1,0:T(8,128)(2,1)S(1)}, u32[]{:S(2)}, u32[]{:S(2)}) collective-permute-start(bf16[64,1024]{1,0:T(8,128)(2,1)S(1)} %shard_map.65), channel_id=1, source_target_pairs={{9,8},{8,1},{1,0},{11,10},{10,3},{3,2},{13,12},{12,5},{5,4},{15,14... | collective-permute-start | bytes 393224 | tf_op jit(solution)/shard_map/ppermute | solution.py:355
  9.6 4.5 %collective-permute-start.5 = (bf16[64,1024]{1,0:T(8,128)(2,1)S(1)}, bf16[64,1024]{1,0:T(8,128)(2,1)S(1)}, u32[]{:S(2)}, u32[]{:S(2)}) collective-permute-start(bf16[64,1024]{1,0:T(8,128)(2,1)S(1)} %shard_map.67), channel_id=1, source_target_pairs={{16,17},{17,8},{8,9},{18,19},{19,10},{10,11},{20,21},{21,12},{12,1... | collective-permute-start | bytes 393224 | tf_op jit(solution)/shard_map/ppermute | solution.py:355
  14.2 7.8 %collective-permute-start.6 = (bf16[64,1024]{1,0:T(8,128)(2,1)S(1)}, bf16[64,1024]{1,0:T(8,128)(2,1)S(1)}, u32[]{:S(2)}, u32[]{:S(2)}) collective-permute-start(bf16[64,1024]{1,0:T(8,128)(2,1)S(1)} %shard_map.68), channel_id=1, source_target_pairs={{25,24},{24,17},{17,16},{27,26},{26,19},{19,18},{29,28},{28,21},{2... | collective-permute-start | bytes 393224 | tf_op jit(solution)/shard_map/ppermute | solution.py:359
  22.0 6.0 %collective-permute-start.10 = (bf16[16,640]{1,0:T(8,128)(2,1)S(1)}, bf16[16,640]{1,0:T(8,128)(2,1)S(1)}, u32[]{:S(2)}, u32[]{:S(2)}) collective-permute-start(bf16[16,640]{1,0:T(8,128)(2,1)S(1)} %get-tuple-element.32), channel_id=1, source_target_pairs={{25,14},{27,4},{29,26},{31,16},{14,15},{4,5},{26,27},{16,17},{15,3... | collective-permute-start | bytes 61448 | tf_op jit(solution)/shard_map/ppermute | solution.py:370
  27.1 1.2 %collective-permute-start.7 = (bf16[16,640]{1,0:T(8,128)(2,1)S(1)}, bf16[16,640]{1,0:T(8,128)(2,1)S(1)}, u32[]{:S(2)}, u32[]{:S(2)}) collective-permute-start(bf16[16,640]{1,0:T(8,128)(2,1)S(1)} %get-tuple-element.29), channel_id=1, source_target_pairs={{25,12},{27,6},{29,24},{31,18},{12,13},{6,7},{24,25},{18,19},{26,2... | collective-permute-start | bytes 61448 | tf_op jit(solution)/shard_map/ppermute | solution.py:370
  27.1 1.4 %collective-permute-start.8 = (bf16[16,640]{1,0:T(8,128)(2,1)S(1)}, bf16[16,640]{1,0:T(8,128)(2,1)S(1)}, u32[]{:S(2)}, u32[]{:S(2)}) collective-permute-start(bf16[16,640]{1,0:T(8,128)(2,1)S(1)} %get-tuple-element.30), channel_id=1, source_target_pairs={{25,10},{27,0},{29,30},{31,20},{10,11},{0,1},{30,31},{20,21},{11,2... | collective-permute-start | bytes 61448 | tf_op jit(solution)/shard_map/ppermute | solution.py:370
  27.6 1.2 %collective-permute-start.9 = (bf16[16,640]{1,0:T(8,128)(2,1)S(1)}, bf16[16,640]{1,0:T(8,128)(2,1)S(1)}, u32[]{:S(2)}, u32[]{:S(2)}) collective-permute-start(bf16[16,640]{1,0:T(8,128)(2,1)S(1)} %get-tuple-element.31), channel_id=1, source_target_pairs={{25,8},{27,2},{29,28},{31,22},{8,9},{2,3},{28,29},{22,23},{9,25},{... | collective-permute-start | bytes 61448 | tf_op jit(solution)/shard_map/ppermute | solution.py:370
  28.8 3.2 %collective-permute-start.11 = (bf16[8,640]{1,0:T(8,128)(2,1)S(1)}, bf16[8,640]{1,0:T(8,128)(2,1)S(1)}, u32[]{:S(2)}, u32[]{:S(2)}) collective-permute-start(bf16[8,640]{1,0:T(8,128)(2,1)S(1)} %slice.8), channel_id=1, source_target_pairs={{0,1},{1,0},{2,3},{3,2},{4,5},{5,4},{6,7},{7,6},{8,9},{9,8},{10,11... | collective-permute-start | bytes 30728 | tf_op jit(solution)/shard_map/ppermute | solution.py:375
